TPU v7x, 1024 devices: a whole 4x8x16 slice. The times are simulated.
1024 devices in a mesh: dp: 32 (over x, y), fsdp: 32 (over z, core).
Axes of the slice: x: 4, y: 8, z: 16, core: 2. Of those that a mesh axis runs over, the one named last changes fastest.
Arguments:
- proj_grads: bfloat16 [1024, 4096], P('fsdp'), may hold values from -6 to 6
- inv_factor: bfloat16 [4096, 4096], P('dp'), as said below
- counts: int32 [1024], P('fsdp'), may hold values from 1 to 3
- dests: int32 [1024, 1], P('fsdp'), may hold values from 0 to 31; in each aligned block of 32 rows (0 to 31, 32 to 63, ...) at most 2 rows name the same one
- rows: bfloat16 [1024, 8192], P('fsdp'), may hold values from -6 to 6
- weight: bfloat16 [8192, 16384], P('fsdp', 'dp'), may hold values from -0.0625 to 0.0625
- cotangent: bfloat16 [2048, 16384], P('fsdp', 'dp'), may hold values from -1.1953125 to 1.1953125
Outputs:
- activated: bfloat16 [2048, 16384], P('fsdp', 'dp')
- weight_grad: float32 [8192, 16384], P('fsdp', 'dp')
Inputs may be any that keep to these rules, and one draw needn't show every extreme that they name: `dests`: within the 32 examples of one device (aligned blocks), no destination is named more than 2 times, a bound that some block reaches. `inv_factor`: an inverse Cholesky factor: lower triangular with a positive diagonal.
All inputs are finite; a program needn't handle non-finite values.
Results may differ from a plain program's by a relative error of at most 0.0051.
Values may be sent and summed in bfloat16 or wider, within the bound.
No kernel may reach another device: no remote copies, remote signals or barrier semaphores. Data moves between devices by JAX's collectives and lax.ppermute only.
A program may use at most 32 MiB of HBM per device.

v0:
```python
import jax
import jax.numpy as jnp
from jax import lax
from jax.sharding import PartitionSpec as P


def shards(proj_grads, inv_factor, counts, dests, rows, weight, cotangent):
    projected = lax.dot_general(
        proj_grads, inv_factor, (((1,), (1,)), ((), ())), preferred_element_type=jnp.float32
    )
    scores = lax.psum(jnp.sum(projected * projected, axis=1), "dp")
    full_dim = proj_grads.shape[1]
    importance = (counts.astype(jnp.float32) * full_dim / scores).astype(jnp.bfloat16)
    groups = lax.axis_size("fsdp")
    local_rows = rows.shape[0]
    capacity = 2 * local_rows // groups
    d_piece = weight.shape[0]
    target = dests[:, 0]
    dest_hot = (target[:, None] == jnp.arange(groups, dtype=jnp.int32)[None, :]).astype(jnp.int32)
    order = jnp.arange(local_rows, dtype=jnp.int32)
    earlier = (order[:, None] > order[None, :]).astype(jnp.int32)
    slot_rank = jnp.sum(jnp.dot(earlier, dest_hot) * dest_hot, axis=1)
    position = target * capacity + slot_rank
    placer = (position[None, :] == jnp.arange(groups * capacity, dtype=jnp.int32)[:, None]).astype(
        jnp.bfloat16
    )
    packed = jnp.dot(placer, rows, preferred_element_type=jnp.float32).astype(jnp.bfloat16)
    pack_w = jnp.dot(placer, importance[:, None], preferred_element_type=jnp.float32).astype(
        jnp.bfloat16
    )
    arrived, arrived_w = (
        lax.all_to_all(packed, "fsdp", split_axis=0, concat_axis=0, tiled=True),
        lax.all_to_all(pack_w[:, 0], "fsdp", split_axis=0, concat_axis=0, tiled=True),
    )
    own_rows = arrived.shape[0]
    moved = lax.all_to_all(
        arrived.reshape(own_rows, groups, d_piece), "fsdp", split_axis=1, concat_axis=0, tiled=True
    )
    spread = moved.reshape(groups * own_rows, d_piece)
    x_block = spread
    hidden = lax.psum_scatter(
        jnp.dot(x_block, weight, preferred_element_type=jnp.float32),
        "fsdp",
        scatter_dimension=0,
        tiled=True,
    )
    squash = jax.nn.sigmoid(hidden)
    activated = (hidden * squash).astype(jnp.bfloat16)
    grad_hidden = (
        arrived_w.astype(jnp.float32)[:, None]
        * cotangent.astype(jnp.float32)
        * squash
        * (1.0 + hidden * (1.0 - squash))
    ).astype(jnp.bfloat16)
    x_block = spread
    weight_grad = lax.dot_general(
        x_block,
        lax.all_gather(grad_hidden, "fsdp", axis=0, tiled=True),
        (((0,), (0,)), ((), ())),
        preferred_element_type=jnp.float32,
    )
    return (activated, weight_grad)


def solution(mesh):
    in_specs = (
        P("fsdp", None),
        P("dp", None),
        P("fsdp"),
        P("fsdp", None),
        P("fsdp", None),
        P("fsdp", "dp"),
        P("fsdp", "dp"),
    )
    out_specs = (P("fsdp", "dp"), P("fsdp", "dp"))
    return jax.shard_map(shards, mesh=mesh, in_specs=in_specs, out_specs=out_specs, check_vma=False)
```

profile of v0, /device:TPU:1, one launch (start us, length us, event | category | flops | bytes accessed | tf_op | source)
XLA Modules:
  0.0 345.6 jit_solution(1601918668604452502)
XLA Ops:
  7.2 0.0 copy-start
  7.2 0.0 reduce-scatter.2.cloned.1.call-start
  7.2 0.9 fusion
  8.1 0.7 multiply_add_fusion
  8.8 1.4 convolution_convert_fusion
  10.2 0.7 all_to_all.23
  11.0 75.9 %all_to_all.34 = bf16[32,2,8192]{2,1,0:T(2,128)(2,1)S(1)} all-to-all(bf16[32,2,8192]{2,1,0:T(2,128)(2,1)S(1)} %all_to_all.23), channel_id=1, replica_groups=mesh['dp'=32,'fsdp'=32] {'fsdp'}, dimensions={0} | all-to-all | bytes 2097152 | tf_op jit(solution)/shard_map/all_to_all | solution.py:32
  86.9 0.7 reshape.37
  87.6 0.0 copy-start.1
  87.6 0.6 copy.10
  88.2 59.0 %all_to_all.35 = bf16[64,32,256]{2,0,1:T(8,128)(2,1)S(1)} all-to-all(bf16[64,32,256]{2,0,1:T(8,128)(2,1)S(1)} %copy.10), channel_id=1, replica_groups=mesh['dp'=32,'fsdp'=32] {'fsdp'}, dimensions={1} | all-to-all | bytes 2097152 | tf_op jit(solution)/shard_map/all_to_all | solution.py:36
  147.2 0.0 copy-done.1
  147.2 2.6 fusion.9
  149.8 0.0 copy-start.2
  149.8 0.0 copy-start.4
  149.8 0.0 copy-start.3
  149.8 0.0 reduce-scatter.2.cloned.1.call-update
  149.8 0.0 all-gather.2.cloned.1.call-start
  149.9 0.0 copy-done
  149.9 0.9 copy-done.2
  150.8 0.6 fusion.1
  151.3 61.3 %psum.7 = f32[32]{0:T(128)S(1)} all-reduce(f32[32]{0:T(128)S(1)} %fusion.1), channel_id=1, replica_groups=mesh['dp'=32,'fsdp'=32] {'dp'}, use_global_device_ids=true, to_apply=%region_3.0 | all-reduce | flops 32 | bytes 256 | tf_op jit(solution)/shard_map/psum | solution.py:11
  212.7 0.0 copy-done.4
  212.7 0.1 fusion.2
  212.8 0.1 all_to_all.30
  212.9 29.5 %all_to_all.36 = bf16[32,2,1]{1,2,0:T(2,128)(2,1)S(1)} all-to-all(bf16[32,2,1]{1,2,0:T(2,128)(2,1)S(1)} %all_to_all.30), channel_id=1, replica_groups=mesh['dp'=32,'fsdp'=32] {'fsdp'}, dimensions={0} | all-to-all | bytes 256 | tf_op jit(solution)/shard_map/all_to_all | solution.py:33
  242.4 0.1 convert_reduce_fusion
  242.5 0.1 reshape.39
  242.6 14.9 %reduce-scatter.2.cloned.1.call-done = f32[64,512]{1,0:T(8,128)} async-done(((f32[2048,512]{1,0:T(8,128)}), f32[64,512]{1,0:T(8,128)}) %reduce-scatter.2.cloned.1.call-update) | async-done | bytes 131088 | tf_op jit(solution)/shard_map/reduce_scatter | solution.py:41
  257.5 0.0 copy-done.3
  257.5 1.6 multiply_convert_fusion
  259.1 0.0 all-gather.2.cloned.1.call-update
  259.1 76.5 %all-gather.2.cloned.1.call-done = bf16[2048,512]{1,0:T(8,128)(2,1)} async-done(((bf16[64,512]{1,0:T(8,128)(2,1)}), bf16[2048,512]{1,0:T(8,128)(2,1)}) %all-gather.2.cloned.1.call-update) | async-done | bytes 2097168 | tf_op jit(solution)/shard_map/all_gather | solution.py:58
  335.6 3.1 fusion.10
Async XLA Ops:
  7.2 142.7 %copy-start = (bf16[128,4096]{1,0:T(8,128)(2,1)S(1)}, bf16[128,4096]{1,0:T(8,128)(2,1)}, u32[]{:S(2)}) copy-start(bf16[128,4096]{1,0:T(8,128)(2,1)} %param.8) | copy-start | bytes 3145732
  7.2 250.3 %reduce-scatter.2.cloned.1.call-start = ((), (), s32[]{:S(2)}) async-start(), calls=%async_computation.4 | async-start | bytes 4325376 | tf_op jit(solution)/shard_map/reduce_scatter | solution.py:41
  87.6 59.6 %copy-start.1 = (bf16[256,512]{1,0:T(8,128)(2,1)S(1)}, bf16[256,512]{1,0:T(8,128)(2,1)}, u32[]{:S(2)}) copy-start(bf16[256,512]{1,0:T(8,128)(2,1)} %param.12) | copy-start | bytes 786436
  149.8 0.9 copy-start.2
  149.8 62.9 %copy-start.4 = (s32[32]{0:T(128)S(1)}, s32[32]{0:T(128)}, u32[]{:S(2)}) copy-start(s32[32]{0:T(128)} %param.9) | copy-start | bytes 388
  149.8 107.7 %copy-start.3 = (bf16[64,512]{1,0:T(8,128)(2,1)S(1)}, bf16[64,512]{1,0:T(8,128)(2,1)}, u32[]{:S(2)}) copy-start(bf16[64,512]{1,0:T(8,128)(2,1)} %param.13) | copy-start | bytes 196612
  149.8 185.8 %all-gather.2.cloned.1.call-start = ((), (), s32[]{:S(2)}) async-start(), calls=%async_computation.5 | async-start | bytes 2162688 | tf_op jit(solution)/shard_map/all_gather | solution.py:58
Sparse Core Ops, SparseCore 0:
  150.0 107.4 reduce-scatter.1
  260.8 74.8 all-gather.1
where the time goes:
time: 346 us
  blocking collectives  226 us (65%)
  waiting for transfers between devices  91.4 us (26%)
  between operations  14.1 us (4%)
  matrix products  8.78 us (3%)
    all_gather x1, waiting for transfers between devices, shards(): lax.all_gather(grad_hidden, 'fsdp', axis=0, tiled=True)  76.5 us
    all_to_all x1, blocking collectives, shards(): lax.all_to_all(packed, 'fsdp', split_axis=0, concat_axis=0, tiled=True)  75.9 us
    psum x1, blocking collectives, shards(): scores = lax.psum(jnp.sum(projected * projected, axis=1), 'dp')  61.3 us
    all_to_all x1, blocking collectives, shards(): lax.all_to_all(arrived.reshape(own_rows, groups, d_piece), 'fsdp', split_...  59 us
    all_to_all x1, blocking collectives, shards(): lax.all_to_all(pack_w[:, 0], 'fsdp', split_axis=0, concat_axis=0, tiled=T...  29.5 us
    reduce_scatter x1, waiting for transfers between devices, shards(): lax.psum_scatter(jnp.dot(x_block, weight, preferred_element_type=jnp.floa...  14.9 us
  transfers between devices with their start and end apart: 2, of which 2 were waited for; matrix products, arithmetic and copies ran while one was open for 0% of the time, Pallas kernels for 0%

commit v1 on v0

v1 whole, which is shorter than its diff:
```python
import jax
import jax.numpy as jnp
from jax import lax
from jax.sharding import Mesh, PartitionSpec as P

BF = jnp.bfloat16
F32 = jnp.float32
SWAP = [(0, 1), (1, 0)]


def both(flag, own, other, axis):
    return jnp.where(flag == 0, jnp.stack([own, other], axis), jnp.stack([other, own], axis))


def at(array, index, axis):
    return lax.dynamic_index_in_dim(array, index, axis, keepdims=False)


def butterfly(value, axis):
    size, step = lax.axis_size(axis), 1
    while step < size:
        value = value + lax.ppermute(value, axis, [(i, i ^ step) for i in range(size)])
        step *= 2
    return value


def shards(proj_grads, inv_factor, counts, dests, rows, weight, cotangent):
    nx, nj = lax.axis_size("x"), lax.axis_size("j")
    nz = 2 * nj
    groups = 2 * nz
    x, j, b, c = (lax.axis_index(a) for a in "xjbc")
    z = 2 * j + b
    local, width = rows.shape
    piece, cols = weight.shape
    quad = 4 * piece

    by_source = cotangent.reshape(nz, 2, 2, cols)
    cot_other = lax.ppermute(at(by_source, 1 - c, 1), "c", SWAP)
    cot_chip = both(c, at(by_source, c, 1), cot_other, 0).reshape(2 * groups, cols)
    target = dests[:, 0]
    dest_hot = (target[:, None] == jnp.arange(groups, dtype=jnp.int32)[None, :]).astype(jnp.int32)
    order = jnp.arange(local, dtype=jnp.int32)
    earlier = (order[:, None] > order[None, :]).astype(jnp.int32)
    rank = jnp.sum(jnp.dot(earlier, dest_hot) * dest_hot, axis=1)
    code = (2 * target + rank).astype(BF)
    code_rows = jnp.zeros((8, cols), BF).at[0, :local].set(code)
    gathered = lax.all_gather(
        jnp.concatenate([cot_chip, code_rows], 0), ("j", "b"), axis=0, tiled=False
    )

    share = local // nx
    mine = lax.dynamic_slice_in_dim(rows, x * share, share, 0)
    mine = mine.reshape(share, nj, quad).transpose(1, 0, 2)
    came = lax.all_to_all(mine, "j", 0, 0, tiled=True)
    x_class = lax.all_gather(came, "x", axis=1, tiled=True).reshape(nj * local, quad)

    w_pair = both(b, weight, lax.ppermute(weight, "b", SWAP), 0)
    w_quad = both(c, w_pair, lax.ppermute(w_pair, "c", SWAP), 1).reshape(quad, cols)

    partial = jnp.dot(x_class, w_quad, preferred_element_type=F32).astype(BF)
    partial = lax.all_to_all(partial.reshape(nj, local, cols), "j", 0, 0, tiled=True)
    hidden = jnp.sum(partial.astype(F32), axis=0)

    projected = lax.dot_general(
        proj_grads, inv_factor, (((1,), (1,)), ((), ())), preferred_element_type=F32
    )
    scores = butterfly(butterfly(jnp.sum(projected * projected, axis=1), "x"), "y")
    importance = (counts.astype(F32) * proj_grads.shape[1] / scores).astype(BF)

    payload = jnp.concatenate(
        [hidden.astype(BF), jnp.broadcast_to(importance[:, None], (local, 128))], 1
    )
    payload = lax.all_gather(payload, ("j", "b"), axis=0, tiled=True)
    hid = payload[:, :cols]
    imp = payload[:, cols : cols + 1].astype(F32)

    codes = gathered[:, 2 * groups, :local].astype(jnp.int32)
    from_z = jnp.arange(nz, dtype=jnp.int32)[:, None]
    place = ((codes // 2) * groups + 2 * from_z + codes % 2).reshape(nz * local)
    slots = jnp.arange(nz * 2 * groups, dtype=jnp.int32)
    hot = (slots[:, None] == place[None, :]).astype(BF)
    cot_slots = gathered[:, : 2 * groups].reshape(nz * 2 * groups, cols)
    cot = lax.dot_general(hot, cot_slots, (((0,), (0,)), ((), ())), preferred_element_type=F32)

    hf = hid.astype(F32)
    squash = jax.nn.sigmoid(hf)
    grad_own = (imp * cot * squash * (1.0 + hf * (1.0 - squash))).astype(BF)
    grad_other = lax.ppermute(grad_own, "c", SWAP)

    x_blocks = x_class.reshape(nj, local, 2, 2 * piece)
    x_pair = lax.ppermute(at(x_blocks, 1 - b, 2), "b", SWAP)
    x_chip = both(b, at(x_blocks, b, 2), x_pair, 1).reshape(nz * local, 2, piece)
    x_own = at(x_chip, c, 1)
    x_other = lax.ppermute(at(x_chip, 1 - c, 1), "c", SWAP)
    over_rows = (((0,), (0,)), ((), ()))
    weight_grad = lax.dot_general(x_own, grad_own, over_rows, preferred_element_type=F32)
    weight_grad = weight_grad + lax.dot_general(
        x_other, grad_other, over_rows, preferred_element_type=F32
    )

    chip_slots = jnp.arange(2 * groups, dtype=jnp.int32) + z * 2 * groups
    pick = (chip_slots[:, None] == place[None, :]).astype(BF)
    at_slots = jnp.dot(pick, hid, preferred_element_type=F32)
    act = (at_slots * jax.nn.sigmoid(at_slots)).astype(BF).reshape(2, nz, 2, cols)
    act_other = lax.ppermute(at(act, 1 - c, 0), "c", SWAP)
    activated = both(c, at(act, c, 0), act_other, 1).reshape(2 * groups, cols)
    return activated, weight_grad


def solution(mesh, nx=4):
    dp, fsdp = mesh.devices.shape
    fine = Mesh(mesh.devices.reshape(nx, dp // nx, fsdp // 4, 2, 2), ("x", "y", "j", "b", "c"))
    dp, fsdp = ("x", "y"), ("j", "b", "c")
    in_specs = (
        P(fsdp, None),
        P(dp, None),
        P(fsdp),
        P(fsdp, None),
        P(fsdp, None),
        P(fsdp, dp),
        P(fsdp, dp),
    )
    out_specs = (P(fsdp, dp), P(fsdp, dp))
    return jax.shard_map(shards, mesh=fine, in_specs=in_specs, out_specs=out_specs, check_vma=False)
```

time: 346 us -> 167 us (0.48)
  blocking collectives: 226 us -> 38 us
  starting transfers between devices: 0.08 us -> 79.7 us
  waiting for transfers between devices: 91.4 us -> 13.7 us
  local copies, waits for them, and re-layouts: 3.09 us -> 8.58 us
    all_to_all x3 -> x0, blocking collectives: 164 us -> none  [the longest x1 75.9 us: shards(): lax.all_to_all(packed, 'fsdp', split_axis=0, concat_axis=0, tiled=True)]
    all_gather x1, waiting for transfers between devices: 76.5 us -> 0.02 us  [shards(): lax.all_gather(jnp.concatenate([cot_chip, code_rows], 0), ('j', 'b'), axi...]
    psum x1 -> x0, blocking collectives: 61.3 us -> none  [shards(): scores = lax.psum(jnp.sum(projected * projected, axis=1), 'dp')]
    ppermute x0 -> x12, starting transfers between devices: none -> 50.3 us  [the longest x5 18.9 us: butterfly(): lax.ppermute(value, axis, [(i, i ^ step) for i in range(size)])]
    all_gather x0 -> x2, blocking collectives: none -> 38 us  [the longest x1 27.2 us: shards(): payload = lax.all_gather(payload, ('j', 'b'), axis=0, tiled=True)]
    all_to_all x0 -> x2, starting transfers between devices: none -> 29.4 us  [the longest x1 19.3 us: shards(): came = lax.all_to_all(mine, 'j', 0, 0, tiled=True)]
    reduce_scatter x1 -> x0, waiting for transfers between devices: 14.9 us -> none  [shards(): lax.psum_scatter(jnp.dot(x_block, weight, preferred_element_type=jnp.floa...]
    ppermute x0 -> x12, waiting for transfers between devices: none -> 13.6 us  [the longest x5 8.31 us: butterfly(): lax.ppermute(value, axis, [(i, i ^ step) for i in range(size)])]
  transfers between devices with their start and end apart: 2 -> 15, of which waited for: 2 -> 5; matrix products, arithmetic and copies ran while one was open for 0% -> 10% of each run, Pallas kernels for 0% -> 0%
where the time goes in v1:
time: 167 us
  starting transfers between devices  79.7 us (48%)
  blocking collectives  38 us (23%)
  between operations  14.5 us (9%)
  waiting for transfers between devices  13.7 us (8%)
  local copies, waits for them, and re-layouts  8.58 us (5%)
  matrix products  8.12 us (5%)
  other arithmetic  3.91 us (2%)
    all_gather x1, blocking collectives, shards(): payload = lax.all_gather(payload, ('j', 'b'), axis=0, tiled=True)  27.2 us
    all_to_all x1, starting transfers between devices, shards(): came = lax.all_to_all(mine, 'j', 0, 0, tiled=True)  19.3 us
    ppermute x5, starting transfers between devices, butterfly(): lax.ppermute(value, axis, [(i, i ^ step) for i in range(size)])  18.9 us
    all_gather x1, blocking collectives, shards(): lax.all_gather(came, 'x', axis=1, tiled=True).reshape(nj * local, quad)  10.9 us
    all_to_all x1, starting transfers between devices, shards(): lax.all_to_all(partial.reshape(nj, local, cols), 'j', 0, 0, tiled=True)  10.1 us
    ppermute x1, starting transfers between devices, shards(): x_other = lax.ppermute(at(x_chip, 1 - c, 1), 'c', SWAP)  9.05 us
    ppermute x1, starting transfers between devices, shards(): grad_other = lax.ppermute(grad_own, 'c', SWAP)  8.46 us
    ppermute x5, waiting for transfers between devices, butterfly(): lax.ppermute(value, axis, [(i, i ^ step) for i in range(size)])  8.31 us
  transfers between devices with their start and end apart: 15, of which 5 were waited for; matrix products, arithmetic and copies ran while one was open for 10% of the time, Pallas kernels for 0%

profile of v1, /device:TPU:1, one launch (start us, length us, event | category | flops | bytes accessed | tf_op | source)
XLA Modules:
  0.0 166.5 jit_solution(3014397698309682963)
XLA Ops:
  7.2 1.7 %constant_dynamic-slice_fusion.4 = bf16[8,8192]{1,0:T(8,128)(2,1)} fusion(bf16[32,8192]{1,0:T(8,128)(2,1)} %param.13, s32[]{:T(128)S(6)} %select_n.124), kind=kLoop, calls=%fused_computation.60 | loop fusion | bytes 262148 | tf_op jit(solution)/shard_map/dynamic_slice | solution.py:52
  8.9 19.3 %all-to-all-start = ((bf16[8,8,1024]{2,1,0:T(8,128)(2,1)}), bf16[8,8,1024]{2,1,0:T(8,128)(2,1)S(1)}, u32[]{:S(2)}, u32[]{:S(2)}) async-start(bf16[8,8,1024]{2,1,0:T(8,128)(2,1)} %bitcast.8), calls=%async_computation | async-start | bytes 262144 | tf_op jit(solution)/shard_map/all_to_all | solution.py:54
  28.2 3.1 %collective-permute-start.1 = (bf16[256,512]{1,0:T(8,128)(2,1)}, bf16[256,512]{1,0:T(8,128)(2,1)S(1)}, u32[]{:S(2)}, u32[]{:S(2)}) collective-permute-start(bf16[256,512]{1,0:T(8,128)(2,1)} %param.14), channel_id=1, source_target_pairs={{0,2},{2,0},{1,3},{3,1},{4,6},{6,4},{5,7},{7,5},{8,10},{10,8},{9,1... | collective-permute-start | bytes 786440 | tf_op jit(solution)/shard_map/ppermute | solution.py:57
  31.3 0.9 reshape.208
  32.3 3.1 %collective-permute-start = (bf16[16,2,512]{2,1,0:T(2,128)(2,1)S(1)}, bf16[16,2,512]{2,1,0:T(2,128)(2,1)S(1)}, u32[]{:S(2)}, u32[]{:S(2)}) collective-permute-start(bf16[16,2,512]{2,1,0:T(2,128)(2,1)S(1)} %get-tuple-element.21), channel_id=1, source_target_pairs={{0,1},{1,0},{2,3},{3,2},{4,5},{5,4},{6,7},{7,6},{8,9},{9,8},{10,11... | collective-permute-start | bytes 98312 | tf_op jit(solution)/shard_map/ppermute | solution.py:38
  35.4 0.9 fusion.5
  36.3 0.7 fusion.31
  37.0 5.3 %collective-permute-done.1 = bf16[256,512]{1,0:T(8,128)(2,1)S(1)} collective-permute-done((bf16[256,512]{1,0:T(8,128)(2,1)}, bf16[256,512]{1,0:T(8,128)(2,1)S(1)}, u32[]{:S(2)}, u32[]{:S(2)}) %collective-permute-start.1) | collective-permute-done | bytes 262176 | tf_op jit(solution)/shard_map/ppermute | solution.py:57
  42.3 1.1 maximum_select_fusion.2
  43.4 2.5 %collective-permute-start.2 = (bf16[2,256,512]{2,1,0:T(8,128)(2,1)S(1)}, bf16[2,256,512]{2,1,0:T(8,128)(2,1)S(1)}, u32[]{:S(2)}, u32[]{:S(2)}) collective-permute-start(bf16[2,256,512]{2,1,0:T(8,128)(2,1)S(1)} %maximum_select_fusion.2), channel_id=1, source_target_pairs={{0,1},{1,0},{2,3},{3,2},{4,5},{5,4},{6,7},{7,6},{8,9},{9,8},{10,11... | collective-permute-start | bytes 1572872 | tf_op jit(solution)/shard_map/ppermute | solution.py:58
  45.9 0.1 broadcast_select_fusion
  46.1 0.6 fusion.21
  46.7 0.1 maximum_select_fusion.1
  46.8 10.9 %all_gather.14 = bf16[8,32,1024]{2,1,0:T(8,128)(2,1)S(1)} all-gather(bf16[8,8,1024]{2,1,0:T(8,128)(2,1)S(1)} %all-to-all-done), channel_id=1, replica_groups=mesh['x'=4,'y'=8,'j'=8,'b'=2,'c'=2] {'x'}, dimensions={1}, use_global_device_ids=true | all-gather | bytes 655360 | tf_op jit(solution)/shard_map/all_gather | solution.py:55
  57.7 0.1 maximum_select_fusion
  57.9 1.2 convolution_convert_fusion
  59.0 10.1 %all-to-all-start.1 = ((bf16[8,32,512]{2,1,0:T(8,128)(2,1)}), bf16[8,32,512]{2,1,0:T(8,128)(2,1)S(1)}, u32[]{:S(2)}, u32[]{:S(2)}) async-start(bf16[8,32,512]{2,1,0:T(8,128)(2,1)} %bitcast.16), calls=%async_computation.1 | async-start | bytes 524288 | tf_op jit(solution)/shard_map/all_to_all | solution.py:61
  69.1 0.6 fusion.6
  69.7 2.8 %collective-permute-start.3 = (f32[32]{0:T(128)S(1)}, f32[32]{0:T(128)S(1)}, u32[]{:S(2)}, u32[]{:S(2)}) collective-permute-start(f32[32]{0:T(128)S(1)} %fusion.6), channel_id=1, source_target_pairs={{0,256},{256,0},{512,768},{768,512},{1,257},{257,1},{513,769},{769... | collective-permute-start | bytes 392 | tf_op jit(solution)/shard_map/ppermute | solution.py:22
  72.5 1.9 %collective-permute-done.3 = f32[32]{0:T(128)S(1)} collective-permute-done((f32[32]{0:T(128)S(1)}, f32[32]{0:T(128)S(1)}, u32[]{:S(2)}, u32[]{:S(2)}) %collective-permute-start.3) | collective-permute-done | bytes 160 | tf_op jit(solution)/shard_map/ppermute | solution.py:22
  74.4 3.7 %collective-permute-start.4 = (f32[32]{0:T(128)S(1)}, f32[32]{0:T(128)S(1)}, u32[]{:S(2)}, u32[]{:S(2)}) collective-permute-start(f32[32]{0:T(128)S(1)} %add.125), channel_id=1, source_target_pairs={{0,512},{256,768},{512,0},{768,256},{1,513},{257,769},{513,1},{769... | collective-permute-start | bytes 392 | tf_op jit(solution)/shard_map/ppermute | solution.py:22
  78.1 2.0 %collective-permute-done.4 = f32[32]{0:T(128)S(1)} collective-permute-done((f32[32]{0:T(128)S(1)}, f32[32]{0:T(128)S(1)}, u32[]{:S(2)}, u32[]{:S(2)}) %collective-permute-start.4) | collective-permute-done | bytes 160 | tf_op jit(solution)/shard_map/ppermute | solution.py:22
  80.2 2.8 %collective-permute-start.5 = (f32[32]{0:T(128)S(1)}, f32[32]{0:T(128)S(1)}, u32[]{:S(2)}, u32[]{:S(2)}) collective-permute-start(f32[32]{0:T(128)S(1)} %add.126), channel_id=1, source_target_pairs={{0,32},{32,0},{64,96},{96,64},{128,160},{160,128},{192,224},{224,1... | collective-permute-start | bytes 392 | tf_op jit(solution)/shard_map/ppermute | solution.py:22
  83.0 1.9 %collective-permute-done.5 = f32[32]{0:T(128)S(1)} collective-permute-done((f32[32]{0:T(128)S(1)}, f32[32]{0:T(128)S(1)}, u32[]{:S(2)}, u32[]{:S(2)}) %collective-permute-start.5) | collective-permute-done | bytes 160 | tf_op jit(solution)/shard_map/ppermute | solution.py:22
  84.9 4.0 %collective-permute-start.6 = (f32[32]{0:T(128)S(1)}, f32[32]{0:T(128)S(1)}, u32[]{:S(2)}, u32[]{:S(2)}) collective-permute-start(f32[32]{0:T(128)S(1)} %add.127), channel_id=1, source_target_pairs={{0,64},{32,96},{64,0},{96,32},{128,192},{160,224},{192,128},{224,1... | collective-permute-start | bytes 392 | tf_op jit(solution)/shard_map/ppermute | solution.py:22
  88.9 0.4 reshape_reshape.3
  89.3 1.1 constant_dynamic-slice_fusion.3
  90.5 3.2 %collective-permute-start.9 = (bf16[8,32,512]{2,1,0:T(8,128)(2,1)S(1)}, bf16[8,32,512]{2,1,0:T(8,128)(2,1)S(1)}, u32[]{:S(2)}, u32[]{:S(2)}) collective-permute-start(bf16[8,32,512]{2,1,0:T(8,128)(2,1)S(1)} %bitcast.64), channel_id=1, source_target_pairs={{0,2},{2,0},{1,3},{3,1},{4,6},{6,4},{5,7},{7,5},{8,10},{10,8},{9,1... | collective-permute-start | bytes 786440 | tf_op jit(solution)/shard_map/ppermute | solution.py:91
  93.7 5.5 %collective-permute-start.7 = (f32[32]{0:T(128)S(1)}, f32[32]{0:T(128)S(1)}, u32[]{:S(2)}, u32[]{:S(2)}) collective-permute-start(f32[32]{0:T(128)S(1)} %add.128), channel_id=1, source_target_pairs={{0,128},{32,160},{64,192},{96,224},{128,0},{160,32},{192,64},{224,... | collective-permute-start | bytes 392 | tf_op jit(solution)/shard_map/ppermute | solution.py:22
  99.3 0.1 add.120
  99.4 2.5 %collective-permute-done.7 = f32[32]{0:T(128)S(1)} collective-permute-done((f32[32]{0:T(128)S(1)}, f32[32]{0:T(128)S(1)}, u32[]{:S(2)}, u32[]{:S(2)}) %collective-permute-start.7) | collective-permute-done | bytes 160 | tf_op jit(solution)/shard_map/ppermute | solution.py:22
  102.0 0.1 maximum_select_fusion.3
  102.1 0.1 select_n.138
  102.3 1.1 constant_dynamic-slice_fusion
  103.4 0.8 copy.22
  104.1 9.0 %collective-permute-start.10 = (bf16[512,256]{1,0:T(8,128)(2,1)}, bf16[512,256]{1,0:T(8,128)(2,1)}, u32[]{:S(2)}, u32[]{:S(2)}) collective-permute-start(bf16[512,256]{1,0:T(8,128)(2,1)} %bitcast.50), channel_id=1, source_target_pairs={{0,1},{1,0},{2,3},{3,2},{4,5},{5,4},{6,7},{7,6},{8,9},{9,8},{10,11... | collective-permute-start | bytes 786440 | tf_op jit(solution)/shard_map/ppermute | solution.py:94
  113.3 27.2 %all_gather.15 = bf16[512,640]{1,0:T(8,128)(2,1)S(1)} all-gather(bf16[32,640]{1,0:T(8,128)(2,1)S(1)} %pad_maximum_fusion), channel_id=1, replica_groups=mesh['x'=4,'y'=8,'j'=8,'b'=2,'c'=2] {'j','b'}, dimensions={0}, use_global_device_ids=true | all-gather | bytes 696320 | tf_op jit(solution)/shard_map/all_gather | solution.py:73
  140.5 0.1 convert_reduce_fusion
  140.6 0.8 fusion.24
  141.4 1.3 slice.35
  142.8 1.8 %fusion.4 = bf16[512,512]{1,0:T(8,128)(2,1)} fusion(bf16[1024,512]{1,0:T(8,128)(2,1)S(1)} %bitcast.55, s32[512]{0:T(512)S(1)} %fusion.28, f32[512]{0:T(512)S(1)} %convert_reduce_fusion, bf16[512,640]{1,0:T(8,128)(2,1)S(1)} %all_gather.15), kind=kOutput, calls=%fused_computation.7 | convolution fusion | flops 540278784 | bytes 2101248 | tf_op jit(solution)/shard_map/dot_general | solution.py:83
  144.7 8.5 %collective-permute-start.11 = (bf16[512,512]{1,0:T(8,128)(2,1)}, bf16[512,512]{1,0:T(8,128)(2,1)S(1)}, u32[]{:S(2)}, u32[]{:S(2)}) collective-permute-start(bf16[512,512]{1,0:T(8,128)(2,1)} %fusion.4), channel_id=1, source_target_pairs={{0,1},{1,0},{2,3},{3,2},{4,5},{5,4},{6,7},{7,6},{8,9},{9,8},{10,11... | collective-permute-start | bytes 1572872 | tf_op jit(solution)/shard_map/ppermute | solution.py:88
  153.1 0.3 multiply_convert_fusion
  153.5 1.9 %collective-permute-start.8 = (bf16[16,2,512]{2,1,0:T(2,128)(2,1)S(1)}, bf16[16,2,512]{2,1,0:T(2,128)(2,1)S(1)}, u32[]{:S(2)}, u32[]{:S(2)}) collective-permute-start(bf16[16,2,512]{2,1,0:T(2,128)(2,1)S(1)} %get-tuple-element.19), channel_id=1, source_target_pairs={{0,1},{1,0},{2,3},{3,2},{4,5},{5,4},{6,7},{7,6},{8,9},{9,8},{10,11... | collective-permute-start | bytes 98312 | tf_op jit(solution)/shard_map/ppermute | solution.py:105
  155.4 1.4 fusion.14
  156.8 0.1 broadcast_select_fusion.1
  156.9 0.7 select_n.133
  157.6 2.1 %convolution_add_fusion = f32[256,512]{1,0:T(8,128)} fusion(f32[256,512]{1,0:T(8,128)S(1)} %fusion.14, bf16[512,256]{1,0:T(8,128)(2,1)} %collective-permute-done.10, bf16[512,512]{1,0:T(8,128)(2,1)S(1)} %collective-permute-done.11), kind=kOutput, calls=%fused_computation.8 | convolution fusion | flops 134348800 | bytes 1835008 | tf_op jit(solution)/shard_map/dot_general | solution.py:97
  (40 shorter events, 0.7 us)
Async XLA Ops:
  7.2 62.0 %copy-start = (bf16[128,4096]{1,0:T(8,128)(2,1)S(1)}, bf16[128,4096]{1,0:T(8,128)(2,1)}, u32[]{:S(2)}) copy-start(bf16[128,4096]{1,0:T(8,128)(2,1)} %param.10) | copy-start | bytes 3145732
  7.2 39.5 %copy-start.1 = (bf16[256,512]{1,0:T(8,128)(2,1)S(1)}, bf16[256,512]{1,0:T(8,128)(2,1)}, u32[]{:S(2)}) copy-start(bf16[256,512]{1,0:T(8,128)(2,1)} %param.14) | copy-start | bytes 786436
  8.9 37.9 %all-to-all-start = ((bf16[8,8,1024]{2,1,0:T(8,128)(2,1)}), bf16[8,8,1024]{2,1,0:T(8,128)(2,1)S(1)}, u32[]{:S(2)}, u32[]{:S(2)}) async-start(bf16[8,8,1024]{2,1,0:T(8,128)(2,1)} %bitcast.8), calls=%async_computation | async-start | bytes 262144 | tf_op jit(solution)/shard_map/all_to_all | solution.py:54
  28.2 112.4 %all-gather.3.cloned.1.call-start = ((), (), s32[]{:S(2)}) async-start(), calls=%async_computation.2 | async-start | bytes 1253376 | tf_op jit(solution)/shard_map/all_gather | solution.py:47
  28.2 14.1 %collective-permute-start.1 = (bf16[256,512]{1,0:T(8,128)(2,1)}, bf16[256,512]{1,0:T(8,128)(2,1)S(1)}, u32[]{:S(2)}, u32[]{:S(2)}) collective-permute-start(bf16[256,512]{1,0:T(8,128)(2,1)} %param.14), channel_id=1, source_target_pairs={{0,2},{2,0},{1,3},{3,1},{4,6},{6,4},{5,7},{7,5},{8,10},{10,8},{9,1... | collective-permute-start | bytes 786440 | tf_op jit(solution)/shard_map/ppermute | solution.py:57
  32.3 13.6 %collective-permute-start = (bf16[16,2,512]{2,1,0:T(2,128)(2,1)S(1)}, bf16[16,2,512]{2,1,0:T(2,128)(2,1)S(1)}, u32[]{:S(2)}, u32[]{:S(2)}) collective-permute-start(bf16[16,2,512]{2,1,0:T(2,128)(2,1)S(1)} %get-tuple-element.21), channel_id=1, source_target_pairs={{0,1},{1,0},{2,3},{3,2},{4,5},{5,4},{6,7},{7,6},{8,9},{9,8},{10,11... | collective-permute-start | bytes 98312 | tf_op jit(solution)/shard_map/ppermute | solution.py:38
  43.4 14.3 %collective-permute-start.2 = (bf16[2,256,512]{2,1,0:T(8,128)(2,1)S(1)}, bf16[2,256,512]{2,1,0:T(8,128)(2,1)S(1)}, u32[]{:S(2)}, u32[]{:S(2)}) collective-permute-start(bf16[2,256,512]{2,1,0:T(8,128)(2,1)S(1)} %maximum_select_fusion.2), channel_id=1, source_target_pairs={{0,1},{1,0},{2,3},{3,2},{4,5},{5,4},{6,7},{7,6},{8,9},{9,8},{10,11... | collective-permute-start | bytes 1572872 | tf_op jit(solution)/shard_map/ppermute | solution.py:58
  57.9 11.3 %copy-start.2 = (bf16[32,4096]{1,0:T(8,128)(2,1)S(1)}, bf16[32,4096]{1,0:T(8,128)(2,1)}, u32[]{:S(2)}) copy-start(bf16[32,4096]{1,0:T(8,128)(2,1)} %param.9) | copy-start | bytes 786436
  59.0 54.2 %all-to-all-start.1 = ((bf16[8,32,512]{2,1,0:T(8,128)(2,1)}), bf16[8,32,512]{2,1,0:T(8,128)(2,1)S(1)}, u32[]{:S(2)}, u32[]{:S(2)}) async-start(bf16[8,32,512]{2,1,0:T(8,128)(2,1)} %bitcast.16), calls=%async_computation.1 | async-start | bytes 524288 | tf_op jit(solution)/shard_map/all_to_all | solution.py:61
  69.7 4.7 %collective-permute-start.3 = (f32[32]{0:T(128)S(1)}, f32[32]{0:T(128)S(1)}, u32[]{:S(2)}, u32[]{:S(2)}) collective-permute-start(f32[32]{0:T(128)S(1)} %fusion.6), channel_id=1, source_target_pairs={{0,256},{256,0},{512,768},{768,512},{1,257},{257,1},{513,769},{769... | collective-permute-start | bytes 392 | tf_op jit(solution)/shard_map/ppermute | solution.py:22
  74.4 5.8 %collective-permute-start.4 = (f32[32]{0:T(128)S(1)}, f32[32]{0:T(128)S(1)}, u32[]{:S(2)}, u32[]{:S(2)}) collective-permute-start(f32[32]{0:T(128)S(1)} %add.125), channel_id=1, source_target_pairs={{0,512},{256,768},{512,0},{768,256},{1,513},{257,769},{513,1},{769... | collective-permute-start | bytes 392 | tf_op jit(solution)/shard_map/ppermute | solution.py:22
  80.2 4.7 %collective-permute-start.5 = (f32[32]{0:T(128)S(1)}, f32[32]{0:T(128)S(1)}, u32[]{:S(2)}, u32[]{:S(2)}) collective-permute-start(f32[32]{0:T(128)S(1)} %add.126), channel_id=1, source_target_pairs={{0,32},{32,0},{64,96},{96,64},{128,160},{160,128},{192,224},{224,1... | collective-permute-start | bytes 392 | tf_op jit(solution)/shard_map/ppermute | solution.py:22
  84.9 8.9 %collective-permute-start.6 = (f32[32]{0:T(128)S(1)}, f32[32]{0:T(128)S(1)}, u32[]{:S(2)}, u32[]{:S(2)}) collective-permute-start(f32[32]{0:T(128)S(1)} %add.127), channel_id=1, source_target_pairs={{0,64},{32,96},{64,0},{96,32},{128,192},{160,224},{192,128},{224,1... | collective-permute-start | bytes 392 | tf_op jit(solution)/shard_map/ppermute | solution.py:22
  89.3 12.6 %copy-start.3 = (s32[32]{0:T(128)S(1)}, s32[32]{0:T(128)}, u32[]{:S(2)}) copy-start(s32[32]{0:T(128)} %param.11) | copy-start | bytes 388
  90.5 11.5 %collective-permute-start.9 = (bf16[8,32,512]{2,1,0:T(8,128)(2,1)S(1)}, bf16[8,32,512]{2,1,0:T(8,128)(2,1)S(1)}, u32[]{:S(2)}, u32[]{:S(2)}) collective-permute-start(bf16[8,32,512]{2,1,0:T(8,128)(2,1)S(1)} %bitcast.64), channel_id=1, source_target_pairs={{0,2},{2,0},{1,3},{3,1},{4,6},{6,4},{5,7},{7,5},{8,10},{10,8},{9,1... | collective-permute-start | bytes 786440 | tf_op jit(solution)/shard_map/ppermute | solution.py:91
  93.7 8.2 %collective-permute-start.7 = (f32[32]{0:T(128)S(1)}, f32[32]{0:T(128)S(1)}, u32[]{:S(2)}, u32[]{:S(2)}) collective-permute-start(f32[32]{0:T(128)S(1)} %add.128), channel_id=1, source_target_pairs={{0,128},{32,160},{64,192},{96,224},{128,0},{160,32},{192,64},{224,... | collective-permute-start | bytes 392 | tf_op jit(solution)/shard_map/ppermute | solution.py:22
  104.1 53.5 %collective-permute-start.10 = (bf16[512,256]{1,0:T(8,128)(2,1)}, bf16[512,256]{1,0:T(8,128)(2,1)}, u32[]{:S(2)}, u32[]{:S(2)}) collective-permute-start(bf16[512,256]{1,0:T(8,128)(2,1)} %bitcast.50), channel_id=1, source_target_pairs={{0,1},{1,0},{2,3},{3,2},{4,5},{5,4},{6,7},{7,6},{8,9},{9,8},{10,11... | collective-permute-start | bytes 786440 | tf_op jit(solution)/shard_map/ppermute | solution.py:94
  144.7 12.9 %collective-permute-start.11 = (bf16[512,512]{1,0:T(8,128)(2,1)}, bf16[512,512]{1,0:T(8,128)(2,1)S(1)}, u32[]{:S(2)}, u32[]{:S(2)}) collective-permute-start(bf16[512,512]{1,0:T(8,128)(2,1)} %fusion.4), channel_id=1, source_target_pairs={{0,1},{1,0},{2,3},{3,2},{4,5},{5,4},{6,7},{7,6},{8,9},{9,8},{10,11... | collective-permute-start | bytes 1572872 | tf_op jit(solution)/shard_map/ppermute | solution.py:88
  153.5 3.3 %collective-permute-start.8 = (bf16[16,2,512]{2,1,0:T(2,128)(2,1)S(1)}, bf16[16,2,512]{2,1,0:T(2,128)(2,1)S(1)}, u32[]{:S(2)}, u32[]{:S(2)}) collective-permute-start(bf16[16,2,512]{2,1,0:T(2,128)(2,1)S(1)} %get-tuple-element.19), channel_id=1, source_target_pairs={{0,1},{1,0},{2,3},{3,2},{4,5},{5,4},{6,7},{7,6},{8,9},{9,8},{10,11... | collective-permute-start | bytes 98312 | tf_op jit(solution)/shard_map/ppermute | solution.py:105
Sparse Core Ops, SparseCore 0:
  46.8 70.5 all-gather.2

commit v2 on v1

v2 whole, which is shorter than its diff:
```python
import jax
import jax.numpy as jnp
from jax import lax
from jax.sharding import Mesh, PartitionSpec as P

BF = jnp.bfloat16
F32 = jnp.float32
SWAP = [(0, 1), (1, 0)]


def both(flag, own, other, axis):
    return jnp.where(flag == 0, jnp.stack([own, other], axis), jnp.stack([other, own], axis))


def shards(proj_grads, inv_factor, counts, dests, rows, weight, cotangent):
    nz = lax.axis_size("z")
    nj, groups = nz // 2, 2 * nz
    z, c = lax.axis_index("z"), lax.axis_index("c")
    b = z % 2
    fsdp = ("z", "c")
    local, width = rows.shape
    piece, cols = weight.shape
    quad = 4 * piece
    stride2 = [[2 * i + k for i in range(nj)] for k in range(2)]
    flip = [(i, i ^ 1) for i in range(nz)]

    cot_slots = lax.all_gather(cotangent, fsdp, axis=0, tiled=True)

    sent = rows.reshape(local, nj, quad).transpose(1, 0, 2)
    came = lax.all_to_all(sent, "z", 0, 0, tiled=True, axis_index_groups=stride2)

    projected = lax.dot_general(
        proj_grads, inv_factor, (((1,), (1,)), ((), ())), preferred_element_type=F32
    )
    scores = lax.psum(lax.psum(jnp.sum(projected * projected, axis=1), "x"), "y")
    came, scores = lax.optimization_barrier((came, scores))
    x_class = came.reshape(nj * local, quad)

    w_pair = both(b, weight, lax.ppermute(weight, "z", flip), 0)
    w_quad = both(c, w_pair, lax.ppermute(w_pair, "c", SWAP), 1).reshape(quad, cols)

    partial = jnp.dot(x_class, w_quad, preferred_element_type=F32).astype(BF)

    blocks = [
        lax.dynamic_slice_in_dim(x_class, (2 * bb + cc) * piece, piece, 1)
        for bb, cc in ((b, c), (1 - b, c), (b, 1 - c), (1 - b, 1 - c))
    ]
    _, *blocks = lax.optimization_barrier((partial[:8, :128], *blocks))
    x_own = blocks[0]
    x_b = lax.ppermute(blocks[1], "z", flip)
    x_c = lax.ppermute(blocks[2], "c", SWAP)
    x_bc = lax.ppermute(blocks[3], fsdp, [(i, i ^ 3) for i in range(groups)])

    partial = lax.all_to_all(
        partial.reshape(nj, local, cols), "z", 0, 0, tiled=True, axis_index_groups=stride2
    )
    hidden = jnp.sum(partial.astype(F32), axis=0)

    importance = (counts.astype(F32) * proj_grads.shape[1] / scores).astype(BF)

    target = dests[:, 0]
    dest_hot = (target[:, None] == jnp.arange(groups, dtype=jnp.int32)[None, :]).astype(jnp.int32)
    order = jnp.arange(local, dtype=jnp.int32)
    earlier = (order[:, None] > order[None, :]).astype(jnp.int32)
    rank = jnp.sum(jnp.dot(earlier, dest_hot) * dest_hot, axis=1)
    code = (2 * target + rank).astype(BF)

    lane = jnp.arange(128)[None, :]
    extra = jnp.where(lane == 0, importance[:, None], code[:, None])
    payload = jnp.concatenate([hidden.astype(BF), extra], 1)
    own = lax.all_gather(payload, "z", axis=0, tiled=True)
    other = lax.ppermute(own, "c", SWAP)

    def place_of(part, parity):
        codes = part[:, cols + 1].astype(jnp.int32)
        from_z = jnp.arange(nz * local, dtype=jnp.int32) // local
        return (codes // 2) * (2 * groups) + (2 * from_z + parity) * 2 + codes % 2

    def grad_of(part, place):
        hf = part[:, :cols].astype(F32)
        imp = part[:, cols : cols + 1].astype(F32)
        slots = jnp.arange(2 * groups * groups, dtype=jnp.int32)
        hot = (slots[:, None] == place[None, :]).astype(BF)
        cot = lax.dot_general(hot, cot_slots, (((0,), (0,)), ((), ())), preferred_element_type=F32)
        squash = jax.nn.sigmoid(hf)
        grad = (imp * cot * squash * (1.0 + hf * (1.0 - squash))).astype(BF)
        return grad.reshape(nj, 2, local, cols)

    def product(x_same, x_flip, grad):
        out = 0.0
        for x_part, bb in ((x_same, b), (x_flip, 1 - b)):
            grad_part = lax.dynamic_index_in_dim(grad, bb, 1, keepdims=False)
            out = out + lax.dot_general(
                x_part,
                grad_part.reshape(nj * local, cols),
                (((0,), (0,)), ((), ())),
                preferred_element_type=F32,
            )
        return out

    def picked(part, place):
        mine = jnp.arange(2 * groups, dtype=jnp.int32) + (2 * z + c) * 2 * groups
        pick = (mine[:, None] == place[None, :]).astype(BF)
        return jnp.dot(pick, part[:, :cols], preferred_element_type=F32)

    place_own, place_other = place_of(own, c), place_of(other, 1 - c)
    weight_grad = product(x_own, x_b, grad_of(own, place_own))
    weight_grad = weight_grad + product(x_c, x_bc, grad_of(other, place_other))
    at_slots = picked(own, place_own) + picked(other, place_other)
    activated = (at_slots * jax.nn.sigmoid(at_slots)).astype(BF)
    return activated, weight_grad


def solution(mesh, nx=4):
    dp, fsdp = mesh.devices.shape
    fine = Mesh(mesh.devices.reshape(nx, dp // nx, fsdp // 2, 2), ("x", "y", "z", "c"))
    dp, fsdp = ("x", "y"), ("z", "c")
    in_specs = (
        P(fsdp, None),
        P(dp, None),
        P(fsdp),
        P(fsdp, None),
        P(fsdp, None),
        P(fsdp, dp),
        P(fsdp, dp),
    )
    out_specs = (P(fsdp, dp), P(fsdp, dp))
    return jax.shard_map(shards, mesh=fine, in_specs=in_specs, out_specs=out_specs, check_vma=False)
```

time: 167 us -> 173 us (1.036)
  waiting for transfers between devices: 13.7 us -> 30.3 us
  starting transfers between devices: 79.7 us -> 65.5 us
  blocking collectives: 38 us -> 49.1 us
  local copies, waits for them, and re-layouts: 8.58 us -> 2.73 us
  other arithmetic: 3.91 us -> 1.17 us
    psum x0 -> x2, blocking collectives: none -> 22.9 us  [the longest x1 13.8 us: shards(): lax.psum(lax.psum(jnp.sum(projected * projected, axis=1), 'x'), 'y')]
    ppermute x11 -> x5, starting transfers between devices: 47.8 us -> 30.8 us  [the longest x1 15.2 us: shards(): other = lax.ppermute(own, 'c', SWAP)]
    ppermute x11 -> x5, waiting for transfers between devices: 13.6 us -> 28 us  [the longest x1 26.9 us: shards(): w_pair = both(b, weight, lax.ppermute(weight, 'z', flip), 0)]
    all_gather x2 -> x1, blocking collectives: 38 us -> 26.2 us  [shards(): own = lax.all_gather(payload, 'z', axis=0, tiled=True)]
    dynamic_slice x3 -> x2, local copies, waits for them, and re-layouts: 3.85 us -> 0.16 us  [the longest x1 0.08 us: shards(): lax.dynamic_slice_in_dim(x_class, (2 * bb + cc) * piece, piece, 1)]
    all_to_all x2, waiting for transfers between devices: 0.01 us -> 2.28 us  [the longest x1 2.28 us: shards(): lax.all_to_all(partial.reshape(nj, local, cols), 'z', 0, 0, tiled=True, a...]
    dot_general x4 -> x8, matrix products: 5.52 us -> 7.78 us  [the longest x2 4.86 us: grad_of(): lax.dot_general(hot, cot_slots, (((0,), (0,)), ((), ())), preferred_eleme...]
  transfers between devices with their start and end apart: 15 -> 9, of which waited for: 5 -> 3; matrix products, arithmetic and copies ran while one was open for 10% -> 6% of each run, Pallas kernels for 0% -> 0%
where the time goes in v2:
time: 173 us
  starting transfers between devices  65.5 us (38%)
  blocking collectives  49.1 us (28%)
  waiting for transfers between devices  30.3 us (18%)
  between operations  14.4 us (8%)
  matrix products  9.63 us (6%)
  local copies, waits for them, and re-layouts  2.73 us (2%)
    ppermute x1, waiting for transfers between devices, shards(): w_pair = both(b, weight, lax.ppermute(weight, 'z', flip), 0)  26.9 us
    all_gather x1, blocking collectives, shards(): own = lax.all_gather(payload, 'z', axis=0, tiled=True)  26.2 us
    all_to_all x1, starting transfers between devices, shards(): lax.all_to_all(sent, 'z', 0, 0, tiled=True, axis_index_groups=stride2)  19.3 us
    ppermute x1, starting transfers between devices, shards(): other = lax.ppermute(own, 'c', SWAP)  15.2 us
    psum x1, blocking collectives, shards(): lax.psum(lax.psum(jnp.sum(projected * projected, axis=1), 'x'), 'y')  13.8 us
    all_to_all x1, starting transfers between devices, shards(): lax.all_to_all(partial.reshape(nj, local, cols), 'z', 0, 0, tiled=True, a...  11.3 us
    psum x1, blocking collectives, shards(): lax.psum(jnp.sum(projected * projected, axis=1), 'x')  9.11 us
    ppermute x1, starting transfers between devices, shards(): x_bc = lax.ppermute(blocks[3], fsdp, [(i, i ^ 3) for i in range(groups)])  8.05 us
  transfers between devices with their start and end apart: 9, of which 3 were waited for; matrix products, arithmetic and copies ran while one was open for 6% of the time, Pallas kernels for 0%

profile of v2, /device:TPU:1, one launch (start us, length us, event | category | flops | bytes accessed | tf_op | source)
XLA Modules:
  0.0 172.8 jit_solution(10826839849933783706)
XLA Ops:
  7.2 0.0 copy-start
  7.2 1.5 copy.11
  8.7 1.1 copy.10
  9.7 19.3 %all-to-all-start = ((bf16[8,32,1024]{2,1,0:T(8,128)(2,1)}), bf16[8,32,1024]{2,1,0:T(8,128)(2,1)S(1)}, u32[]{:S(2)}, u32[]{:S(2)}) async-start(bf16[8,32,1024]{2,1,0:T(8,128)(2,1)} %copy.10), calls=%async_computation | async-start | bytes 1048576 | tf_op jit(solution)/shard_map/all_to_all | solution.py:30
  29.0 0.0 all-gather.2.cloned.1.call-start
  29.1 3.1 %collective-permute-start = (bf16[256,512]{1,0:T(8,128)(2,1)S(1)}, bf16[256,512]{1,0:T(8,128)(2,1)S(1)}, u32[]{:S(2)}, u32[]{:S(2)}) collective-permute-start(bf16[256,512]{1,0:T(8,128)(2,1)S(1)} %copy-done.1), channel_id=1, source_target_pairs={{0,2},{2,0},{4,6},{6,4},{8,10},{10,8},{12,14},{14,12},{16,18},{18,... | collective-permute-start | bytes 786440 | tf_op jit(solution)/shard_map/ppermute | solution.py:39
  32.2 0.0 all-gather.2.cloned.1.call-update
  32.2 26.9 %collective-permute-done = bf16[256,512]{1,0:T(8,128)(2,1)S(1)} collective-permute-done((bf16[256,512]{1,0:T(8,128)(2,1)S(1)}, bf16[256,512]{1,0:T(8,128)(2,1)S(1)}, u32[]{:S(2)}, u32[]{:S(2)}) %collective-permute-start) | collective-permute-done | bytes 262176 | tf_op jit(solution)/shard_map/ppermute | solution.py:39
  59.1 0.1 maximum_select_fusion.2
  59.2 4.0 %collective-permute-start.1 = (bf16[2,256,512]{2,1,0:T(8,128)(2,1)S(1)}, bf16[2,256,512]{2,1,0:T(8,128)(2,1)S(1)}, u32[]{:S(2)}, u32[]{:S(2)}) collective-permute-start(bf16[2,256,512]{2,1,0:T(8,128)(2,1)S(1)} %maximum_select_fusion.2), channel_id=1, source_target_pairs={{0,1},{1,0},{2,3},{3,2},{4,5},{5,4},{6,7},{7,6},{8,9},{9,8},{10,11... | collective-permute-start | bytes 1572872 | tf_op jit(solution)/shard_map/ppermute | solution.py:40
  63.3 0.6 fusion.10
  63.9 9.1 %psum.14 = f32[32]{0:T(128)S(1)} all-reduce(f32[32]{0:T(128)S(1)} %fusion.10), channel_id=1, replica_groups=mesh['x'=4,'y'=8,'z'=16,'c'=2] {'x'}, use_global_device_ids=true, to_apply=%region_1.2 | all-reduce | flops 32 | bytes 256 | tf_op jit(solution)/shard_map/psum | solution.py:35
  73.0 13.8 %psum.15 = f32[32]{0:T(128)S(1)} all-reduce(f32[32]{0:T(128)S(1)} %psum.14), channel_id=1, replica_groups=mesh['x'=4,'y'=8,'z'=16,'c'=2] {'y'}, use_global_device_ids=true, to_apply=%region_2.3 | all-reduce | flops 32 | bytes 256 | tf_op jit(solution)/shard_map/psum | solution.py:35
  86.8 0.1 maximum_select_fusion.1
  86.8 0.0 collective-permute-done.1
  86.9 0.0 copy-start.4
  86.9 0.2 maximum_select_fusion
  87.0 0.0 copy-start.5
  87.0 0.0 all-to-all-done
  87.0 1.1 convolution_convert_fusion
  88.2 11.3 %all-to-all-start.1 = ((bf16[8,32,512]{2,1,0:T(8,128)(2,1)}), bf16[8,32,512]{2,1,0:T(8,128)(2,1)S(1)}, u32[]{:S(2)}, u32[]{:S(2)}) async-start(bf16[8,32,512]{2,1,0:T(8,128)(2,1)} %bitcast.8), calls=%async_computation.1 | async-start | bytes 524288 | tf_op jit(solution)/shard_map/all_to_all | solution.py:54
  99.5 0.0 copy-done.4
  99.5 0.1 fusion.9
  99.7 0.1 constant_dynamic-slice_fusion.4
  99.8 2.5 %collective-permute-start.3 = (bf16[256,256]{1,0:T(8,128)(2,1)S(1)}, bf16[256,256]{1,0:T(8,128)(2,1)S(1)}, u32[]{:S(2)}, u32[]{:S(2)}) collective-permute-start(bf16[256,256]{1,0:T(8,128)(2,1)S(1)} %get-tuple-element.11), channel_id=1, source_target_pairs={{0,2},{2,0},{4,6},{6,4},{8,10},{10,8},{12,14},{14,12},{16,18},{18,... | collective-permute-start | bytes 393224 | tf_op jit(solution)/shard_map/ppermute | solution.py:50
  102.3 8.1 %collective-permute-start.5 = (bf16[256,256]{1,0:T(8,128)(2,1)S(1)}, bf16[256,256]{1,0:T(8,128)(2,1)S(1)}, u32[]{:S(2)}, u32[]{:S(2)}) collective-permute-start(bf16[256,256]{1,0:T(8,128)(2,1)S(1)} %get-tuple-element.13), channel_id=1, source_target_pairs={{0,3},{1,2},{2,1},{3,0},{4,7},{5,6},{6,5},{7,4},{8,11},{9,10},{10,... | collective-permute-start | bytes 393224 | tf_op jit(solution)/shard_map/ppermute | solution.py:52
  110.4 2.0 %collective-permute-start.4 = (bf16[256,256]{1,0:T(8,128)(2,1)S(1)}, bf16[256,256]{1,0:T(8,128)(2,1)S(1)}, u32[]{:S(2)}, u32[]{:S(2)}) collective-permute-start(bf16[256,256]{1,0:T(8,128)(2,1)S(1)} %get-tuple-element.12), channel_id=1, source_target_pairs={{0,1},{1,0},{2,3},{3,2},{4,5},{5,4},{6,7},{7,6},{8,9},{9,8},{10,11... | collective-permute-start | bytes 393224 | tf_op jit(solution)/shard_map/ppermute | solution.py:51
  112.4 0.1 broadcast_select_fusion
  112.5 2.3 %all-to-all-done.1 = bf16[8,32,512]{2,1,0:T(8,128)(2,1)S(1)} async-done(((bf16[8,32,512]{2,1,0:T(8,128)(2,1)}), bf16[8,32,512]{2,1,0:T(8,128)(2,1)S(1)}, u32[]{:S(2)}, u32[]{:S(2)}) %all-to-all-start.1) | async-done | bytes 262176 | tf_op jit(solution)/shard_map/all_to_all | solution.py:54
  114.8 26.2 %all_gather.6 = bf16[512,640]{1,0:T(8,128)(2,1)S(1)} all-gather(bf16[32,640]{1,0:T(8,128)(2,1)S(1)} %pad_maximum_fusion), channel_id=1, replica_groups=mesh['x'=4,'y'=8,'z'=16,'c'=2] {'z'}, dimensions={0}, use_global_device_ids=true | all-gather | bytes 696320 | tf_op jit(solution)/shard_map/all_gather | solution.py:71
  141.0 15.2 %collective-permute-start.2 = (bf16[512,640]{1,0:T(8,128)(2,1)S(1)}, bf16[512,640]{1,0:T(8,128)(2,1)S(1)}, u32[]{:S(2)}, u32[]{:S(2)}) collective-permute-start(bf16[512,640]{1,0:T(8,128)(2,1)S(1)} %all_gather.6), channel_id=1, source_target_pairs={{0,1},{1,0},{2,3},{3,2},{4,5},{5,4},{6,7},{7,6},{8,9},{9,8},{10,11... | collective-permute-start | bytes 1966088 | tf_op jit(solution)/shard_map/ppermute | solution.py:72
  156.2 0.2 convert_reduce_fusion.3
  156.4 0.1 convert_reduce_fusion.1
  156.6 0.2 fusion.22
  156.8 1.1 collective-permute-done.2
  157.9 0.2 convert_reduce_fusion.2
  158.1 0.1 convert_reduce_fusion
  158.3 0.9 multiply_convert_fusion
  159.2 3.3 %fusion.20 = bf16[512,512]{1,0:T(8,128)(2,1)S(1)} fusion(f32[512]{0:T(512)S(1)} %convert_reduce_fusion, bf16[512,640]{1,0:T(8,128)(2,1)S(1)} %collective-permute-done.2, bf16[2048,512]{1,0:T(8,128)(2,1)} %all-gather.2.cloned.1.call-done, s32[512]{0:T(512)S(1)} %fusion.39), kind=kOutput, calls=%fused_computation.32 | convolution fusion | flops 1077673984 | bytes 3149824 | tf_op jit(solution)/shard_map/dot_general | solution.py:84
  162.5 1.6 fusion.7
  164.1 0.1 constant_dynamic-slice_fusion.1
  164.2 0.2 fusion.50
  164.4 0.0 collective-permute-done.3
  164.4 0.2 convolution_add_fusion.1
  164.7 0.0 collective-permute-done.5
  164.7 0.2 fusion.51
  164.9 0.0 collective-permute-done.4
  165.0 1.0 fusion.8
  (17 shorter events, 0.1 us)
Async XLA Ops:
  7.2 56.1 %copy-start = (bf16[128,4096]{1,0:T(8,128)(2,1)S(1)}, bf16[128,4096]{1,0:T(8,128)(2,1)}, u32[]{:S(2)}) copy-start(bf16[128,4096]{1,0:T(8,128)(2,1)} %param.8) | copy-start | bytes 3145732
  7.2 21.9 %copy-start.1 = (bf16[256,512]{1,0:T(8,128)(2,1)S(1)}, bf16[256,512]{1,0:T(8,128)(2,1)}, u32[]{:S(2)}) copy-start(bf16[256,512]{1,0:T(8,128)(2,1)} %param.12) | copy-start | bytes 786436
  7.2 56.1 %copy-start.2 = (bf16[32,4096]{1,0:T(8,128)(2,1)S(1)}, bf16[32,4096]{1,0:T(8,128)(2,1)}, u32[]{:S(2)}) copy-start(bf16[32,4096]{1,0:T(8,128)(2,1)} %param.7) | copy-start | bytes 786436
  9.7 77.3 %all-to-all-start = ((bf16[8,32,1024]{2,1,0:T(8,128)(2,1)}), bf16[8,32,1024]{2,1,0:T(8,128)(2,1)S(1)}, u32[]{:S(2)}, u32[]{:S(2)}) async-start(bf16[8,32,1024]{2,1,0:T(8,128)(2,1)} %copy.10), calls=%async_computation | async-start | bytes 1048576 | tf_op jit(solution)/shard_map/all_to_all | solution.py:30
  29.0 130.2 %all-gather.2.cloned.1.call-start = ((), (), s32[]{:S(2)}) async-start(), calls=%async_computation.2 | async-start | bytes 2162688 | tf_op jit(solution)/shard_map/all_gather | solution.py:27
  29.1 30.0 %collective-permute-start = (bf16[256,512]{1,0:T(8,128)(2,1)S(1)}, bf16[256,512]{1,0:T(8,128)(2,1)S(1)}, u32[]{:S(2)}, u32[]{:S(2)}) collective-permute-start(bf16[256,512]{1,0:T(8,128)(2,1)S(1)} %copy-done.1), channel_id=1, source_target_pairs={{0,2},{2,0},{4,6},{6,4},{8,10},{10,8},{12,14},{14,12},{16,18},{18,... | collective-permute-start | bytes 786440 | tf_op jit(solution)/shard_map/ppermute | solution.py:39
  59.2 27.6 %collective-permute-start.1 = (bf16[2,256,512]{2,1,0:T(8,128)(2,1)S(1)}, bf16[2,256,512]{2,1,0:T(8,128)(2,1)S(1)}, u32[]{:S(2)}, u32[]{:S(2)}) collective-permute-start(bf16[2,256,512]{2,1,0:T(8,128)(2,1)S(1)} %maximum_select_fusion.2), channel_id=1, source_target_pairs={{0,1},{1,0},{2,3},{3,2},{4,5},{5,4},{6,7},{7,6},{8,9},{9,8},{10,11... | collective-permute-start | bytes 1572872 | tf_op jit(solution)/shard_map/ppermute | solution.py:40
  86.9 12.7 %copy-start.4 = (s32[32,1]{0,1:T(1,128)S(1)}, s32[32,1]{0,1:T(1,128)}, u32[]{:S(2)}) copy-start(s32[32,1]{0,1:T(1,128)} %param.10) | copy-start | bytes 388
  87.0 25.3 %copy-start.5 = (s32[32]{0:T(128)S(1)}, s32[32]{0:T(128)}, u32[]{:S(2)}) copy-start(s32[32]{0:T(128)} %param.9) | copy-start | bytes 388
  88.2 26.6 %all-to-all-start.1 = ((bf16[8,32,512]{2,1,0:T(8,128)(2,1)}), bf16[8,32,512]{2,1,0:T(8,128)(2,1)S(1)}, u32[]{:S(2)}, u32[]{:S(2)}) async-start(bf16[8,32,512]{2,1,0:T(8,128)(2,1)} %bitcast.8), calls=%async_computation.1 | async-start | bytes 524288 | tf_op jit(solution)/shard_map/all_to_all | solution.py:54
  99.8 64.6 %collective-permute-start.3 = (bf16[256,256]{1,0:T(8,128)(2,1)S(1)}, bf16[256,256]{1,0:T(8,128)(2,1)S(1)}, u32[]{:S(2)}, u32[]{:S(2)}) collective-permute-start(bf16[256,256]{1,0:T(8,128)(2,1)S(1)} %get-tuple-element.11), channel_id=1, source_target_pairs={{0,2},{2,0},{4,6},{6,4},{8,10},{10,8},{12,14},{14,12},{16,18},{18,... | collective-permute-start | bytes 393224 | tf_op jit(solution)/shard_map/ppermute | solution.py:50
  102.3 62.4 %collective-permute-start.5 = (bf16[256,256]{1,0:T(8,128)(2,1)S(1)}, bf16[256,256]{1,0:T(8,128)(2,1)S(1)}, u32[]{:S(2)}, u32[]{:S(2)}) collective-permute-start(bf16[256,256]{1,0:T(8,128)(2,1)S(1)} %get-tuple-element.13), channel_id=1, source_target_pairs={{0,3},{1,2},{2,1},{3,0},{4,7},{5,6},{6,5},{7,4},{8,11},{9,10},{10,... | collective-permute-start | bytes 393224 | tf_op jit(solution)/shard_map/ppermute | solution.py:52
  110.4 54.6 %collective-permute-start.4 = (bf16[256,256]{1,0:T(8,128)(2,1)S(1)}, bf16[256,256]{1,0:T(8,128)(2,1)S(1)}, u32[]{:S(2)}, u32[]{:S(2)}) collective-permute-start(bf16[256,256]{1,0:T(8,128)(2,1)S(1)} %get-tuple-element.12), channel_id=1, source_target_pairs={{0,1},{1,0},{2,3},{3,2},{4,5},{5,4},{6,7},{7,6},{8,9},{9,8},{10,11... | collective-permute-start | bytes 393224 | tf_op jit(solution)/shard_map/ppermute | solution.py:51
  141.0 16.9 %collective-permute-start.2 = (bf16[512,640]{1,0:T(8,128)(2,1)S(1)}, bf16[512,640]{1,0:T(8,128)(2,1)S(1)}, u32[]{:S(2)}, u32[]{:S(2)}) collective-permute-start(bf16[512,640]{1,0:T(8,128)(2,1)S(1)} %all_gather.6), channel_id=1, source_target_pairs={{0,1},{1,0},{2,3},{3,2},{4,5},{5,4},{6,7},{7,6},{8,9},{9,8},{10,11... | collective-permute-start | bytes 1966088 | tf_op jit(solution)/shard_map/ppermute | solution.py:72
  159.2 3.3 %copy-start.3 = (bf16[2048,512]{1,0:T(8,128)(2,1)S(1)}, bf16[2048,512]{1,0:T(8,128)(2,1)}, u32[]{:S(2)}) copy-start(bf16[2048,512]{1,0:T(8,128)(2,1)} %all-gather.2.cloned.1.call-done) | copy-start | bytes 6291460
Sparse Core Ops, SparseCore 0:
  32.6 78.5 all-gather.1

commit v3 on v2

v3 whole, which is shorter than its diff:
```python
import jax
import jax.numpy as jnp
from jax import lax
from jax.sharding import Mesh, PartitionSpec as P

BF = jnp.bfloat16
F32 = jnp.float32
SWAP = [(0, 1), (1, 0)]


def both(flag, own, other, axis):
    return jnp.where(flag == 0, jnp.stack([own, other], axis), jnp.stack([other, own], axis))


def at(array, index):
    return lax.dynamic_index_in_dim(array, index, 0, keepdims=False)


def shards(proj_grads, inv_factor, counts, dests, rows, weight, cotangent):
    nx, nz = lax.axis_size("x"), lax.axis_size("z")
    nj, groups = nz // 2, 2 * nz
    z, c = lax.axis_index("z"), lax.axis_index("c")
    b = z % 2
    fsdp = ("z", "c")
    local, width = rows.shape
    piece, cols = weight.shape
    quad = 4 * piece
    stride2 = [[2 * i + k for i in range(nj)] for k in range(2)]
    flip = [(i, i ^ 1) for i in range(nz)]

    cot_slots = lax.all_gather(cotangent, fsdp, axis=0, tiled=True)

    w_chip = both(c, weight, lax.ppermute(weight, "c", SWAP), 0)
    w_quad = both(b, w_chip, lax.ppermute(w_chip, "z", flip), 0).reshape(quad, cols)

    share = local // nx
    sent = lax.dynamic_slice_in_dim(rows, lax.axis_index("x") * share, share, 0)
    sent = sent.reshape(share, nj, quad).transpose(1, 0, 2)
    came = lax.all_to_all(sent, "z", 0, 0, tiled=True, axis_index_groups=stride2)

    projected = lax.dot_general(
        proj_grads, inv_factor, (((1,), (1,)), ((), ())), preferred_element_type=F32
    )
    score = jnp.sum(projected * projected, axis=1)
    high = lax.reduce_precision(score, 8, 7)
    middle = lax.reduce_precision(score - high, 8, 7)
    low = score - high - middle
    thirds = jnp.concatenate([high, middle, low, jnp.zeros(quad - 3 * local, F32)]).astype(BF)
    thirds = jnp.broadcast_to(thirds[None, None, :], (1, share, quad))

    came = lax.all_gather(jnp.concatenate([came, thirds], 0), "x", axis=1, tiled=True)
    x_class = came[:nj].reshape(nj * local, quad)
    thirds = came[nj].reshape(nx, share, quad)[:, 0, : 3 * local].astype(F32)
    score = jnp.sum(thirds.reshape(nx * 3, local), axis=0)

    partial = jnp.dot(x_class, w_quad, preferred_element_type=F32).astype(BF)

    blocks = [
        lax.dynamic_slice_in_dim(x_class, 2 * bb * piece, 2 * piece, 1) for bb in (b, 1 - b)
    ]
    _, score, *blocks = lax.optimization_barrier((partial[:8, :128], score, *blocks))
    x_same, x_flip = blocks[0], lax.ppermute(blocks[1], "z", flip)
    scores = lax.psum(score, "y")

    partial = lax.all_to_all(
        partial.reshape(nj, local, cols), "z", 0, 0, tiled=True, axis_index_groups=stride2
    )
    hidden = jnp.sum(partial.astype(F32), axis=0)

    importance = (counts.astype(F32) * proj_grads.shape[1] / scores).astype(BF)

    target = dests[:, 0]
    dest_hot = (target[:, None] == jnp.arange(groups, dtype=jnp.int32)[None, :]).astype(jnp.int32)
    order = jnp.arange(local, dtype=jnp.int32)
    earlier = (order[:, None] > order[None, :]).astype(jnp.int32)
    rank = jnp.sum(jnp.dot(earlier, dest_hot) * dest_hot, axis=1)
    code = (2 * target + rank).astype(BF)

    lane = jnp.arange(128)[None, :]
    extra = jnp.where(lane == 0, importance[:, None], code[:, None])
    payload = jnp.concatenate([hidden.astype(BF), extra], 1)
    part = lax.all_gather(payload, "z", axis=0, tiled=True)

    codes = part[:, cols + 1].astype(jnp.int32)
    from_z = jnp.arange(nz * local, dtype=jnp.int32) // local
    place = (codes // 2) * (2 * groups) + (2 * from_z + c) * 2 + codes % 2

    slots = jnp.arange(4 * groups, dtype=jnp.int32) + 4 * z * groups
    pick = (slots[:, None] == place[None, :]).astype(BF)
    at_slots = jnp.dot(pick, part[:, :cols], preferred_element_type=F32)
    act = (at_slots * jax.nn.sigmoid(at_slots)).astype(BF).reshape(2, 2 * groups, cols)
    act_other = lax.ppermute(at(act, 1 - c), "c", SWAP)
    activated = at(act, c) + act_other

    hf = part[:, :cols].astype(F32)
    imp = part[:, cols : cols + 1].astype(F32)
    slots = jnp.arange(2 * groups * groups, dtype=jnp.int32)
    hot = (slots[:, None] == place[None, :]).astype(BF)
    cot = lax.dot_general(hot, cot_slots, (((0,), (0,)), ((), ())), preferred_element_type=F32)
    squash = jax.nn.sigmoid(hf)
    grad = (imp * cot * squash * (1.0 + hf * (1.0 - squash))).astype(BF)
    grad = grad.reshape(nj, 2, local, cols)

    def product(core):
        out = 0.0
        for x_part, bb in ((x_same, b), (x_flip, 1 - b)):
            x_block = lax.dynamic_slice_in_dim(x_part, core * piece, piece, 1)
            grad_part = lax.dynamic_index_in_dim(grad, bb, 1, keepdims=False)
            out = out + lax.dot_general(
                x_block,
                grad_part.reshape(nj * local, cols),
                (((0,), (0,)), ((), ())),
                preferred_element_type=F32,
            )
        return out

    other = lax.ppermute(product(1 - c).astype(BF), "c", SWAP)
    weight_grad = product(c) + other.astype(F32)
    return activated, weight_grad


def solution(mesh, nx=4):
    dp, fsdp = mesh.devices.shape
    fine = Mesh(mesh.devices.reshape(nx, dp // nx, fsdp // 2, 2), ("x", "y", "z", "c"))
    dp, fsdp = ("x", "y"), ("z", "c")
    in_specs = (
        P(fsdp, None),
        P(dp, None),
        P(fsdp),
        P(fsdp, None),
        P(fsdp, None),
        P(fsdp, dp),
        P(fsdp, dp),
    )
    out_specs = (P(fsdp, dp), P(fsdp, dp))
    return jax.shard_map(shards, mesh=fine, in_specs=in_specs, out_specs=out_specs, check_vma=False)
```

time: 173 us -> 141 us (0.82)
  waiting for transfers between devices: 30.3 us -> 9.53 us
  starting transfers between devices: 65.5 us -> 48.9 us
  blocking collectives: 49.1 us -> 53.7 us
  other arithmetic: 1.17 us -> 3.09 us
    ppermute x6 -> x5, waiting for transfers between devices: 28 us -> 0.61 us  [the longest x1 0.6 us: shards(): other = lax.ppermute(product(1 - c).astype(BF), 'c', SWAP)]
    all_to_all x1, starting transfers between devices: 19.3 us -> 5.82 us  [shards(): lax.all_to_all(sent, 'z', 0, 0, tiled=True, axis_index_groups=stride2)]
    all_gather x1 -> x2, blocking collectives: 26.2 us -> 38.5 us  [the longest x1 28.1 us: shards(): part = lax.all_gather(payload, 'z', axis=0, tiled=True)]
    psum x2 -> x1, blocking collectives: 22.9 us -> 15.3 us  [shards(): scores = lax.psum(score, 'y')]
    all_to_all x1, waiting for transfers between devices: 0.01 us -> 7.16 us  [shards(): lax.all_to_all(sent, 'z', 0, 0, tiled=True, axis_index_groups=stride2)]
    all_to_all x1, starting transfers between devices: 11.3 us -> 5.77 us  [shards(): lax.all_to_all(partial.reshape(nj, local, cols), 'z', 0, 0, tiled=True, a...]
    dot_general x8 -> x6, matrix products: 7.78 us -> 5.3 us  [the longest x1 3.16 us: shards(): lax.dot_general(hot, cot_slots, (((0,), (0,)), ((), ())), preferred_eleme...]
    ppermute x6 -> x5, starting transfers between devices: 34.9 us -> 37.2 us  [the longest x1 16.2 us: shards(): w_chip = both(c, weight, lax.ppermute(weight, 'c', SWAP), 0)]
  transfers between devices with their start and end apart: 9 -> 8, of which waited for: 3 -> 3; matrix products, arithmetic and copies ran while one was open for 6% -> 9% of each run, Pallas kernels for 0% -> 0%
where the time goes in v3:
time: 141 us; the launch traced here: 140 us
  blocking collectives  53.7 us (38%)
  starting transfers between devices  48.9 us (35%)
  between operations  14.3 us (10%)
  waiting for transfers between devices  9.53 us (7%)
  matrix products  8.84 us (6%)
  other arithmetic  3.09 us (2%)
  local copies, waits for them, and re-layouts  1.81 us (1%)
    all_gather x1, blocking collectives, shards(): part = lax.all_gather(payload, 'z', axis=0, tiled=True)  28.1 us
    ppermute x1, starting transfers between devices, shards(): w_chip = both(c, weight, lax.ppermute(weight, 'c', SWAP), 0)  16.2 us
    psum x1, blocking collectives, shards(): scores = lax.psum(score, 'y')  15.3 us
    ppermute x1, starting transfers between devices, shards(): act_other = lax.ppermute(at(act, 1 - c), 'c', SWAP)  13.1 us
    all_gather x1, blocking collectives, shards(): lax.all_gather(jnp.concatenate([came, thirds], 0), 'x', axis=1, tiled=True)  10.4 us
    all_to_all x1, waiting for transfers between devices, shards(): lax.all_to_all(sent, 'z', 0, 0, tiled=True, axis_index_groups=stride2)  7.16 us
    all_to_all x1, starting transfers between devices, shards(): lax.all_to_all(sent, 'z', 0, 0, tiled=True, axis_index_groups=stride2)  5.82 us
    all_to_all x1, starting transfers between devices, shards(): lax.all_to_all(partial.reshape(nj, local, cols), 'z', 0, 0, tiled=True, a...  5.77 us
  transfers between devices with their start and end apart: 8, of which 3 were waited for; matrix products, arithmetic and copies ran while one was open for 9% of the time, Pallas kernels for 0%

profile of v3, /device:TPU:1, one launch (start us, length us, event | category | flops | bytes accessed | tf_op | source)
XLA Modules:
  0.0 140.2 jit_solution(3465153231303509946)
XLA Ops:
  7.2 0.0 copy-start
  7.2 0.0 copy-start.1
  7.2 16.2 %collective-permute-start = (bf16[256,512]{1,0:T(8,128)(2,1)}, bf16[256,512]{1,0:T(8,128)(2,1)S(1)}, u32[]{:S(2)}, u32[]{:S(2)}) collective-permute-start(bf16[256,512]{1,0:T(8,128)(2,1)} %param.12), channel_id=1, source_target_pairs={{0,1},{1,0},{2,3},{3,2},{4,5},{5,4},{6,7},{7,6},{8,9},{9,8},{10,11... | collective-permute-start | bytes 786440 | tf_op jit(solution)/shard_map/ppermute | solution.py:33
  23.4 1.6 %constant_dynamic-slice_fusion.4 = bf16[8,8192]{1,0:T(8,128)(2,1)} fusion(bf16[32,8192]{1,0:T(8,128)(2,1)} %param.11, s32[]{:T(128)S(6)} %select_n.107), kind=kLoop, calls=%fused_computation.65 | loop fusion | bytes 262148 | tf_op jit(solution)/shard_map/dynamic_slice | solution.py:37
  25.0 5.8 %all-to-all-start = ((bf16[8,8,1024]{2,1,0:T(8,128)(2,1)}), bf16[8,8,1024]{2,1,0:T(8,128)(2,1)S(1)}, u32[]{:S(2)}, u32[]{:S(2)}) async-start(bf16[8,8,1024]{2,1,0:T(8,128)(2,1)} %bitcast.1), calls=%async_computation | async-start | bytes 262144 | tf_op jit(solution)/shard_map/all_to_all | solution.py:39
  30.8 0.0 all-gather.2.cloned.1.call-start
  30.8 0.7 all-gather.2.cloned.1.call-update
  31.5 0.0 copy-done
  31.5 1.5 %fusion.9 = f32[32]{0:T(128)S(1)} fusion(bf16[32,4096]{1,0:T(8,128)(2,1)} %param.7, bf16[128,4096]{1,0:T(8,128)(2,1)S(1)} %copy-done), kind=kOutput, calls=%fused_computation.17 | convolution fusion | flops 33562592 | bytes 1310848 | tf_op jit(solution)/shard_map/dot_general | solution.py:41
  33.1 0.9 fusion.8
  34.0 0.7 fusion.46
  34.6 0.1 pad_maximum_fusion.2
  34.7 0.0 collective-permute-done
  34.7 0.0 copy-done.1
  34.7 0.9 maximum_select_fusion.2
  35.6 3.1 %collective-permute-start.1 = (bf16[2,256,512]{2,1,0:T(8,128)(2,1)}, bf16[2,256,512]{2,1,0:T(8,128)(2,1)S(1)}, u32[]{:S(2)}, u32[]{:S(2)}) collective-permute-start(bf16[2,256,512]{2,1,0:T(8,128)(2,1)} %maximum_select_fusion.2), channel_id=1, source_target_pairs={{0,2},{2,0},{4,6},{6,4},{8,10},{10,8},{12,14},{14,12},{16,18},{18,... | collective-permute-start | bytes 1572872 | tf_op jit(solution)/shard_map/ppermute | solution.py:34
  38.7 0.1 maximum_select_fusion.1
  38.8 7.2 %all-to-all-done = bf16[8,8,1024]{2,1,0:T(8,128)(2,1)S(1)} async-done(((bf16[8,8,1024]{2,1,0:T(8,128)(2,1)}), bf16[8,8,1024]{2,1,0:T(8,128)(2,1)S(1)}, u32[]{:S(2)}, u32[]{:S(2)}) %all-to-all-start) | async-done | bytes 131104 | tf_op jit(solution)/shard_map/all_to_all | solution.py:39
  46.0 10.4 %all_gather.9 = bf16[9,32,1024]{2,1,0:T(8,128)(2,1)S(1)} all-gather(bf16[9,8,1024]{2,1,0:T(8,128)(2,1)S(1)} %pad_maximum_fusion), channel_id=1, replica_groups=mesh['x'=4,'y'=8,'z'=16,'c'=2] {'x'}, dimensions={1}, use_global_device_ids=true | all-gather | bytes 737280 | tf_op jit(solution)/shard_map/all_gather | solution.py:51
  56.4 0.0 collective-permute-done.1
  56.4 0.2 maximum_select_fusion
  56.6 0.0 copy-start.2
  56.6 1.2 convolution_convert_fusion
  57.8 5.8 %all-to-all-start.1 = ((bf16[8,32,512]{2,1,0:T(8,128)(2,1)}), bf16[8,32,512]{2,1,0:T(8,128)(2,1)S(1)}, u32[]{:S(2)}, u32[]{:S(2)}) async-start(bf16[8,32,512]{2,1,0:T(8,128)(2,1)} %bitcast.9), calls=%async_computation.1 | async-start | bytes 524288 | tf_op jit(solution)/shard_map/all_to_all | solution.py:65
  63.6 0.1 reshape.200
  63.7 2.9 %collective-permute-start.3 = (bf16[256,512]{1,0:T(8,128)(2,1)S(1)}, bf16[256,512]{1,0:T(8,128)(2,1)S(1)}, u32[]{:S(2)}, u32[]{:S(2)}) collective-permute-start(bf16[256,512]{1,0:T(8,128)(2,1)S(1)} %get-tuple-element.7), channel_id=1, source_target_pairs={{0,2},{2,0},{4,6},{6,4},{8,10},{10,8},{12,14},{14,12},{16,18},{18,... | collective-permute-start | bytes 786440 | tf_op jit(solution)/shard_map/ppermute | solution.py:62
  66.7 15.3 %psum.7 = f32[32]{0:T(128)S(1)} all-reduce(f32[32]{0:T(128)S(1)} %reduce_sum.43), channel_id=1, replica_groups=mesh['x'=4,'y'=8,'z'=16,'c'=2] {'y'}, use_global_device_ids=true, to_apply=%region_3.4 | all-reduce | flops 32 | bytes 256 | tf_op jit(solution)/shard_map/psum | solution.py:63
  82.0 0.0 copy-done.2
  82.0 0.1 broadcast_select_fusion
  82.0 1.1 all-to-all-done.1
  83.2 28.1 %all_gather.10 = bf16[512,640]{1,0:T(8,128)(2,1)S(1)} all-gather(bf16[32,640]{1,0:T(8,128)(2,1)S(1)} %pad_maximum_fusion.1), channel_id=1, replica_groups=mesh['x'=4,'y'=8,'z'=16,'c'=2] {'z'}, dimensions={0}, use_global_device_ids=true | all-gather | bytes 696320 | tf_op jit(solution)/shard_map/all_gather | solution.py:82
  111.2 0.2 convert_reduce_fusion.1
  111.5 0.3 multiply_convert_fusion
  111.8 13.1 %collective-permute-start.2 = (bf16[64,512]{1,0:T(8,128)(2,1)S(1)}, bf16[64,512]{1,0:T(8,128)(2,1)S(1)}, u32[]{:S(2)}, u32[]{:S(2)}) collective-permute-start(bf16[64,512]{1,0:T(8,128)(2,1)S(1)} %dynamic-slice_bitcast_fusion), channel_id=1, source_target_pairs={{0,1},{1,0},{2,3},{3,2},{4,5},{5,4},{6,7},{7,6},{8,9},{9,8},{10,11... | collective-permute-start | bytes 196616 | tf_op jit(solution)/shard_map/ppermute | solution.py:92
  124.9 0.1 convert_reduce_fusion
  125.0 0.0 all-gather.2.cloned.1.call-done
  125.1 3.2 %fusion.5 = bf16[512,512]{1,0:T(8,128)(2,1)S(1)} fusion(bf16[2048,512]{1,0:T(8,128)(2,1)} %all-gather.2.cloned.1.call-done, s32[512]{0:T(512)S(1)} %fusion.34, f32[512]{0:T(512)S(1)} %convert_reduce_fusion, bf16[512,640]{1,0:T(8,128)(2,1)S(1)} %all_gather.10), kind=kOutput, calls=%fused_computation.8 | convolution fusion | flops 1077673984 | bytes 3149824 | tf_op jit(solution)/shard_map/dot_general | solution.py:99
  128.3 0.3 fusion.20
  128.6 0.0 collective-permute-done.3
  128.6 0.3 fusion.7
  128.8 1.9 %collective-permute-start.4 = (bf16[256,512]{1,0:T(8,128)(2,1)S(1)}, bf16[256,512]{1,0:T(8,128)(2,1)S(1)}, u32[]{:S(2)}, u32[]{:S(2)}) collective-permute-start(bf16[256,512]{1,0:T(8,128)(2,1)S(1)} %fusion.7), channel_id=1, source_target_pairs={{0,1},{1,0},{2,3},{3,2},{4,5},{5,4},{6,7},{7,6},{8,9},{9,8},{10,11... | collective-permute-start | bytes 786440 | tf_op jit(solution)/shard_map/ppermute | solution.py:117
  130.8 0.0 collective-permute-done.2
  130.8 0.6 bitcast_add_fusion
  131.4 0.2 fusion.23
  131.7 0.6 collective-permute-done.4
  132.3 1.1 fusion.6
  (17 shorter events, 0.3 us)
Async XLA Ops:
  7.2 24.4 %copy-start = (bf16[128,4096]{1,0:T(8,128)(2,1)S(1)}, bf16[128,4096]{1,0:T(8,128)(2,1)}, u32[]{:S(2)}) copy-start(bf16[128,4096]{1,0:T(8,128)(2,1)} %param.8) | copy-start | bytes 3145732
  7.2 27.5 %copy-start.1 = (bf16[256,512]{1,0:T(8,128)(2,1)S(1)}, bf16[256,512]{1,0:T(8,128)(2,1)}, u32[]{:S(2)}) copy-start(bf16[256,512]{1,0:T(8,128)(2,1)} %param.12) | copy-start | bytes 786436
  7.2 27.5 %collective-permute-start = (bf16[256,512]{1,0:T(8,128)(2,1)}, bf16[256,512]{1,0:T(8,128)(2,1)S(1)}, u32[]{:S(2)}, u32[]{:S(2)}) collective-permute-start(bf16[256,512]{1,0:T(8,128)(2,1)} %param.12), channel_id=1, source_target_pairs={{0,1},{1,0},{2,3},{3,2},{4,5},{5,4},{6,7},{7,6},{8,9},{9,8},{10,11... | collective-permute-start | bytes 786440 | tf_op jit(solution)/shard_map/ppermute | solution.py:33
  25.0 21.0 %all-to-all-start = ((bf16[8,8,1024]{2,1,0:T(8,128)(2,1)}), bf16[8,8,1024]{2,1,0:T(8,128)(2,1)S(1)}, u32[]{:S(2)}, u32[]{:S(2)}) async-start(bf16[8,8,1024]{2,1,0:T(8,128)(2,1)} %bitcast.1), calls=%async_computation | async-start | bytes 262144 | tf_op jit(solution)/shard_map/all_to_all | solution.py:39
  30.8 94.3 %all-gather.2.cloned.1.call-start = ((), (), s32[]{:S(2)}) async-start(), calls=%async_computation.2 | async-start | bytes 2162688 | tf_op jit(solution)/shard_map/all_gather | solution.py:31
  35.6 20.8 %collective-permute-start.1 = (bf16[2,256,512]{2,1,0:T(8,128)(2,1)}, bf16[2,256,512]{2,1,0:T(8,128)(2,1)S(1)}, u32[]{:S(2)}, u32[]{:S(2)}) collective-permute-start(bf16[2,256,512]{2,1,0:T(8,128)(2,1)} %maximum_select_fusion.2), channel_id=1, source_target_pairs={{0,2},{2,0},{4,6},{6,4},{8,10},{10,8},{12,14},{14,12},{16,18},{18,... | collective-permute-start | bytes 1572872 | tf_op jit(solution)/shard_map/ppermute | solution.py:34
  56.6 25.4 %copy-start.2 = (s32[32]{0:T(128)S(1)}, s32[32]{0:T(128)}, u32[]{:S(2)}) copy-start(s32[32]{0:T(128)} %param.9) | copy-start | bytes 388
  57.8 25.3 %all-to-all-start.1 = ((bf16[8,32,512]{2,1,0:T(8,128)(2,1)}), bf16[8,32,512]{2,1,0:T(8,128)(2,1)S(1)}, u32[]{:S(2)}, u32[]{:S(2)}) async-start(bf16[8,32,512]{2,1,0:T(8,128)(2,1)} %bitcast.9), calls=%async_computation.1 | async-start | bytes 524288 | tf_op jit(solution)/shard_map/all_to_all | solution.py:65
  63.7 64.8 %collective-permute-start.3 = (bf16[256,512]{1,0:T(8,128)(2,1)S(1)}, bf16[256,512]{1,0:T(8,128)(2,1)S(1)}, u32[]{:S(2)}, u32[]{:S(2)}) collective-permute-start(bf16[256,512]{1,0:T(8,128)(2,1)S(1)} %get-tuple-element.7), channel_id=1, source_target_pairs={{0,2},{2,0},{4,6},{6,4},{8,10},{10,8},{12,14},{14,12},{16,18},{18,... | collective-permute-start | bytes 786440 | tf_op jit(solution)/shard_map/ppermute | solution.py:62
  111.8 18.9 %collective-permute-start.2 = (bf16[64,512]{1,0:T(8,128)(2,1)S(1)}, bf16[64,512]{1,0:T(8,128)(2,1)S(1)}, u32[]{:S(2)}, u32[]{:S(2)}) collective-permute-start(bf16[64,512]{1,0:T(8,128)(2,1)S(1)} %dynamic-slice_bitcast_fusion), channel_id=1, source_target_pairs={{0,1},{1,0},{2,3},{3,2},{4,5},{5,4},{6,7},{7,6},{8,9},{9,8},{10,11... | collective-permute-start | bytes 196616 | tf_op jit(solution)/shard_map/ppermute | solution.py:92
  128.8 3.4 %collective-permute-start.4 = (bf16[256,512]{1,0:T(8,128)(2,1)S(1)}, bf16[256,512]{1,0:T(8,128)(2,1)S(1)}, u32[]{:S(2)}, u32[]{:S(2)}) collective-permute-start(bf16[256,512]{1,0:T(8,128)(2,1)S(1)} %fusion.7), channel_id=1, source_target_pairs={{0,1},{1,0},{2,3},{3,2},{4,5},{5,4},{6,7},{7,6},{8,9},{9,8},{10,11... | collective-permute-start | bytes 786440 | tf_op jit(solution)/shard_map/ppermute | solution.py:117
Sparse Core Ops, SparseCore 0:
  34.3 80.7 all-gather.1

commit v4 on v3

--- a/solution.py
+++ b/solution.py
@@ -30,8 +30,8 @@
 
     cot_slots = lax.all_gather(cotangent, fsdp, axis=0, tiled=True)
 
-    w_chip = both(c, weight, lax.ppermute(weight, "c", SWAP), 0)
-    w_quad = both(b, w_chip, lax.ppermute(w_chip, "z", flip), 0).reshape(quad, cols)
+    w_pair = both(b, weight, lax.ppermute(weight, "z", flip), 0)
+    w_quad = both(c, w_pair, lax.ppermute(w_pair, "c", SWAP), 1).reshape(quad, cols)
 
     share = local // nx
     sent = lax.dynamic_slice_in_dim(rows, lax.axis_index("x") * share, share, 0)
@@ -89,9 +89,6 @@
     pick = (slots[:, None] == place[None, :]).astype(BF)
     at_slots = jnp.dot(pick, part[:, :cols], preferred_element_type=F32)
     act = (at_slots * jax.nn.sigmoid(at_slots)).astype(BF).reshape(2, 2 * groups, cols)
-    act_other = lax.ppermute(at(act, 1 - c), "c", SWAP)
-    activated = at(act, c) + act_other
-
     hf = part[:, :cols].astype(F32)
     imp = part[:, cols : cols + 1].astype(F32)
     slots = jnp.arange(2 * groups * groups, dtype=jnp.int32)
@@ -114,8 +111,11 @@
             )
         return out
 
-    other = lax.ppermute(product(1 - c).astype(BF), "c", SWAP)
+    half = product(1 - c).astype(BF)
+    half, act_sent = lax.optimization_barrier((half, at(act, 1 - c)))
+    other = lax.ppermute(half, "c", SWAP)
     weight_grad = product(c) + other.astype(F32)
+    activated = at(act, c) + lax.ppermute(act_sent, "c", SWAP)
     return activated, weight_grad
 
 

time: 141 us -> 141 us (level)
  waiting for transfers between devices: 9.53 us -> 14.3 us
  starting transfers between devices: 48.9 us -> 46.2 us
    ppermute x4, starting transfers between devices: 34.3 us -> 18.7 us  [the longest x1 8.66 us: shards(): other = lax.ppermute(half, 'c', SWAP)]
    all_to_all x1, starting transfers between devices: 5.82 us -> 17.6 us  [shards(): lax.all_to_all(sent, 'z', 0, 0, tiled=True, axis_index_groups=stride2)]
    all_gather x1, waiting for transfers between devices: 0.02 us -> 3.42 us  [shards(): cot_slots = lax.all_gather(cotangent, fsdp, axis=0, tiled=True)]
    all_to_all x1, waiting for transfers between devices: 1.06 us -> 4.24 us  [shards(): lax.all_to_all(partial.reshape(nj, local, cols), 'z', 0, 0, tiled=True, a...]
    all_to_all x1, waiting for transfers between devices: 7.16 us -> 5.02 us  [shards(): lax.all_to_all(sent, 'z', 0, 0, tiled=True, axis_index_groups=stride2)]
    all_to_all x1, starting transfers between devices: 5.77 us -> 7.71 us  [shards(): lax.all_to_all(partial.reshape(nj, local, cols), 'z', 0, 0, tiled=True, a...]
    all_gather x1, blocking collectives: 28.1 us -> 26.5 us  [shards(): part = lax.all_gather(payload, 'z', axis=0, tiled=True)]
  transfers between devices with their start and end apart: 8 -> 8, of which waited for: 3 -> 4; matrix products, arithmetic and copies ran while one was open for 9% -> 9% of each run, Pallas kernels for 0% -> 0%
where the time goes in v4:
time: 141 us
  blocking collectives  52.3 us (37%)
  starting transfers between devices  46.2 us (33%)
  waiting for transfers between devices  14.3 us (10%)
  between operations  14.3 us (10%)
  matrix products  8.86 us (6%)
  other arithmetic  3.06 us (2%)
  local copies, waits for them, and re-layouts  1.81 us (1%)
    all_gather x1, blocking collectives, shards(): part = lax.all_gather(payload, 'z', axis=0, tiled=True)  26.5 us
    all_to_all x1, starting transfers between devices, shards(): lax.all_to_all(sent, 'z', 0, 0, tiled=True, axis_index_groups=stride2)  17.6 us
    psum x1, blocking collectives, shards(): scores = lax.psum(score, 'y')  15.5 us
    all_gather x1, blocking collectives, shards(): lax.all_gather(jnp.concatenate([came, thirds], 0), 'x', axis=1, tiled=True)  10.4 us
    ppermute x1, starting transfers between devices, shards(): other = lax.ppermute(half, 'c', SWAP)  8.66 us
    all_to_all x1, starting transfers between devices, shards(): lax.all_to_all(partial.reshape(nj, local, cols), 'z', 0, 0, tiled=True, a...  7.71 us
    all_to_all x1, waiting for transfers between devices, shards(): lax.all_to_all(sent, 'z', 0, 0, tiled=True, axis_index_groups=stride2)  5.02 us
    ppermute x1, starting transfers between devices, shards(): w_pair = both(b, weight, lax.ppermute(weight, 'z', flip), 0)  4.96 us
  transfers between devices with their start and end apart: 8, of which 4 were waited for; matrix products, arithmetic and copies ran while one was open for 9% of the time, Pallas kernels for 0%

profile of v4, /device:TPU:1, one launch (start us, length us, event | category | flops | bytes accessed | tf_op | source)
XLA Modules:
  0.0 140.9 jit_solution(15952978908820407630)
XLA Ops:
  7.2 0.0 copy-start
  7.2 0.0 copy-start.1
  7.2 5.0 %collective-permute-start = (bf16[256,512]{1,0:T(8,128)(2,1)}, bf16[256,512]{1,0:T(8,128)(2,1)S(1)}, u32[]{:S(2)}, u32[]{:S(2)}) collective-permute-start(bf16[256,512]{1,0:T(8,128)(2,1)} %param.12), channel_id=1, source_target_pairs={{0,2},{2,0},{4,6},{6,4},{8,10},{10,8},{12,14},{14,12},{16,18},{18,... | collective-permute-start | bytes 786440 | tf_op jit(solution)/shard_map/ppermute | solution.py:33
  12.2 1.6 %constant_dynamic-slice_fusion.4 = bf16[8,8192]{1,0:T(8,128)(2,1)} fusion(bf16[32,8192]{1,0:T(8,128)(2,1)} %param.11, s32[]{:T(128)S(6)} %select_n.107), kind=kLoop, calls=%fused_computation.65 | loop fusion | bytes 262148 | tf_op jit(solution)/shard_map/dynamic_slice | solution.py:37
  13.7 17.6 %all-to-all-start = ((bf16[8,8,1024]{2,1,0:T(8,128)(2,1)}), bf16[8,8,1024]{2,1,0:T(8,128)(2,1)S(1)}, u32[]{:S(2)}, u32[]{:S(2)}) async-start(bf16[8,8,1024]{2,1,0:T(8,128)(2,1)} %bitcast.1), calls=%async_computation | async-start | bytes 262144 | tf_op jit(solution)/shard_map/all_to_all | solution.py:39
  31.3 0.0 all-gather.2.cloned.1.call-start
  31.3 0.7 all-gather.2.cloned.1.call-update
  32.0 0.0 copy-done
  32.0 1.5 %fusion.9 = f32[32]{0:T(128)S(1)} fusion(bf16[32,4096]{1,0:T(8,128)(2,1)} %param.7, bf16[128,4096]{1,0:T(8,128)(2,1)S(1)} %copy-done), kind=kOutput, calls=%fused_computation.17 | convolution fusion | flops 33562592 | bytes 1310848 | tf_op jit(solution)/shard_map/dot_general | solution.py:41
  33.6 0.9 fusion.8
  34.5 0.7 fusion.46
  35.1 0.1 pad_maximum_fusion.2
  35.2 0.0 collective-permute-done
  35.2 0.0 copy-done.1
  35.2 0.9 maximum_select_fusion.2
  36.1 3.1 %collective-permute-start.1 = (bf16[2,256,512]{2,1,0:T(8,128)(2,1)}, bf16[2,256,512]{2,1,0:T(8,128)(2,1)S(1)}, u32[]{:S(2)}, u32[]{:S(2)}) collective-permute-start(bf16[2,256,512]{2,1,0:T(8,128)(2,1)} %maximum_select_fusion.2), channel_id=1, source_target_pairs={{0,1},{1,0},{2,3},{3,2},{4,5},{5,4},{6,7},{7,6},{8,9},{9,8},{10,11... | collective-permute-start | bytes 1572872 | tf_op jit(solution)/shard_map/ppermute | solution.py:34
  39.3 0.1 maximum_select_fusion.1
  39.3 5.0 %all-to-all-done = bf16[8,8,1024]{2,1,0:T(8,128)(2,1)S(1)} async-done(((bf16[8,8,1024]{2,1,0:T(8,128)(2,1)}), bf16[8,8,1024]{2,1,0:T(8,128)(2,1)S(1)}, u32[]{:S(2)}, u32[]{:S(2)}) %all-to-all-start) | async-done | bytes 131104 | tf_op jit(solution)/shard_map/all_to_all | solution.py:39
  44.4 10.4 %all_gather.9 = bf16[9,32,1024]{2,1,0:T(8,128)(2,1)S(1)} all-gather(bf16[9,8,1024]{2,1,0:T(8,128)(2,1)S(1)} %pad_maximum_fusion), channel_id=1, replica_groups=mesh['x'=4,'y'=8,'z'=16,'c'=2] {'x'}, dimensions={1}, use_global_device_ids=true | all-gather | bytes 737280 | tf_op jit(solution)/shard_map/all_gather | solution.py:51
  54.8 0.0 collective-permute-done.1
  54.8 0.1 maximum_select_fusion
  55.0 0.0 copy-start.2
  55.0 1.2 convolution_convert_fusion
  56.1 7.7 %all-to-all-start.1 = ((bf16[8,32,512]{2,1,0:T(8,128)(2,1)}), bf16[8,32,512]{2,1,0:T(8,128)(2,1)S(1)}, u32[]{:S(2)}, u32[]{:S(2)}) async-start(bf16[8,32,512]{2,1,0:T(8,128)(2,1)} %bitcast.9), calls=%async_computation.1 | async-start | bytes 524288 | tf_op jit(solution)/shard_map/all_to_all | solution.py:65
  63.9 0.1 reshape.200
  64.1 2.2 %collective-permute-start.2 = (bf16[256,512]{1,0:T(8,128)(2,1)S(1)}, bf16[256,512]{1,0:T(8,128)(2,1)S(1)}, u32[]{:S(2)}, u32[]{:S(2)}) collective-permute-start(bf16[256,512]{1,0:T(8,128)(2,1)S(1)} %get-tuple-element.9), channel_id=1, source_target_pairs={{0,2},{2,0},{4,6},{6,4},{8,10},{10,8},{12,14},{14,12},{16,18},{18,... | collective-permute-start | bytes 786440 | tf_op jit(solution)/shard_map/ppermute | solution.py:62
  66.3 15.5 %psum.7 = f32[32]{0:T(128)S(1)} all-reduce(f32[32]{0:T(128)S(1)} %reduce_sum.43), channel_id=1, replica_groups=mesh['x'=4,'y'=8,'z'=16,'c'=2] {'y'}, use_global_device_ids=true, to_apply=%region_3.4 | all-reduce | flops 32 | bytes 256 | tf_op jit(solution)/shard_map/psum | solution.py:63
  81.7 0.0 copy-done.2
  81.7 0.1 broadcast_select_fusion
  81.8 4.2 %all-to-all-done.1 = bf16[8,32,512]{2,1,0:T(8,128)(2,1)S(1)} async-done(((bf16[8,32,512]{2,1,0:T(8,128)(2,1)}), bf16[8,32,512]{2,1,0:T(8,128)(2,1)S(1)}, u32[]{:S(2)}, u32[]{:S(2)}) %all-to-all-start.1) | async-done | bytes 262176 | tf_op jit(solution)/shard_map/all_to_all | solution.py:65
  86.1 26.5 %all_gather.10 = bf16[512,640]{1,0:T(8,128)(2,1)S(1)} all-gather(bf16[32,640]{1,0:T(8,128)(2,1)S(1)} %pad_maximum_fusion.1), channel_id=1, replica_groups=mesh['x'=4,'y'=8,'z'=16,'c'=2] {'z'}, dimensions={0}, use_global_device_ids=true | all-gather | bytes 696320 | tf_op jit(solution)/shard_map/all_gather | solution.py:82
  112.6 0.2 convert_reduce_fusion.1
  112.9 0.3 multiply_convert_fusion
  113.2 0.1 convert_reduce_fusion
  113.3 3.4 %all-gather.2.cloned.1.call-done = bf16[2048,512]{1,0:T(8,128)(2,1)} async-done(((bf16[64,512]{1,0:T(8,128)(2,1)}), bf16[2048,512]{1,0:T(8,128)(2,1)}) %all-gather.2.cloned.1.call-update) | async-done | bytes 2097168 | tf_op jit(solution)/shard_map/all_gather | solution.py:31
  116.7 3.2 %fusion.5 = bf16[512,512]{1,0:T(8,128)(2,1)S(1)} fusion(bf16[2048,512]{1,0:T(8,128)(2,1)} %all-gather.2.cloned.1.call-done, s32[512]{0:T(512)S(1)} %fusion.34, f32[512]{0:T(512)S(1)} %convert_reduce_fusion, bf16[512,640]{1,0:T(8,128)(2,1)S(1)} %all_gather.10), kind=kOutput, calls=%fused_computation.8 | convolution fusion | flops 1077673984 | bytes 3149824 | tf_op jit(solution)/shard_map/dot_general | solution.py:96
  120.0 0.3 fusion.23
  120.2 0.0 collective-permute-done.2
  120.2 0.3 fusion.7
  120.5 8.7 %collective-permute-start.4 = (bf16[256,512]{1,0:T(8,128)(2,1)S(1)}, bf16[256,512]{1,0:T(8,128)(2,1)S(1)}, u32[]{:S(2)}, u32[]{:S(2)}) collective-permute-start(bf16[256,512]{1,0:T(8,128)(2,1)S(1)} %fusion.7), channel_id=1, source_target_pairs={{0,1},{1,0},{2,3},{3,2},{4,5},{5,4},{6,7},{7,6},{8,9},{9,8},{10,11... | collective-permute-start | bytes 786440 | tf_op jit(solution)/shard_map/ppermute | solution.py:116
  129.2 1.9 %collective-permute-start.3 = (bf16[64,512]{1,0:T(8,128)(2,1)S(1)}, bf16[64,512]{1,0:T(8,128)(2,1)S(1)}, u32[]{:S(2)}, u32[]{:S(2)}) collective-permute-start(bf16[64,512]{1,0:T(8,128)(2,1)S(1)} %dynamic-slice_bitcast_fusion), channel_id=1, source_target_pairs={{0,1},{1,0},{2,3},{3,2},{4,5},{5,4},{6,7},{7,6},{8,9},{9,8},{10,11... | collective-permute-start | bytes 196616 | tf_op jit(solution)/shard_map/ppermute | solution.py:118
  131.1 0.3 fusion.20
  131.4 1.0 collective-permute-done.3
  132.3 0.6 bitcast_add_fusion
  133.0 0.0 collective-permute-done.4
  133.0 1.0 fusion.6
  (17 shorter events, 0.3 us)
Async XLA Ops:
  7.2 24.9 %copy-start = (bf16[128,4096]{1,0:T(8,128)(2,1)S(1)}, bf16[128,4096]{1,0:T(8,128)(2,1)}, u32[]{:S(2)}) copy-start(bf16[128,4096]{1,0:T(8,128)(2,1)} %param.8) | copy-start | bytes 3145732
  7.2 28.0 %copy-start.1 = (bf16[256,512]{1,0:T(8,128)(2,1)S(1)}, bf16[256,512]{1,0:T(8,128)(2,1)}, u32[]{:S(2)}) copy-start(bf16[256,512]{1,0:T(8,128)(2,1)} %param.12) | copy-start | bytes 786436
  7.2 28.0 %collective-permute-start = (bf16[256,512]{1,0:T(8,128)(2,1)}, bf16[256,512]{1,0:T(8,128)(2,1)S(1)}, u32[]{:S(2)}, u32[]{:S(2)}) collective-permute-start(bf16[256,512]{1,0:T(8,128)(2,1)} %param.12), channel_id=1, source_target_pairs={{0,2},{2,0},{4,6},{6,4},{8,10},{10,8},{12,14},{14,12},{16,18},{18,... | collective-permute-start | bytes 786440 | tf_op jit(solution)/shard_map/ppermute | solution.py:33
  13.7 30.6 %all-to-all-start = ((bf16[8,8,1024]{2,1,0:T(8,128)(2,1)}), bf16[8,8,1024]{2,1,0:T(8,128)(2,1)S(1)}, u32[]{:S(2)}, u32[]{:S(2)}) async-start(bf16[8,8,1024]{2,1,0:T(8,128)(2,1)} %bitcast.1), calls=%async_computation | async-start | bytes 262144 | tf_op jit(solution)/shard_map/all_to_all | solution.py:39
  31.3 85.4 %all-gather.2.cloned.1.call-start = ((), (), s32[]{:S(2)}) async-start(), calls=%async_computation.2 | async-start | bytes 2162688 | tf_op jit(solution)/shard_map/all_gather | solution.py:31
  36.1 18.7 %collective-permute-start.1 = (bf16[2,256,512]{2,1,0:T(8,128)(2,1)}, bf16[2,256,512]{2,1,0:T(8,128)(2,1)S(1)}, u32[]{:S(2)}, u32[]{:S(2)}) collective-permute-start(bf16[2,256,512]{2,1,0:T(8,128)(2,1)} %maximum_select_fusion.2), channel_id=1, source_target_pairs={{0,1},{1,0},{2,3},{3,2},{4,5},{5,4},{6,7},{7,6},{8,9},{9,8},{10,11... | collective-permute-start | bytes 1572872 | tf_op jit(solution)/shard_map/ppermute | solution.py:34
  55.0 26.8 %copy-start.2 = (s32[32]{0:T(128)S(1)}, s32[32]{0:T(128)}, u32[]{:S(2)}) copy-start(s32[32]{0:T(128)} %param.9) | copy-start | bytes 388
  56.1 29.9 %all-to-all-start.1 = ((bf16[8,32,512]{2,1,0:T(8,128)(2,1)}), bf16[8,32,512]{2,1,0:T(8,128)(2,1)S(1)}, u32[]{:S(2)}, u32[]{:S(2)}) async-start(bf16[8,32,512]{2,1,0:T(8,128)(2,1)} %bitcast.9), calls=%async_computation.1 | async-start | bytes 524288 | tf_op jit(solution)/shard_map/all_to_all | solution.py:65
  64.1 56.2 %collective-permute-start.2 = (bf16[256,512]{1,0:T(8,128)(2,1)S(1)}, bf16[256,512]{1,0:T(8,128)(2,1)S(1)}, u32[]{:S(2)}, u32[]{:S(2)}) collective-permute-start(bf16[256,512]{1,0:T(8,128)(2,1)S(1)} %get-tuple-element.9), channel_id=1, source_target_pairs={{0,2},{2,0},{4,6},{6,4},{8,10},{10,8},{12,14},{14,12},{16,18},{18,... | collective-permute-start | bytes 786440 | tf_op jit(solution)/shard_map/ppermute | solution.py:62
  120.5 12.5 %collective-permute-start.4 = (bf16[256,512]{1,0:T(8,128)(2,1)S(1)}, bf16[256,512]{1,0:T(8,128)(2,1)S(1)}, u32[]{:S(2)}, u32[]{:S(2)}) collective-permute-start(bf16[256,512]{1,0:T(8,128)(2,1)S(1)} %fusion.7), channel_id=1, source_target_pairs={{0,1},{1,0},{2,3},{3,2},{4,5},{5,4},{6,7},{7,6},{8,9},{9,8},{10,11... | collective-permute-start | bytes 786440 | tf_op jit(solution)/shard_map/ppermute | solution.py:116
  129.2 3.1 %collective-permute-start.3 = (bf16[64,512]{1,0:T(8,128)(2,1)S(1)}, bf16[64,512]{1,0:T(8,128)(2,1)S(1)}, u32[]{:S(2)}, u32[]{:S(2)}) collective-permute-start(bf16[64,512]{1,0:T(8,128)(2,1)S(1)} %dynamic-slice_bitcast_fusion), channel_id=1, source_target_pairs={{0,1},{1,0},{2,3},{3,2},{4,5},{5,4},{6,7},{7,6},{8,9},{9,8},{10,11... | collective-permute-start | bytes 196616 | tf_op jit(solution)/shard_map/ppermute | solution.py:118
Sparse Core Ops, SparseCore 0:
  34.8 81.8 all-gather.1

commit v5 on v2

v5 whole, which is shorter than its diff:
```python
import jax
import jax.numpy as jnp
from jax import lax
from jax.sharding import Mesh, PartitionSpec as P

BF = jnp.bfloat16
F32 = jnp.float32
SWAP = [(0, 1), (1, 0)]


def both(flag, own, other, axis):
    return jnp.where(flag == 0, jnp.stack([own, other], axis), jnp.stack([other, own], axis))


def at(array, index, axis=0):
    return lax.dynamic_index_in_dim(array, index, axis, keepdims=False)


def shards(proj_grads, inv_factor, counts, dests, rows, weight, cotangent):
    nz = lax.axis_size("z")
    nj, groups = nz // 2, 2 * nz
    z, c = lax.axis_index("z"), lax.axis_index("c")
    b = z % 2
    local, width = rows.shape
    piece, cols = weight.shape
    quad = 4 * piece
    stride2 = [[2 * i + k for i in range(nj)] for k in range(2)]
    flip = [(i, i ^ 1) for i in range(nz)]

    def pair(x):
        return lax.ppermute(x, "z", flip)

    def core(x):
        return lax.ppermute(x, "c", SWAP)

    def exchange(x):
        return lax.all_to_all(x, "z", 0, 0, tiled=True, axis_index_groups=stride2)

    w_pair = both(b, weight, pair(weight), 0)
    w_quad = both(c, w_pair, core(w_pair), 1).reshape(quad, cols)

    came = exchange(rows.reshape(local, nj, quad).transpose(1, 0, 2))

    projected = lax.dot_general(
        proj_grads, inv_factor, (((1,), (1,)), ((), ())), preferred_element_type=F32
    )
    score = lax.psum(jnp.sum(projected * projected, axis=1), "x")
    came, score = lax.optimization_barrier((came, score))
    x_class = came.reshape(nj * local, quad)

    slots = cotangent.reshape(nj, 2, 2, 2, cols)
    slots = both(c, at(slots, c, 2), core(at(slots, 1 - c, 2)), 0)
    slots = both(b, at(slots, b, 2), pair(at(slots, 1 - b, 2)), 0)
    slots = slots.transpose(2, 0, 1, 3, 4).reshape(nj, 8, cols)

    target = dests[:, 0]
    dest_hot = (target[:, None] == jnp.arange(groups, dtype=jnp.int32)[None, :]).astype(jnp.int32)
    order = jnp.arange(local, dtype=jnp.int32)
    earlier = (order[:, None] > order[None, :]).astype(jnp.int32)
    rank = jnp.sum(jnp.dot(earlier, dest_hot) * dest_hot, axis=1)
    place = 2 * target + rank
    placer = (place[:, None] == jnp.arange(2 * groups, dtype=jnp.int32)[None, :]).astype(BF)

    partial = jnp.dot(x_class, w_quad, preferred_element_type=F32).astype(BF)
    sent = jnp.concatenate([partial.reshape(nj, local, cols), slots], 1)
    sent, score = lax.optimization_barrier((sent, score))
    came = exchange(sent)
    scores = lax.psum(score, "y")
    importance = (counts.astype(F32) * proj_grads.shape[1] / scores).astype(BF)
    x_blocks = x_class.reshape(nj * local, 2, 2 * piece)
    importance, x_sent = lax.optimization_barrier((importance, at(x_blocks, 1 - b, 1)))
    hidden = jnp.sum(came[:, :local].astype(F32), axis=0)
    cot = jnp.dot(placer, came[:, local:].reshape(2 * groups, cols), preferred_element_type=F32)
    squash = jax.nn.sigmoid(hidden)
    act = (hidden * squash).astype(BF)
    grad = importance[:, None].astype(F32) * cot * squash * (1.0 + hidden * (1.0 - squash))
    grad = jnp.broadcast_to(grad.astype(BF)[None], (nj, local, cols))
    act = lax.dot_general(placer, act, (((0,), (0,)), ((), ())), preferred_element_type=F32)
    act = act.astype(BF).reshape(nj, 8, cols)

    came = exchange(jnp.concatenate([grad, act], 1))
    grad = came[:, :local].reshape(nj * local, cols)
    grad_flip = pair(grad)
    x_same, x_flip = at(x_blocks, b, 1), pair(x_sent)

    def product(which):
        out = 0.0
        for x_part, g_part in ((x_same, grad), (x_flip, grad_flip)):
            out = out + lax.dot_general(
                lax.dynamic_slice_in_dim(x_part, which * piece, piece, 1),
                g_part,
                (((0,), (0,)), ((), ())),
                preferred_element_type=F32,
            )
        return out

    weight_grad = core(product(1 - c).astype(BF)).astype(F32) + product(c)

    act = came[:, local:].reshape(nj, 2, 2, 2, cols)
    act = both(b, at(act, b, 1), pair(at(act, 1 - b, 1)), 1)
    act = both(c, at(act, c, 2), core(at(act, 1 - c, 2)), 2)
    return act.reshape(2 * groups, cols), weight_grad


def solution(mesh, nx=4):
    dp, fsdp = mesh.devices.shape
    fine = Mesh(mesh.devices.reshape(nx, dp // nx, fsdp // 2, 2), ("x", "y", "z", "c"))
    dp, fsdp = ("x", "y"), ("z", "c")
    in_specs = (
        P(fsdp, None),
        P(dp, None),
        P(fsdp),
        P(fsdp, None),
        P(fsdp, None),
        P(fsdp, dp),
        P(fsdp, dp),
    )
    out_specs = (P(fsdp, dp), P(fsdp, dp))
    return jax.shard_map(shards, mesh=fine, in_specs=in_specs, out_specs=out_specs, check_vma=False)
```

time: 173 us -> 153 us (0.88)
  blocking collectives: 49.1 us -> 22.9 us
  between operations: 14.4 us -> 1.04 us
  waiting for transfers between devices: 30.3 us -> 43.6 us
  starting transfers between devices: 65.5 us -> 73.2 us
  matrix products: 9.63 us -> 3.41 us
  local copies, waits for them, and re-layouts: 2.73 us -> 6.3 us
    all_gather x1 -> x0, blocking collectives: 26.2 us -> none  [shards(): own = lax.all_gather(payload, 'z', axis=0, tiled=True)]
    all_to_all x2 -> x3, waiting for transfers between devices: 2.28 us -> 18 us  [exchange(): return lax.all_to_all(x, 'z', 0, 0, tiled=True, axis_index_groups=stride2)]
    all_to_all x2 -> x3, starting transfers between devices: 30.6 us -> 39.2 us  [exchange(): return lax.all_to_all(x, 'z', 0, 0, tiled=True, axis_index_groups=stride2)]
    dot_general x8 -> x6, matrix products: 7.78 us -> 2.27 us  [the longest x4 1.8 us: product(): lax.dot_general(lax.dynamic_slice_in_dim(x_part, which * piece, piece, 1)...]
    ppermute x6 -> x9, waiting for transfers between devices: 28 us -> 25.6 us  [the longest x5 24.3 us: pair(): return lax.ppermute(x, 'z', flip)]
    ppermute x6 -> x9, starting transfers between devices: 34.9 us -> 34 us  [the longest x4 21.3 us: core(): return lax.ppermute(x, 'c', SWAP)]
  transfers between devices with their start and end apart: 9 -> 12, of which waited for: 3 -> 6; matrix products, arithmetic and copies ran while one was open for 6% -> 3% of each run, Pallas kernels for 0% -> 0%
where the time goes in v5:
time: 153 us
  starting transfers between devices  73.2 us (48%)
  waiting for transfers between devices  43.6 us (28%)
  blocking collectives  22.9 us (15%)
  local copies, waits for them, and re-layouts  6.3 us (4%)
  matrix products  3.41 us (2%)
  other arithmetic  2.26 us (1%)
    all_to_all x3, starting transfers between devices, exchange(): return lax.all_to_all(x, 'z', 0, 0, tiled=True, axis_index_groups=stride2)  39.2 us
    ppermute x5, waiting for transfers between devices, pair(): return lax.ppermute(x, 'z', flip)  24.3 us
    ppermute x4, starting transfers between devices, core(): return lax.ppermute(x, 'c', SWAP)  21.3 us
    all_to_all x3, waiting for transfers between devices, exchange(): return lax.all_to_all(x, 'z', 0, 0, tiled=True, axis_index_groups=stride2)  18 us
    psum x1, blocking collectives, shards(): scores = lax.psum(score, 'y')  14.5 us
    ppermute x5, starting transfers between devices, pair(): return lax.ppermute(x, 'z', flip)  12.7 us
    psum x1, blocking collectives, shards(): score = lax.psum(jnp.sum(projected * projected, axis=1), 'x')  8.47 us
  transfers between devices with their start and end apart: 12, of which 6 were waited for; matrix products, arithmetic and copies ran while one was open for 3% of the time, Pallas kernels for 0%

profile of v5, /device:TPU:1, one launch (start us, length us, event | category | flops | bytes accessed | tf_op | source)
XLA Modules:
  0.0 152.7 jit_solution(9707203175069201336)
XLA Ops:
  0.6 1.4 copy.23
  2.1 1.1 copy.17
  3.2 19.4 %all-to-all-start = ((bf16[8,32,1024]{2,1,0:T(8,128)(2,1)}), bf16[8,32,1024]{2,1,0:T(8,128)(2,1)S(1)}, u32[]{:S(2)}, u32[]{:S(2)}) async-start(bf16[8,32,1024]{2,1,0:T(8,128)(2,1)} %copy.17), calls=%async_computation | async-start | bytes 1048576 | tf_op jit(solution)/shard_map/all_to_all | solution.py:37
  22.6 3.1 %collective-permute-start = (bf16[256,512]{1,0:T(8,128)(2,1)S(1)}, bf16[256,512]{1,0:T(8,128)(2,1)S(1)}, u32[]{:S(2)}, u32[]{:S(2)}) collective-permute-start(bf16[256,512]{1,0:T(8,128)(2,1)S(1)} %copy-done.1), channel_id=1, source_target_pairs={{0,2},{2,0},{4,6},{6,4},{8,10},{10,8},{12,14},{14,12},{16,18},{18,... | collective-permute-start | bytes 786440 | tf_op jit(solution)/shard_map/ppermute | solution.py:31
  25.8 0.1 dynamic-slice_bitcast_fusion.3
  25.8 3.1 %collective-permute-start.2 = (bf16[8,2,2,512]{3,2,1,0:T(2,128)(2,1)S(1)}, bf16[8,2,2,512]{3,2,1,0:T(2,128)(2,1)S(1)}, u32[]{:S(2)}, u32[]{:S(2)}) collective-permute-start(bf16[8,2,2,512]{3,2,1,0:T(2,128)(2,1)S(1)} %get-tuple-element.23), channel_id=1, source_target_pairs={{0,1},{1,0},{2,3},{3,2},{4,5},{5,4},{6,7},{7,6},{8,9},{9,8},{10,11... | collective-permute-start | bytes 98312 | tf_op jit(solution)/shard_map/ppermute | solution.py:34
  29.0 0.8 collective-permute-done.2
  29.8 0.1 broadcast_select_fusion
  29.9 21.9 %collective-permute-done = bf16[256,512]{1,0:T(8,128)(2,1)S(1)} collective-permute-done((bf16[256,512]{1,0:T(8,128)(2,1)S(1)}, bf16[256,512]{1,0:T(8,128)(2,1)S(1)}, u32[]{:S(2)}, u32[]{:S(2)}) %collective-permute-start) | collective-permute-done | bytes 262176 | tf_op jit(solution)/shard_map/ppermute | solution.py:31
  51.8 0.1 maximum_select_fusion.2
  51.9 3.7 %collective-permute-start.1 = (bf16[2,256,512]{2,1,0:T(8,128)(2,1)S(1)}, bf16[2,256,512]{2,1,0:T(8,128)(2,1)S(1)}, u32[]{:S(2)}, u32[]{:S(2)}) collective-permute-start(bf16[2,256,512]{2,1,0:T(8,128)(2,1)S(1)} %maximum_select_fusion.2), channel_id=1, source_target_pairs={{0,1},{1,0},{2,3},{3,2},{4,5},{5,4},{6,7},{7,6},{8,9},{9,8},{10,11... | collective-permute-start | bytes 1572872 | tf_op jit(solution)/shard_map/ppermute | solution.py:34
  55.6 0.1 constant_dynamic-slice_fusion.6
  55.7 2.1 %collective-permute-start.3 = (bf16[2,8,2,512]{3,2,0,1:T(2,128)(2,1)S(1)}, bf16[2,8,2,512]{3,2,0,1:T(2,128)(2,1)S(1)}, u32[]{:S(2)}, u32[]{:S(2)}) collective-permute-start(bf16[2,8,2,512]{3,2,0,1:T(2,128)(2,1)S(1)} %bitcast.77), channel_id=1, source_target_pairs={{0,2},{2,0},{4,6},{6,4},{8,10},{10,8},{12,14},{14,12},{16,18},{18,... | collective-permute-start | bytes 98312 | tf_op jit(solution)/shard_map/ppermute | solution.py:31
  57.8 0.6 fusion.6
  58.4 8.5 %psum.14 = f32[32]{0:T(128)S(1)} all-reduce(f32[32]{0:T(128)S(1)} %fusion.6), channel_id=1, replica_groups=mesh['x'=4,'y'=8,'z'=16,'c'=2] {'x'}, use_global_device_ids=true, to_apply=%region_1.2 | all-reduce | flops 32 | bytes 256 | tf_op jit(solution)/shard_map/psum | solution.py:47
  66.9 0.1 fusion.17
  67.1 0.1 maximum_select_fusion.1
  67.2 0.2 maximum_select_fusion
  67.3 0.4 convolution_convert_fusion
  67.8 0.7 pad_maximum_fusion
  68.5 11.6 %all-to-all-start.1 = ((bf16[8,40,512]{2,1,0:T(8,128)(2,1)}), bf16[8,40,512]{2,1,0:T(8,128)(2,1)S(1)}, u32[]{:S(2)}, u32[]{:S(2)}) async-start(bf16[8,40,512]{2,1,0:T(8,128)(2,1)} %pad_maximum_fusion), calls=%async_computation.1 | async-start | bytes 655360 | tf_op jit(solution)/shard_map/all_to_all | solution.py:37
  80.2 0.7 copy-done.4
  80.8 0.1 fusion.5
  81.0 0.4 reshape_reshape.3
  81.3 0.5 constant_dynamic-slice_fusion.4
  82.0 14.5 %psum.15 = f32[32]{0:T(128)S(1)} all-reduce(f32[32]{0:T(128)S(1)} %psum.14), channel_id=1, replica_groups=mesh['x'=4,'y'=8,'z'=16,'c'=2] {'y'}, use_global_device_ids=true, to_apply=%region_2.3 | all-reduce | flops 32 | bytes 256 | tf_op jit(solution)/shard_map/psum | solution.py:68
  96.4 3.7 %all-to-all-done.1 = bf16[8,40,512]{2,1,0:T(8,128)(2,1)S(1)} async-done(((bf16[8,40,512]{2,1,0:T(8,128)(2,1)}), bf16[8,40,512]{2,1,0:T(8,128)(2,1)S(1)}, u32[]{:S(2)}, u32[]{:S(2)}) %all-to-all-start.1) | async-done | bytes 327712 | tf_op jit(solution)/shard_map/all_to_all | solution.py:37
  100.1 0.3 fusion.1
  100.4 0.2 fusion.4
  100.6 0.8 pad_maximum_fusion.1
  101.4 8.1 %all-to-all-start.2 = ((bf16[8,40,512]{2,1,0:T(8,128)(2,1)}), bf16[8,40,512]{2,1,0:T(8,128)(2,1)S(1)}, u32[]{:S(2)}, u32[]{:S(2)}) async-start(bf16[8,40,512]{2,1,0:T(8,128)(2,1)} %pad_maximum_fusion.1), calls=%async_computation.2 | async-start | bytes 655360 | tf_op jit(solution)/shard_map/all_to_all | solution.py:37
  109.5 2.2 %collective-permute-start.6 = (bf16[256,512]{1,0:T(8,128)(2,1)S(1)}, bf16[256,512]{1,0:T(8,128)(2,1)S(1)}, u32[]{:S(2)}, u32[]{:S(2)}) collective-permute-start(bf16[256,512]{1,0:T(8,128)(2,1)S(1)} %bitcast.75), channel_id=1, source_target_pairs={{0,2},{2,0},{4,6},{6,4},{8,10},{10,8},{12,14},{14,12},{16,18},{18,... | collective-permute-start | bytes 786440 | tf_op jit(solution)/shard_map/ppermute | solution.py:31
  111.7 1.1 constant_dynamic-slice_fusion
  112.8 14.4 %all-to-all-done.2 = bf16[8,40,512]{2,1,0:T(8,128)(2,1)S(1)} async-done(((bf16[8,40,512]{2,1,0:T(8,128)(2,1)}), bf16[8,40,512]{2,1,0:T(8,128)(2,1)S(1)}, u32[]{:S(2)}, u32[]{:S(2)}) %all-to-all-start.2) | async-done | bytes 327712 | tf_op jit(solution)/shard_map/all_to_all | solution.py:37
  127.2 1.9 %collective-permute-start.7 = (bf16[256,512]{1,0:T(8,128)(2,1)S(1)}, bf16[256,512]{1,0:T(8,128)(2,1)S(1)}, u32[]{:S(2)}, u32[]{:S(2)}) collective-permute-start(bf16[256,512]{1,0:T(8,128)(2,1)S(1)} %bitcast.64), channel_id=1, source_target_pairs={{0,2},{2,0},{4,6},{6,4},{8,10},{10,8},{12,14},{14,12},{16,18},{18,... | collective-permute-start | bytes 786440 | tf_op jit(solution)/shard_map/ppermute | solution.py:31
  129.1 0.1 constant_dynamic-slice_fusion.3
  129.2 3.4 %collective-permute-start.4 = (bf16[8,2,2,512]{3,2,1,0:T(2,128)(2,1)S(1)}, bf16[8,2,2,512]{3,2,1,0:T(2,128)(2,1)S(1)}, u32[]{:S(2)}, u32[]{:S(2)}) collective-permute-start(bf16[8,2,2,512]{3,2,1,0:T(2,128)(2,1)S(1)} %get-tuple-element.19), channel_id=1, source_target_pairs={{0,2},{2,0},{4,6},{6,4},{8,10},{10,8},{12,14},{14,12},{16,18},{18,... | collective-permute-start | bytes 98312 | tf_op jit(solution)/shard_map/ppermute | solution.py:31
  132.6 0.2 fusion.10
  132.8 2.4 %collective-permute-done.4 = bf16[8,2,2,512]{3,2,1,0:T(2,128)(2,1)S(1)} collective-permute-done((bf16[8,2,2,512]{3,2,1,0:T(2,128)(2,1)S(1)}, bf16[8,2,2,512]{3,2,1,0:T(2,128)(2,1)S(1)}, u32[]{:S(2)}, u32[]{:S(2)}) %collective-permute-start.4) | collective-permute-done | bytes 32800 | tf_op jit(solution)/shard_map/ppermute | solution.py:31
  135.2 0.1 broadcast_select_fusion.2
  135.4 12.6 %collective-permute-start.5 = (bf16[8,2,2,512]{3,2,1,0:T(2,128)(2,1)S(1)}, bf16[8,2,2,512]{3,2,1,0:T(2,128)(2,1)S(1)}, u32[]{:S(2)}, u32[]{:S(2)}) collective-permute-start(bf16[8,2,2,512]{3,2,1,0:T(2,128)(2,1)S(1)} %get-tuple-element.17), channel_id=1, source_target_pairs={{0,1},{1,0},{2,3},{3,2},{4,5},{5,4},{6,7},{7,6},{8,9},{9,8},{10,11... | collective-permute-start | bytes 98312 | tf_op jit(solution)/shard_map/ppermute | solution.py:34
  148.0 0.3 fusion
  148.3 1.9 %collective-permute-start.8 = (bf16[256,512]{1,0:T(8,128)(2,1)S(1)}, bf16[256,512]{1,0:T(8,128)(2,1)S(1)}, u32[]{:S(2)}, u32[]{:S(2)}) collective-permute-start(bf16[256,512]{1,0:T(8,128)(2,1)S(1)} %fusion), channel_id=1, source_target_pairs={{0,1},{1,0},{2,3},{3,2},{4,5},{5,4},{6,7},{7,6},{8,9},{9,8},{10,11... | collective-permute-start | bytes 786440 | tf_op jit(solution)/shard_map/ppermute | solution.py:34
  150.2 0.2 fusion.7
  150.5 0.1 broadcast_select_fusion.3
  150.6 0.7 select_n.134
  151.2 0.5 collective-permute-done.8
  151.7 1.1 convert_add_fusion
  (31 shorter events, 0.4 us)
Async XLA Ops:
  0.6 57.2 %copy-start = (bf16[128,4096]{1,0:T(8,128)(2,1)S(1)}, bf16[128,4096]{1,0:T(8,128)(2,1)}, u32[]{:S(2)}) copy-start(bf16[128,4096]{1,0:T(8,128)(2,1)} %param.8) | copy-start | bytes 3145732
  3.2 19.4 %copy-start.1 = (bf16[256,512]{1,0:T(8,128)(2,1)S(1)}, bf16[256,512]{1,0:T(8,128)(2,1)}, u32[]{:S(2)}) copy-start(bf16[256,512]{1,0:T(8,128)(2,1)} %param.12) | copy-start | bytes 786436
  3.2 22.6 %copy-start.3 = (bf16[64,512]{1,0:T(8,128)(2,1)S(1)}, bf16[64,512]{1,0:T(8,128)(2,1)}, u32[]{:S(2)}) copy-start(bf16[64,512]{1,0:T(8,128)(2,1)} %param.13) | copy-start | bytes 196612
  3.2 64.2 %all-to-all-start = ((bf16[8,32,1024]{2,1,0:T(8,128)(2,1)}), bf16[8,32,1024]{2,1,0:T(8,128)(2,1)S(1)}, u32[]{:S(2)}, u32[]{:S(2)}) async-start(bf16[8,32,1024]{2,1,0:T(8,128)(2,1)} %copy.17), calls=%async_computation | async-start | bytes 1048576 | tf_op jit(solution)/shard_map/all_to_all | solution.py:37
  22.6 29.2 %collective-permute-start = (bf16[256,512]{1,0:T(8,128)(2,1)S(1)}, bf16[256,512]{1,0:T(8,128)(2,1)S(1)}, u32[]{:S(2)}, u32[]{:S(2)}) collective-permute-start(bf16[256,512]{1,0:T(8,128)(2,1)S(1)} %copy-done.1), channel_id=1, source_target_pairs={{0,2},{2,0},{4,6},{6,4},{8,10},{10,8},{12,14},{14,12},{16,18},{18,... | collective-permute-start | bytes 786440 | tf_op jit(solution)/shard_map/ppermute | solution.py:31
  25.8 4.0 %collective-permute-start.2 = (bf16[8,2,2,512]{3,2,1,0:T(2,128)(2,1)S(1)}, bf16[8,2,2,512]{3,2,1,0:T(2,128)(2,1)S(1)}, u32[]{:S(2)}, u32[]{:S(2)}) collective-permute-start(bf16[8,2,2,512]{3,2,1,0:T(2,128)(2,1)S(1)} %get-tuple-element.23), channel_id=1, source_target_pairs={{0,1},{1,0},{2,3},{3,2},{4,5},{5,4},{6,7},{7,6},{8,9},{9,8},{10,11... | collective-permute-start | bytes 98312 | tf_op jit(solution)/shard_map/ppermute | solution.py:34
  51.8 6.0 %copy-start.2 = (bf16[32,4096]{1,0:T(8,128)(2,1)S(1)}, bf16[32,4096]{1,0:T(8,128)(2,1)}, u32[]{:S(2)}) copy-start(bf16[32,4096]{1,0:T(8,128)(2,1)} %param.7) | copy-start | bytes 786436
  51.9 15.3 %collective-permute-start.1 = (bf16[2,256,512]{2,1,0:T(8,128)(2,1)S(1)}, bf16[2,256,512]{2,1,0:T(8,128)(2,1)S(1)}, u32[]{:S(2)}, u32[]{:S(2)}) collective-permute-start(bf16[2,256,512]{2,1,0:T(8,128)(2,1)S(1)} %maximum_select_fusion.2), channel_id=1, source_target_pairs={{0,1},{1,0},{2,3},{3,2},{4,5},{5,4},{6,7},{7,6},{8,9},{9,8},{10,11... | collective-permute-start | bytes 1572872 | tf_op jit(solution)/shard_map/ppermute | solution.py:34
  55.7 11.2 %collective-permute-start.3 = (bf16[2,8,2,512]{3,2,0,1:T(2,128)(2,1)S(1)}, bf16[2,8,2,512]{3,2,0,1:T(2,128)(2,1)S(1)}, u32[]{:S(2)}, u32[]{:S(2)}) collective-permute-start(bf16[2,8,2,512]{3,2,0,1:T(2,128)(2,1)S(1)} %bitcast.77), channel_id=1, source_target_pairs={{0,2},{2,0},{4,6},{6,4},{8,10},{10,8},{12,14},{14,12},{16,18},{18,... | collective-permute-start | bytes 98312 | tf_op jit(solution)/shard_map/ppermute | solution.py:31
  68.5 31.6 %all-to-all-start.1 = ((bf16[8,40,512]{2,1,0:T(8,128)(2,1)}), bf16[8,40,512]{2,1,0:T(8,128)(2,1)S(1)}, u32[]{:S(2)}, u32[]{:S(2)}) async-start(bf16[8,40,512]{2,1,0:T(8,128)(2,1)} %pad_maximum_fusion), calls=%async_computation.1 | async-start | bytes 655360 | tf_op jit(solution)/shard_map/all_to_all | solution.py:37
  80.2 0.7 copy-start.4
  81.9 14.5 %copy-start.5 = (s32[32]{0:T(128)S(1)}, s32[32]{0:T(128)}, u32[]{:S(2)}) copy-start(s32[32]{0:T(128)} %param.9) | copy-start | bytes 388
  101.4 25.7 %all-to-all-start.2 = ((bf16[8,40,512]{2,1,0:T(8,128)(2,1)}), bf16[8,40,512]{2,1,0:T(8,128)(2,1)S(1)}, u32[]{:S(2)}, u32[]{:S(2)}) async-start(bf16[8,40,512]{2,1,0:T(8,128)(2,1)} %pad_maximum_fusion.1), calls=%async_computation.2 | async-start | bytes 655360 | tf_op jit(solution)/shard_map/all_to_all | solution.py:37
  109.5 38.5 %collective-permute-start.6 = (bf16[256,512]{1,0:T(8,128)(2,1)S(1)}, bf16[256,512]{1,0:T(8,128)(2,1)S(1)}, u32[]{:S(2)}, u32[]{:S(2)}) collective-permute-start(bf16[256,512]{1,0:T(8,128)(2,1)S(1)} %bitcast.75), channel_id=1, source_target_pairs={{0,2},{2,0},{4,6},{6,4},{8,10},{10,8},{12,14},{14,12},{16,18},{18,... | collective-permute-start | bytes 786440 | tf_op jit(solution)/shard_map/ppermute | solution.py:31
  127.2 20.8 %collective-permute-start.7 = (bf16[256,512]{1,0:T(8,128)(2,1)S(1)}, bf16[256,512]{1,0:T(8,128)(2,1)S(1)}, u32[]{:S(2)}, u32[]{:S(2)}) collective-permute-start(bf16[256,512]{1,0:T(8,128)(2,1)S(1)} %bitcast.64), channel_id=1, source_target_pairs={{0,2},{2,0},{4,6},{6,4},{8,10},{10,8},{12,14},{14,12},{16,18},{18,... | collective-permute-start | bytes 786440 | tf_op jit(solution)/shard_map/ppermute | solution.py:31
  129.2 6.0 %collective-permute-start.4 = (bf16[8,2,2,512]{3,2,1,0:T(2,128)(2,1)S(1)}, bf16[8,2,2,512]{3,2,1,0:T(2,128)(2,1)S(1)}, u32[]{:S(2)}, u32[]{:S(2)}) collective-permute-start(bf16[8,2,2,512]{3,2,1,0:T(2,128)(2,1)S(1)} %get-tuple-element.19), channel_id=1, source_target_pairs={{0,2},{2,0},{4,6},{6,4},{8,10},{10,8},{12,14},{14,12},{16,18},{18,... | collective-permute-start | bytes 98312 | tf_op jit(solution)/shard_map/ppermute | solution.py:31
  135.4 15.0 %collective-permute-start.5 = (bf16[8,2,2,512]{3,2,1,0:T(2,128)(2,1)S(1)}, bf16[8,2,2,512]{3,2,1,0:T(2,128)(2,1)S(1)}, u32[]{:S(2)}, u32[]{:S(2)}) collective-permute-start(bf16[8,2,2,512]{3,2,1,0:T(2,128)(2,1)S(1)} %get-tuple-element.17), channel_id=1, source_target_pairs={{0,1},{1,0},{2,3},{3,2},{4,5},{5,4},{6,7},{7,6},{8,9},{9,8},{10,11... | collective-permute-start | bytes 98312 | tf_op jit(solution)/shard_map/ppermute | solution.py:34
  148.3 3.4 %collective-permute-start.8 = (bf16[256,512]{1,0:T(8,128)(2,1)S(1)}, bf16[256,512]{1,0:T(8,128)(2,1)S(1)}, u32[]{:S(2)}, u32[]{:S(2)}) collective-permute-start(bf16[256,512]{1,0:T(8,128)(2,1)S(1)} %fusion), channel_id=1, source_target_pairs={{0,1},{1,0},{2,3},{3,2},{4,5},{5,4},{6,7},{7,6},{8,9},{9,8},{10,11... | collective-permute-start | bytes 786440 | tf_op jit(solution)/shard_map/ppermute | solution.py:34

commit v6 on v5

--- a/solution.py
+++ b/solution.py
@@ -36,10 +36,12 @@
     def exchange(x):
         return lax.all_to_all(x, "z", 0, 0, tiled=True, axis_index_groups=stride2)
 
-    w_pair = both(b, weight, pair(weight), 0)
+    sent = rows.reshape(local, nj, quad).transpose(1, 0, 2)
+    sent, w_flip = lax.optimization_barrier((sent, pair(weight)))
+    w_pair = both(b, weight, w_flip, 0)
     w_quad = both(c, w_pair, core(w_pair), 1).reshape(quad, cols)
 
-    came = exchange(rows.reshape(local, nj, quad).transpose(1, 0, 2))
+    came = exchange(sent)
 
     projected = lax.dot_general(
         proj_grads, inv_factor, (((1,), (1,)), ((), ())), preferred_element_type=F32
@@ -63,12 +65,12 @@
 
     partial = jnp.dot(x_class, w_quad, preferred_element_type=F32).astype(BF)
     sent = jnp.concatenate([partial.reshape(nj, local, cols), slots], 1)
-    sent, score = lax.optimization_barrier((sent, score))
+    x_blocks = x_class.reshape(nj * local, 2, 2 * piece)
+    sent, score, x_sent = lax.optimization_barrier((sent, score, at(x_blocks, 1 - b, 1)))
+    x_same, x_flip = at(x_blocks, b, 1), pair(x_sent)
     came = exchange(sent)
     scores = lax.psum(score, "y")
     importance = (counts.astype(F32) * proj_grads.shape[1] / scores).astype(BF)
-    x_blocks = x_class.reshape(nj * local, 2, 2 * piece)
-    importance, x_sent = lax.optimization_barrier((importance, at(x_blocks, 1 - b, 1)))
     hidden = jnp.sum(came[:, :local].astype(F32), axis=0)
     cot = jnp.dot(placer, came[:, local:].reshape(2 * groups, cols), preferred_element_type=F32)
     squash = jax.nn.sigmoid(hidden)
@@ -78,27 +80,27 @@
     act = lax.dot_general(placer, act, (((0,), (0,)), ((), ())), preferred_element_type=F32)
     act = act.astype(BF).reshape(nj, 8, cols)
 
-    came = exchange(jnp.concatenate([grad, act], 1))
+    sent, x_flip = lax.optimization_barrier((jnp.concatenate([grad, act], 1), x_flip))
+    came = exchange(sent)
     grad = came[:, :local].reshape(nj * local, cols)
     grad_flip = pair(grad)
-    x_same, x_flip = at(x_blocks, b, 1), pair(x_sent)
 
-    def product(which):
-        out = 0.0
-        for x_part, g_part in ((x_same, grad), (x_flip, grad_flip)):
-            out = out + lax.dot_general(
-                lax.dynamic_slice_in_dim(x_part, which * piece, piece, 1),
-                g_part,
-                (((0,), (0,)), ((), ())),
-                preferred_element_type=F32,
-            )
-        return out
-
-    weight_grad = core(product(1 - c).astype(BF)).astype(F32) + product(c)
+    def product(which, x_part, g_part):
+        return lax.dot_general(
+            lax.dynamic_slice_in_dim(x_part, which * piece, piece, 1),
+            g_part,
+            (((0,), (0,)), ((), ())),
+            preferred_element_type=F32,
+        )
 
     act = came[:, local:].reshape(nj, 2, 2, 2, cols)
-    act = both(b, at(act, b, 1), pair(at(act, 1 - b, 1)), 1)
-    act = both(c, at(act, c, 2), core(at(act, 1 - c, 2)), 2)
+    half, act_sent = lax.optimization_barrier((product(1 - c, x_same, grad), at(act, 1 - b, 1)))
+    act = both(b, at(act, b, 1), pair(act_sent), 1)
+    half = (half + product(1 - c, x_flip, grad_flip)).astype(BF)
+    half, act_sent = lax.optimization_barrier((half, at(act, 1 - c, 2)))
+    weight_grad = product(c, x_same, grad) + product(c, x_flip, grad_flip)
+    weight_grad = core(half).astype(F32) + weight_grad
+    act = both(c, at(act, c, 2), core(act_sent), 2)
     return act.reshape(2 * groups, cols), weight_grad
 
 

time: 153 us -> 145 us (0.948)
  waiting for transfers between devices: 43.6 us -> 22.7 us
  starting transfers between devices: 73.2 us -> 82.1 us
    ppermute x5, waiting for transfers between devices: 24.3 us -> 4.83 us  [pair(): return lax.ppermute(x, 'z', flip)]
    ppermute x5, starting transfers between devices: 12.7 us -> 19.7 us  [pair(): return lax.ppermute(x, 'z', flip)]
    all_to_all x3, starting transfers between devices: 39.2 us -> 42.2 us  [exchange(): return lax.all_to_all(x, 'z', 0, 0, tiled=True, axis_index_groups=stride2)]
    all_to_all x3, waiting for transfers between devices: 18 us -> 16.2 us  [exchange(): return lax.all_to_all(x, 'z', 0, 0, tiled=True, axis_index_groups=stride2)]
    unnamed x14 -> x18, local copies, waits for them, and re-layouts: 2.14 us -> 3.54 us
  transfers between devices with their start and end apart: 12 -> 12, of which waited for: 6 -> 5; matrix products, arithmetic and copies ran while one was open for 3% -> 5% of each run, Pallas kernels for 0% -> 0%
where the time goes in v6:
time: 145 us; the launch traced here: 144 us
  starting transfers between devices  82.1 us (57%)
  blocking collectives  23.9 us (16%)
  waiting for transfers between devices  22.7 us (16%)
  local copies, waits for them, and re-layouts  7.71 us (5%)
  other arithmetic  3.45 us (2%)
  matrix products  3.4 us (2%)
    all_to_all x3, starting transfers between devices, exchange(): return lax.all_to_all(x, 'z', 0, 0, tiled=True, axis_index_groups=stride2)  42.2 us
    ppermute x4, starting transfers between devices, core(): return lax.ppermute(x, 'c', SWAP)  20.2 us
    ppermute x5, starting transfers between devices, pair(): return lax.ppermute(x, 'z', flip)  19.7 us
    all_to_all x3, waiting for transfers between devices, exchange(): return lax.all_to_all(x, 'z', 0, 0, tiled=True, axis_index_groups=stride2)  16.2 us
    psum x1, blocking collectives, shards(): scores = lax.psum(score, 'y')  14.9 us
    psum x1, blocking collectives, shards(): score = lax.psum(jnp.sum(projected * projected, axis=1), 'x')  9.06 us
    ppermute x5, waiting for transfers between devices, pair(): return lax.ppermute(x, 'z', flip)  4.83 us
    unnamed x18, local copies, waits for them, and re-layouts  3.54 us
  transfers between devices with their start and end apart: 12, of which 5 were waited for; matrix products, arithmetic and copies ran while one was open for 5% of the time, Pallas kernels for 0%

profile of v6, /device:TPU:1, one launch (start us, length us, event | category | flops | bytes accessed | tf_op | source)
XLA Modules:
  0.0 144.4 jit_solution(1110290823497971781)
XLA Ops:
  0.6 5.0 %collective-permute-start = (bf16[256,512]{1,0:T(8,128)(2,1)}, bf16[256,512]{1,0:T(8,128)(2,1)S(1)}, u32[]{:S(2)}, u32[]{:S(2)}) collective-permute-start(bf16[256,512]{1,0:T(8,128)(2,1)} %param.12), channel_id=1, source_target_pairs={{0,2},{2,0},{4,6},{6,4},{8,10},{10,8},{12,14},{14,12},{16,18},{18,... | collective-permute-start | bytes 786440 | tf_op jit(solution)/shard_map/ppermute | solution.py:31
  5.6 1.3 copy.23
  7.0 2.6 %collective-permute-done = bf16[256,512]{1,0:T(8,128)(2,1)S(1)} collective-permute-done((bf16[256,512]{1,0:T(8,128)(2,1)}, bf16[256,512]{1,0:T(8,128)(2,1)S(1)}, u32[]{:S(2)}, u32[]{:S(2)}) %collective-permute-start) | collective-permute-done | bytes 262176 | tf_op jit(solution)/shard_map/ppermute | solution.py:31
  9.6 1.1 copy.17
  10.7 19.9 %all-to-all-start = ((bf16[8,32,1024]{2,1,0:T(8,128)(2,1)}), bf16[8,32,1024]{2,1,0:T(8,128)(2,1)S(1)}, u32[]{:S(2)}, u32[]{:S(2)}) async-start(bf16[8,32,1024]{2,1,0:T(8,128)(2,1)} %copy.17), calls=%async_computation | async-start | bytes 1048576 | tf_op jit(solution)/shard_map/all_to_all | solution.py:37
  30.6 0.1 dynamic-slice_bitcast_fusion.3
  30.7 3.7 %collective-permute-start.2 = (bf16[8,2,2,512]{3,2,1,0:T(2,128)(2,1)S(1)}, bf16[8,2,2,512]{3,2,1,0:T(2,128)(2,1)S(1)}, u32[]{:S(2)}, u32[]{:S(2)}) collective-permute-start(bf16[8,2,2,512]{3,2,1,0:T(2,128)(2,1)S(1)} %get-tuple-element.37), channel_id=1, source_target_pairs={{0,1},{1,0},{2,3},{3,2},{4,5},{5,4},{6,7},{7,6},{8,9},{9,8},{10,11... | collective-permute-start | bytes 98312 | tf_op jit(solution)/shard_map/ppermute | solution.py:34
  34.5 0.8 collective-permute-done.2
  35.3 0.1 broadcast_select_fusion
  35.4 0.1 maximum_select_fusion.2
  35.5 2.3 %collective-permute-start.1 = (bf16[2,256,512]{2,1,0:T(8,128)(2,1)S(1)}, bf16[2,256,512]{2,1,0:T(8,128)(2,1)S(1)}, u32[]{:S(2)}, u32[]{:S(2)}) collective-permute-start(bf16[2,256,512]{2,1,0:T(8,128)(2,1)S(1)} %maximum_select_fusion.2), channel_id=1, source_target_pairs={{0,1},{1,0},{2,3},{3,2},{4,5},{5,4},{6,7},{7,6},{8,9},{9,8},{10,11... | collective-permute-start | bytes 1572872 | tf_op jit(solution)/shard_map/ppermute | solution.py:34
  37.9 3.1 %collective-permute-start.3 = (bf16[2,8,2,512]{3,2,0,1:T(2,128)(2,1)S(1)}, bf16[2,8,2,512]{3,2,0,1:T(2,128)(2,1)S(1)}, u32[]{:S(2)}, u32[]{:S(2)}) collective-permute-start(bf16[2,8,2,512]{3,2,0,1:T(2,128)(2,1)S(1)} %bitcast.77), channel_id=1, source_target_pairs={{0,2},{2,0},{4,6},{6,4},{8,10},{10,8},{12,14},{14,12},{16,18},{18,... | collective-permute-start | bytes 98312 | tf_op jit(solution)/shard_map/ppermute | solution.py:31
  41.0 0.6 fusion.6
  41.5 9.1 %psum.14 = f32[32]{0:T(128)S(1)} all-reduce(f32[32]{0:T(128)S(1)} %fusion.6), channel_id=1, replica_groups=mesh['x'=4,'y'=8,'z'=16,'c'=2] {'x'}, use_global_device_ids=true, to_apply=%region_1.2 | all-reduce | flops 32 | bytes 256 | tf_op jit(solution)/shard_map/psum | solution.py:49
  50.6 0.1 fusion.17
  50.8 0.1 maximum_select_fusion.1
  50.9 0.8 copy-done.2
  51.7 1.4 maximum_select_fusion
  53.1 0.4 reshape_reshape.3
  53.4 0.5 constant_dynamic-slice_fusion.4
  54.0 0.7 copy.35
  54.7 0.4 convolution_convert_fusion
  55.2 0.7 pad_maximum_fusion
  55.9 11.6 %all-to-all-start.1 = ((bf16[8,40,512]{2,1,0:T(8,128)(2,1)}), bf16[8,40,512]{2,1,0:T(8,128)(2,1)S(1)}, u32[]{:S(2)}, u32[]{:S(2)}) async-start(bf16[8,40,512]{2,1,0:T(8,128)(2,1)} %pad_maximum_fusion), calls=%async_computation.1 | async-start | bytes 655360 | tf_op jit(solution)/shard_map/all_to_all | solution.py:37
  67.5 0.7 copy-done.6
  68.2 0.1 fusion.5
  68.3 6.4 %collective-permute-start.4 = (bf16[256,512]{1,0:T(8,128)(2,1)S(1)}, bf16[256,512]{1,0:T(8,128)(2,1)S(1)}, u32[]{:S(2)}, u32[]{:S(2)}) collective-permute-start(bf16[256,512]{1,0:T(8,128)(2,1)S(1)} %bitcast.75), channel_id=1, source_target_pairs={{0,2},{2,0},{4,6},{6,4},{8,10},{10,8},{12,14},{14,12},{16,18},{18,... | collective-permute-start | bytes 786440 | tf_op jit(solution)/shard_map/ppermute | solution.py:31
  74.7 14.9 %psum.15 = f32[32]{0:T(128)S(1)} all-reduce(f32[32]{0:T(128)S(1)} %psum.14), channel_id=1, replica_groups=mesh['x'=4,'y'=8,'z'=16,'c'=2] {'y'}, use_global_device_ids=true, to_apply=%region_2.3 | all-reduce | flops 32 | bytes 256 | tf_op jit(solution)/shard_map/psum | solution.py:72
  89.7 0.2 fusion.4
  89.9 0.3 fusion.1
  90.2 0.7 pad_maximum_fusion.1
  90.9 10.7 %all-to-all-start.2 = ((bf16[8,40,512]{2,1,0:T(8,128)(2,1)}), bf16[8,40,512]{2,1,0:T(8,128)(2,1)S(1)}, u32[]{:S(2)}, u32[]{:S(2)}) async-start(bf16[8,40,512]{2,1,0:T(8,128)(2,1)} %pad_maximum_fusion.1), calls=%async_computation.2 | async-start | bytes 655360 | tf_op jit(solution)/shard_map/all_to_all | solution.py:37
  101.6 1.1 constant_dynamic-slice_fusion
  102.7 16.2 %all-to-all-done.2 = bf16[8,40,512]{2,1,0:T(8,128)(2,1)S(1)} async-done(((bf16[8,40,512]{2,1,0:T(8,128)(2,1)}), bf16[8,40,512]{2,1,0:T(8,128)(2,1)S(1)}, u32[]{:S(2)}, u32[]{:S(2)}) %all-to-all-start.2) | async-done | bytes 327712 | tf_op jit(solution)/shard_map/all_to_all | solution.py:37
  118.9 2.1 %collective-permute-start.6 = (bf16[256,512]{1,0:T(8,128)(2,1)S(1)}, bf16[256,512]{1,0:T(8,128)(2,1)S(1)}, u32[]{:S(2)}, u32[]{:S(2)}) collective-permute-start(bf16[256,512]{1,0:T(8,128)(2,1)S(1)} %bitcast.64), channel_id=1, source_target_pairs={{0,2},{2,0},{4,6},{6,4},{8,10},{10,8},{12,14},{14,12},{16,18},{18,... | collective-permute-start | bytes 786440 | tf_op jit(solution)/shard_map/ppermute | solution.py:31
  121.0 0.2 fusion.10
  121.3 0.1 constant_dynamic-slice_fusion.3
  121.4 3.2 %collective-permute-start.5 = (bf16[8,2,2,512]{3,2,1,0:T(2,128)(2,1)S(1)}, bf16[8,2,2,512]{3,2,1,0:T(2,128)(2,1)S(1)}, u32[]{:S(2)}, u32[]{:S(2)}) collective-permute-start(bf16[8,2,2,512]{3,2,1,0:T(2,128)(2,1)S(1)} %get-tuple-element.23), channel_id=1, source_target_pairs={{0,2},{2,0},{4,6},{6,4},{8,10},{10,8},{12,14},{14,12},{16,18},{18,... | collective-permute-start | bytes 98312 | tf_op jit(solution)/shard_map/ppermute | solution.py:31
  124.6 2.2 %collective-permute-done.5 = bf16[8,2,2,512]{3,2,1,0:T(2,128)(2,1)S(1)} collective-permute-done((bf16[8,2,2,512]{3,2,1,0:T(2,128)(2,1)S(1)}, bf16[8,2,2,512]{3,2,1,0:T(2,128)(2,1)S(1)}, u32[]{:S(2)}, u32[]{:S(2)}) %collective-permute-start.5) | collective-permute-done | bytes 32800 | tf_op jit(solution)/shard_map/ppermute | solution.py:31
  126.8 0.1 broadcast_select_fusion.2
  127.0 0.3 fusion
  127.2 12.3 %collective-permute-start.8 = (bf16[256,512]{1,0:T(8,128)(2,1)S(1)}, bf16[256,512]{1,0:T(8,128)(2,1)S(1)}, u32[]{:S(2)}, u32[]{:S(2)}) collective-permute-start(bf16[256,512]{1,0:T(8,128)(2,1)S(1)} %fusion), channel_id=1, source_target_pairs={{0,1},{1,0},{2,3},{3,2},{4,5},{5,4},{6,7},{7,6},{8,9},{9,8},{10,11... | collective-permute-start | bytes 786440 | tf_op jit(solution)/shard_map/ppermute | solution.py:34
  139.5 1.9 %collective-permute-start.7 = (bf16[8,2,2,512]{3,2,1,0:T(2,128)(2,1)S(1)}, bf16[8,2,2,512]{3,2,1,0:T(2,128)(2,1)S(1)}, u32[]{:S(2)}, u32[]{:S(2)}) collective-permute-start(bf16[8,2,2,512]{3,2,1,0:T(2,128)(2,1)S(1)} %get-tuple-element.26), channel_id=1, source_target_pairs={{0,1},{1,0},{2,3},{3,2},{4,5},{5,4},{6,7},{7,6},{8,9},{9,8},{10,11... | collective-permute-start | bytes 98312 | tf_op jit(solution)/shard_map/ppermute | solution.py:34
  141.4 0.2 fusion.7
  141.7 0.9 collective-permute-done.7
  142.6 0.1 broadcast_select_fusion.3
  142.7 0.7 select_n.137
  143.4 1.1 convert_add_fusion
  (34 shorter events, 0.4 us)
Async XLA Ops:
  0.6 40.3 %copy-start = (bf16[128,4096]{1,0:T(8,128)(2,1)S(1)}, bf16[128,4096]{1,0:T(8,128)(2,1)}, u32[]{:S(2)}) copy-start(bf16[128,4096]{1,0:T(8,128)(2,1)} %param.8) | copy-start | bytes 3145732
  0.6 8.9 %collective-permute-start = (bf16[256,512]{1,0:T(8,128)(2,1)}, bf16[256,512]{1,0:T(8,128)(2,1)S(1)}, u32[]{:S(2)}, u32[]{:S(2)}) collective-permute-start(bf16[256,512]{1,0:T(8,128)(2,1)} %param.12), channel_id=1, source_target_pairs={{0,2},{2,0},{4,6},{6,4},{8,10},{10,8},{12,14},{14,12},{16,18},{18,... | collective-permute-start | bytes 786440 | tf_op jit(solution)/shard_map/ppermute | solution.py:31
  10.7 19.9 %copy-start.5 = (bf16[64,512]{1,0:T(8,128)(2,1)S(1)}, bf16[64,512]{1,0:T(8,128)(2,1)}, u32[]{:S(2)}) copy-start(bf16[64,512]{1,0:T(8,128)(2,1)} %param.13) | copy-start | bytes 196612
  10.7 42.4 %all-to-all-start = ((bf16[8,32,1024]{2,1,0:T(8,128)(2,1)}), bf16[8,32,1024]{2,1,0:T(8,128)(2,1)S(1)}, u32[]{:S(2)}, u32[]{:S(2)}) async-start(bf16[8,32,1024]{2,1,0:T(8,128)(2,1)} %copy.17), calls=%async_computation | async-start | bytes 1048576 | tf_op jit(solution)/shard_map/all_to_all | solution.py:37
  30.6 4.8 %copy-start.1 = (bf16[256,512]{1,0:T(8,128)(2,1)S(1)}, bf16[256,512]{1,0:T(8,128)(2,1)}, u32[]{:S(2)}) copy-start(bf16[256,512]{1,0:T(8,128)(2,1)} %param.12) | copy-start | bytes 786436
  30.7 4.6 %collective-permute-start.2 = (bf16[8,2,2,512]{3,2,1,0:T(2,128)(2,1)S(1)}, bf16[8,2,2,512]{3,2,1,0:T(2,128)(2,1)S(1)}, u32[]{:S(2)}, u32[]{:S(2)}) collective-permute-start(bf16[8,2,2,512]{3,2,1,0:T(2,128)(2,1)S(1)} %get-tuple-element.37), channel_id=1, source_target_pairs={{0,1},{1,0},{2,3},{3,2},{4,5},{5,4},{6,7},{7,6},{8,9},{9,8},{10,11... | collective-permute-start | bytes 98312 | tf_op jit(solution)/shard_map/ppermute | solution.py:34
  35.4 5.6 %copy-start.3 = (bf16[32,4096]{1,0:T(8,128)(2,1)S(1)}, bf16[32,4096]{1,0:T(8,128)(2,1)}, u32[]{:S(2)}) copy-start(bf16[32,4096]{1,0:T(8,128)(2,1)} %param.7) | copy-start | bytes 786436
  35.5 15.4 %collective-permute-start.1 = (bf16[2,256,512]{2,1,0:T(8,128)(2,1)S(1)}, bf16[2,256,512]{2,1,0:T(8,128)(2,1)S(1)}, u32[]{:S(2)}, u32[]{:S(2)}) collective-permute-start(bf16[2,256,512]{2,1,0:T(8,128)(2,1)S(1)} %maximum_select_fusion.2), channel_id=1, source_target_pairs={{0,1},{1,0},{2,3},{3,2},{4,5},{5,4},{6,7},{7,6},{8,9},{9,8},{10,11... | collective-permute-start | bytes 1572872 | tf_op jit(solution)/shard_map/ppermute | solution.py:34
  37.9 12.8 %collective-permute-start.3 = (bf16[2,8,2,512]{3,2,0,1:T(2,128)(2,1)S(1)}, bf16[2,8,2,512]{3,2,0,1:T(2,128)(2,1)S(1)}, u32[]{:S(2)}, u32[]{:S(2)}) collective-permute-start(bf16[2,8,2,512]{3,2,0,1:T(2,128)(2,1)S(1)} %bitcast.77), channel_id=1, source_target_pairs={{0,2},{2,0},{4,6},{6,4},{8,10},{10,8},{12,14},{14,12},{16,18},{18,... | collective-permute-start | bytes 98312 | tf_op jit(solution)/shard_map/ppermute | solution.py:31
  50.9 0.8 copy-start.2
  55.9 12.4 %copy-start.4 = (bf16[256,1,512]{2,0,1:T(8,128)(2,1)S(1)}, bf16[256,1,512]{2,0,1:T(8,128)(2,1)}, u32[]{:S(2)}) copy-start(bf16[256,1,512]{2,0,1:T(8,128)(2,1)} %copy.35) | copy-start | bytes 786436
  55.9 33.7 %all-to-all-start.1 = ((bf16[8,40,512]{2,1,0:T(8,128)(2,1)}), bf16[8,40,512]{2,1,0:T(8,128)(2,1)S(1)}, u32[]{:S(2)}, u32[]{:S(2)}) async-start(bf16[8,40,512]{2,1,0:T(8,128)(2,1)} %pad_maximum_fusion), calls=%async_computation.1 | async-start | bytes 655360 | tf_op jit(solution)/shard_map/all_to_all | solution.py:37
  67.5 0.7 copy-start.6
  68.3 21.3 %copy-start.7 = (s32[32]{0:T(128)S(1)}, s32[32]{0:T(128)}, u32[]{:S(2)}) copy-start(s32[32]{0:T(128)} %param.9) | copy-start | bytes 388
  68.3 22.6 %collective-permute-start.4 = (bf16[256,512]{1,0:T(8,128)(2,1)S(1)}, bf16[256,512]{1,0:T(8,128)(2,1)S(1)}, u32[]{:S(2)}, u32[]{:S(2)}) collective-permute-start(bf16[256,512]{1,0:T(8,128)(2,1)S(1)} %bitcast.75), channel_id=1, source_target_pairs={{0,2},{2,0},{4,6},{6,4},{8,10},{10,8},{12,14},{14,12},{16,18},{18,... | collective-permute-start | bytes 786440 | tf_op jit(solution)/shard_map/ppermute | solution.py:31
  90.9 28.0 %all-to-all-start.2 = ((bf16[8,40,512]{2,1,0:T(8,128)(2,1)}), bf16[8,40,512]{2,1,0:T(8,128)(2,1)S(1)}, u32[]{:S(2)}, u32[]{:S(2)}) async-start(bf16[8,40,512]{2,1,0:T(8,128)(2,1)} %pad_maximum_fusion.1), calls=%async_computation.2 | async-start | bytes 655360 | tf_op jit(solution)/shard_map/all_to_all | solution.py:37
  118.9 8.0 %collective-permute-start.6 = (bf16[256,512]{1,0:T(8,128)(2,1)S(1)}, bf16[256,512]{1,0:T(8,128)(2,1)S(1)}, u32[]{:S(2)}, u32[]{:S(2)}) collective-permute-start(bf16[256,512]{1,0:T(8,128)(2,1)S(1)} %bitcast.64), channel_id=1, source_target_pairs={{0,2},{2,0},{4,6},{6,4},{8,10},{10,8},{12,14},{14,12},{16,18},{18,... | collective-permute-start | bytes 786440 | tf_op jit(solution)/shard_map/ppermute | solution.py:31
  121.4 5.4 %collective-permute-start.5 = (bf16[8,2,2,512]{3,2,1,0:T(2,128)(2,1)S(1)}, bf16[8,2,2,512]{3,2,1,0:T(2,128)(2,1)S(1)}, u32[]{:S(2)}, u32[]{:S(2)}) collective-permute-start(bf16[8,2,2,512]{3,2,1,0:T(2,128)(2,1)S(1)} %get-tuple-element.23), channel_id=1, source_target_pairs={{0,2},{2,0},{4,6},{6,4},{8,10},{10,8},{12,14},{14,12},{16,18},{18,... | collective-permute-start | bytes 98312 | tf_op jit(solution)/shard_map/ppermute | solution.py:31
  127.2 16.1 %collective-permute-start.8 = (bf16[256,512]{1,0:T(8,128)(2,1)S(1)}, bf16[256,512]{1,0:T(8,128)(2,1)S(1)}, u32[]{:S(2)}, u32[]{:S(2)}) collective-permute-start(bf16[256,512]{1,0:T(8,128)(2,1)S(1)} %fusion), channel_id=1, source_target_pairs={{0,1},{1,0},{2,3},{3,2},{4,5},{5,4},{6,7},{7,6},{8,9},{9,8},{10,11... | collective-permute-start | bytes 786440 | tf_op jit(solution)/shard_map/ppermute | solution.py:34
  139.5 3.1 %collective-permute-start.7 = (bf16[8,2,2,512]{3,2,1,0:T(2,128)(2,1)S(1)}, bf16[8,2,2,512]{3,2,1,0:T(2,128)(2,1)S(1)}, u32[]{:S(2)}, u32[]{:S(2)}) collective-permute-start(bf16[8,2,2,512]{3,2,1,0:T(2,128)(2,1)S(1)} %get-tuple-element.26), channel_id=1, source_target_pairs={{0,1},{1,0},{2,3},{3,2},{4,5},{5,4},{6,7},{7,6},{8,9},{9,8},{10,11... | collective-permute-start | bytes 98312 | tf_op jit(solution)/shard_map/ppermute | solution.py:34

commit v7 on v6

--- a/solution.py
+++ b/solution.py
@@ -17,7 +17,7 @@
 
 
 def shards(proj_grads, inv_factor, counts, dests, rows, weight, cotangent):
-    nz = lax.axis_size("z")
+    nx, nz = lax.axis_size("x"), lax.axis_size("z")
     nj, groups = nz // 2, 2 * nz
     z, c = lax.axis_index("z"), lax.axis_index("c")
     b = z % 2
@@ -36,19 +36,27 @@
     def exchange(x):
         return lax.all_to_all(x, "z", 0, 0, tiled=True, axis_index_groups=stride2)
 
-    sent = rows.reshape(local, nj, quad).transpose(1, 0, 2)
-    sent, w_flip = lax.optimization_barrier((sent, pair(weight)))
-    w_pair = both(b, weight, w_flip, 0)
+    w_pair = both(b, weight, pair(weight), 0)
     w_quad = both(c, w_pair, core(w_pair), 1).reshape(quad, cols)
 
-    came = exchange(sent)
+    share = local // nx
+    sent = lax.dynamic_slice_in_dim(rows, lax.axis_index("x") * share, share, 0)
+    came = exchange(sent.reshape(share, nj, quad).transpose(1, 0, 2))
 
     projected = lax.dot_general(
         proj_grads, inv_factor, (((1,), (1,)), ((), ())), preferred_element_type=F32
     )
-    score = lax.psum(jnp.sum(projected * projected, axis=1), "x")
-    came, score = lax.optimization_barrier((came, score))
-    x_class = came.reshape(nj * local, quad)
+    score = jnp.sum(projected * projected, axis=1)
+    high = lax.reduce_precision(score, 8, 7)
+    middle = lax.reduce_precision(score - high, 8, 7)
+    low = score - high - middle
+    thirds = jnp.concatenate([high, middle, low, jnp.zeros(quad - 3 * local, F32)]).astype(BF)
+    thirds = jnp.broadcast_to(thirds[None, None, :], (1, share, quad))
+
+    came = lax.all_gather(jnp.concatenate([came, thirds], 0), "x", axis=1, tiled=True)
+    x_class = came[:nj].reshape(nj * local, quad)
+    thirds = came[nj].reshape(nx, share, quad)[:, 0, : 3 * local].astype(F32)
+    score = jnp.sum(thirds.reshape(nx * 3, local), axis=0)
 
     slots = cotangent.reshape(nj, 2, 2, 2, cols)
     slots = both(c, at(slots, c, 2), core(at(slots, 1 - c, 2)), 0)
@@ -65,9 +73,13 @@
 
     partial = jnp.dot(x_class, w_quad, preferred_element_type=F32).astype(BF)
     sent = jnp.concatenate([partial.reshape(nj, local, cols), slots], 1)
-    x_blocks = x_class.reshape(nj * local, 2, 2 * piece)
-    sent, score, x_sent = lax.optimization_barrier((sent, score, at(x_blocks, 1 - b, 1)))
-    x_same, x_flip = at(x_blocks, b, 1), pair(x_sent)
+    x_same, x_sent = (
+        lax.dynamic_slice_in_dim(x_class, 2 * bb * piece, 2 * piece, 1) for bb in (b, 1 - b)
+    )
+    _, score, x_same, x_sent = lax.optimization_barrier(
+        (partial[:8, :128], score, x_same, x_sent)
+    )
+    x_flip = pair(x_sent)
     came = exchange(sent)
     scores = lax.psum(score, "y")
     importance = (counts.astype(F32) * proj_grads.shape[1] / scores).astype(BF)

time: 145 us -> 135 us (0.931)
  starting transfers between devices: 82.1 us -> 75.2 us
  local copies, waits for them, and re-layouts: 7.71 us -> 3.52 us
    all_gather x0 -> x1, blocking collectives: none -> 10.4 us  [shards(): lax.all_gather(jnp.concatenate([came, thirds], 0), 'x', axis=1, tiled=True)]
    psum x1 -> x0, blocking collectives: 9.06 us -> none  [shards(): score = lax.psum(jnp.sum(projected * projected, axis=1), 'x')]
    ppermute x5, starting transfers between devices: 19.7 us -> 15.4 us  [pair(): return lax.ppermute(x, 'z', flip)]
    all_to_all x3, starting transfers between devices: 42.2 us -> 39.2 us  [exchange(): return lax.all_to_all(x, 'z', 0, 0, tiled=True, axis_index_groups=stride2)]
    unnamed x18 -> x12, local copies, waits for them, and re-layouts: 3.54 us -> 0.68 us
    all_to_all x3, waiting for transfers between devices: 16.2 us -> 18.9 us  [exchange(): return lax.all_to_all(x, 'z', 0, 0, tiled=True, axis_index_groups=stride2)]
    ppermute x5, waiting for transfers between devices: 4.83 us -> 2.97 us  [pair(): return lax.ppermute(x, 'z', flip)]
  transfers between devices with their start and end apart: 12 -> 12, of which waited for: 5 -> 6; matrix products, arithmetic and copies ran while one was open for 5% -> 5% of each run, Pallas kernels for 0% -> 0%
where the time goes in v7:
time: 135 us; the launch traced here: 134 us
  starting transfers between devices  75.2 us (56%)
  blocking collectives  24.8 us (18%)
  waiting for transfers between devices  23 us (17%)
  local copies, waits for them, and re-layouts  3.52 us (3%)
  matrix products  3.43 us (3%)
  other arithmetic  3.19 us (2%)
    all_to_all x3, starting transfers between devices, exchange(): return lax.all_to_all(x, 'z', 0, 0, tiled=True, axis_index_groups=stride2)  39.2 us
    ppermute x4, starting transfers between devices, core(): return lax.ppermute(x, 'c', SWAP)  20.6 us
    all_to_all x3, waiting for transfers between devices, exchange(): return lax.all_to_all(x, 'z', 0, 0, tiled=True, axis_index_groups=stride2)  18.9 us
    ppermute x5, starting transfers between devices, pair(): return lax.ppermute(x, 'z', flip)  15.4 us
    psum x1, blocking collectives, shards(): scores = lax.psum(score, 'y')  14.4 us
    all_gather x1, blocking collectives, shards(): lax.all_gather(jnp.concatenate([came, thirds], 0), 'x', axis=1, tiled=True)  10.4 us
    ppermute x5, waiting for transfers between devices, pair(): return lax.ppermute(x, 'z', flip)  2.97 us
  transfers between devices with their start and end apart: 12, of which 6 were waited for; matrix products, arithmetic and copies ran while one was open for 5% of the time, Pallas kernels for 0%

profile of v7, /device:TPU:1, one launch (start us, length us, event | category | flops | bytes accessed | tf_op | source)
XLA Modules:
  0.0 134.2 jit_solution(11273209989503659356)
XLA Ops:
  0.6 0.0 copy-start
  0.6 5.0 %collective-permute-start = (bf16[256,512]{1,0:T(8,128)(2,1)}, bf16[256,512]{1,0:T(8,128)(2,1)S(1)}, u32[]{:S(2)}, u32[]{:S(2)}) collective-permute-start(bf16[256,512]{1,0:T(8,128)(2,1)} %param.12), channel_id=1, source_target_pairs={{0,2},{2,0},{4,6},{6,4},{8,10},{10,8},{12,14},{14,12},{16,18},{18,... | collective-permute-start | bytes 786440 | tf_op jit(solution)/shard_map/ppermute | solution.py:31
  5.6 1.6 %constant_dynamic-slice_fusion.6 = bf16[8,8192]{1,0:T(8,128)(2,1)} fusion(bf16[32,8192]{1,0:T(8,128)(2,1)} %param.11, s32[]{:T(128)S(6)} %select_n.117), kind=kLoop, calls=%fused_computation.60 | loop fusion | bytes 262148 | tf_op jit(solution)/shard_map/dynamic_slice | solution.py:43
  7.2 17.7 %all-to-all-start = ((bf16[8,8,1024]{2,1,0:T(8,128)(2,1)}), bf16[8,8,1024]{2,1,0:T(8,128)(2,1)S(1)}, u32[]{:S(2)}, u32[]{:S(2)}) async-start(bf16[8,8,1024]{2,1,0:T(8,128)(2,1)} %bitcast.1), calls=%async_computation | async-start | bytes 262144 | tf_op jit(solution)/shard_map/all_to_all | solution.py:37
  25.0 0.1 dynamic-slice_bitcast_fusion.3
  25.0 3.1 %collective-permute-start.2 = (bf16[8,2,2,512]{3,2,1,0:T(2,128)(2,1)S(1)}, bf16[8,2,2,512]{3,2,1,0:T(2,128)(2,1)S(1)}, u32[]{:S(2)}, u32[]{:S(2)}) collective-permute-start(bf16[8,2,2,512]{3,2,1,0:T(2,128)(2,1)S(1)} %get-tuple-element.29), channel_id=1, source_target_pairs={{0,1},{1,0},{2,3},{3,2},{4,5},{5,4},{6,7},{7,6},{8,9},{9,8},{10,11... | collective-permute-start | bytes 98312 | tf_op jit(solution)/shard_map/ppermute | solution.py:34
  28.2 0.6 fusion.6
  28.8 0.1 pad_maximum_fusion.3
  28.9 0.1 collective-permute-done.2
  29.0 0.1 broadcast_select_fusion
  29.1 0.1 constant_dynamic-slice_fusion.3
  29.2 2.2 %collective-permute-start.3 = (bf16[2,8,2,512]{3,2,0,1:T(2,128)(2,1)S(1)}, bf16[2,8,2,512]{3,2,0,1:T(2,128)(2,1)S(1)}, u32[]{:S(2)}, u32[]{:S(2)}) collective-permute-start(bf16[2,8,2,512]{3,2,0,1:T(2,128)(2,1)S(1)} %bitcast.67), channel_id=1, source_target_pairs={{0,2},{2,0},{4,6},{6,4},{8,10},{10,8},{12,14},{14,12},{16,18},{18,... | collective-permute-start | bytes 98312 | tf_op jit(solution)/shard_map/ppermute | solution.py:31
  31.5 0.9 maximum_select_fusion.2
  32.3 2.5 %collective-permute-start.1 = (bf16[2,256,512]{2,1,0:T(8,128)(2,1)}, bf16[2,256,512]{2,1,0:T(8,128)(2,1)S(1)}, u32[]{:S(2)}, u32[]{:S(2)}) collective-permute-start(bf16[2,256,512]{2,1,0:T(8,128)(2,1)} %maximum_select_fusion.2), channel_id=1, source_target_pairs={{0,1},{1,0},{2,3},{3,2},{4,5},{5,4},{6,7},{7,6},{8,9},{9,8},{10,11... | collective-permute-start | bytes 1572872 | tf_op jit(solution)/shard_map/ppermute | solution.py:34
  34.9 0.1 fusion.15
  35.0 0.1 maximum_select_fusion.1
  35.1 2.9 %all-to-all-done = bf16[8,8,1024]{2,1,0:T(8,128)(2,1)S(1)} async-done(((bf16[8,8,1024]{2,1,0:T(8,128)(2,1)}), bf16[8,8,1024]{2,1,0:T(8,128)(2,1)S(1)}, u32[]{:S(2)}, u32[]{:S(2)}) %all-to-all-start) | async-done | bytes 131104 | tf_op jit(solution)/shard_map/all_to_all | solution.py:37
  38.0 10.4 %all_gather.3 = bf16[9,32,1024]{2,1,0:T(8,128)(2,1)S(1)} all-gather(bf16[9,8,1024]{2,1,0:T(8,128)(2,1)S(1)} %pad_maximum_fusion.2), channel_id=1, replica_groups=mesh['x'=4,'y'=8,'z'=16,'c'=2] {'x'}, dimensions={1}, use_global_device_ids=true | all-gather | bytes 737280 | tf_op jit(solution)/shard_map/all_gather | solution.py:56
  48.4 0.1 maximum_select_fusion
  48.6 0.4 convolution_convert_fusion
  49.0 0.7 pad_maximum_fusion
  49.8 10.0 %all-to-all-start.1 = ((bf16[8,40,512]{2,1,0:T(8,128)(2,1)}), bf16[8,40,512]{2,1,0:T(8,128)(2,1)S(1)}, u32[]{:S(2)}, u32[]{:S(2)}) async-start(bf16[8,40,512]{2,1,0:T(8,128)(2,1)} %pad_maximum_fusion), calls=%async_computation.1 | async-start | bytes 655360 | tf_op jit(solution)/shard_map/all_to_all | solution.py:37
  59.8 0.7 copy-done.4
  60.4 0.1 fusion.5
  60.6 0.1 reshape.152
  60.8 3.0 %collective-permute-start.4 = (bf16[256,512]{1,0:T(8,128)(2,1)S(1)}, bf16[256,512]{1,0:T(8,128)(2,1)S(1)}, u32[]{:S(2)}, u32[]{:S(2)}) collective-permute-start(bf16[256,512]{1,0:T(8,128)(2,1)S(1)} %get-tuple-element.12), channel_id=1, source_target_pairs={{0,2},{2,0},{4,6},{6,4},{8,10},{10,8},{12,14},{14,12},{16,18},{18,... | collective-permute-start | bytes 786440 | tf_op jit(solution)/shard_map/ppermute | solution.py:31
  63.8 14.4 %psum.7 = f32[32]{0:T(128)S(1)} all-reduce(f32[32]{0:T(128)S(1)} %reduce_sum.39), channel_id=1, replica_groups=mesh['x'=4,'y'=8,'z'=16,'c'=2] {'y'}, use_global_device_ids=true, to_apply=%region_2.3 | all-reduce | flops 32 | bytes 256 | tf_op jit(solution)/shard_map/psum | solution.py:84
  78.3 0.2 fusion.4
  78.5 0.3 fusion.1
  78.8 0.8 pad_maximum_fusion.1
  79.5 0.2 collective-permute-done.4
  79.8 11.5 %all-to-all-start.2 = ((bf16[8,40,512]{2,1,0:T(8,128)(2,1)}), bf16[8,40,512]{2,1,0:T(8,128)(2,1)S(1)}, u32[]{:S(2)}, u32[]{:S(2)}) async-start(bf16[8,40,512]{2,1,0:T(8,128)(2,1)} %pad_maximum_fusion.1), calls=%async_computation.2 | async-start | bytes 655360 | tf_op jit(solution)/shard_map/all_to_all | solution.py:37
  91.3 16.1 %all-to-all-done.2 = bf16[8,40,512]{2,1,0:T(8,128)(2,1)S(1)} async-done(((bf16[8,40,512]{2,1,0:T(8,128)(2,1)}), bf16[8,40,512]{2,1,0:T(8,128)(2,1)S(1)}, u32[]{:S(2)}, u32[]{:S(2)}) %all-to-all-start.2) | async-done | bytes 327712 | tf_op jit(solution)/shard_map/all_to_all | solution.py:37
  107.4 3.1 %collective-permute-start.6 = (bf16[256,512]{1,0:T(8,128)(2,1)S(1)}, bf16[256,512]{1,0:T(8,128)(2,1)S(1)}, u32[]{:S(2)}, u32[]{:S(2)}) collective-permute-start(bf16[256,512]{1,0:T(8,128)(2,1)S(1)} %bitcast.57), channel_id=1, source_target_pairs={{0,2},{2,0},{4,6},{6,4},{8,10},{10,8},{12,14},{14,12},{16,18},{18,... | collective-permute-start | bytes 786440 | tf_op jit(solution)/shard_map/ppermute | solution.py:31
  110.5 0.2 fusion.13
  110.8 0.1 constant_dynamic-slice_fusion.1
  110.8 2.2 %collective-permute-start.5 = (bf16[8,2,2,512]{3,2,1,0:T(2,128)(2,1)S(1)}, bf16[8,2,2,512]{3,2,1,0:T(2,128)(2,1)S(1)}, u32[]{:S(2)}, u32[]{:S(2)}) collective-permute-start(bf16[8,2,2,512]{3,2,1,0:T(2,128)(2,1)S(1)} %get-tuple-element.15), channel_id=1, source_target_pairs={{0,2},{2,0},{4,6},{6,4},{8,10},{10,8},{12,14},{14,12},{16,18},{18,... | collective-permute-start | bytes 98312 | tf_op jit(solution)/shard_map/ppermute | solution.py:31
  113.1 2.7 %collective-permute-done.5 = bf16[8,2,2,512]{3,2,1,0:T(2,128)(2,1)S(1)} collective-permute-done((bf16[8,2,2,512]{3,2,1,0:T(2,128)(2,1)S(1)}, bf16[8,2,2,512]{3,2,1,0:T(2,128)(2,1)S(1)}, u32[]{:S(2)}, u32[]{:S(2)}) %collective-permute-start.5) | collective-permute-done | bytes 32800 | tf_op jit(solution)/shard_map/ppermute | solution.py:31
  115.8 0.1 broadcast_select_fusion.2
  115.9 0.1 constant_dynamic-slice_fusion
  116.0 0.3 fusion
  116.2 13.0 %collective-permute-start.8 = (bf16[256,512]{1,0:T(8,128)(2,1)S(1)}, bf16[256,512]{1,0:T(8,128)(2,1)S(1)}, u32[]{:S(2)}, u32[]{:S(2)}) collective-permute-start(bf16[256,512]{1,0:T(8,128)(2,1)S(1)} %fusion), channel_id=1, source_target_pairs={{0,1},{1,0},{2,3},{3,2},{4,5},{5,4},{6,7},{7,6},{8,9},{9,8},{10,11... | collective-permute-start | bytes 786440 | tf_op jit(solution)/shard_map/ppermute | solution.py:34
  129.3 1.9 %collective-permute-start.7 = (bf16[8,2,2,512]{3,2,1,0:T(2,128)(2,1)S(1)}, bf16[8,2,2,512]{3,2,1,0:T(2,128)(2,1)S(1)}, u32[]{:S(2)}, u32[]{:S(2)}) collective-permute-start(bf16[8,2,2,512]{3,2,1,0:T(2,128)(2,1)S(1)} %get-tuple-element.18), channel_id=1, source_target_pairs={{0,1},{1,0},{2,3},{3,2},{4,5},{5,4},{6,7},{7,6},{8,9},{9,8},{10,11... | collective-permute-start | bytes 98312 | tf_op jit(solution)/shard_map/ppermute | solution.py:34
  131.2 0.3 fusion.10
  131.4 0.9 collective-permute-done.7
  132.4 0.1 broadcast_select_fusion.3
  132.5 0.7 select_n.138
  133.1 1.1 convert_add_fusion
  (36 shorter events, 0.4 us)
Async XLA Ops:
  0.6 27.6 %copy-start = (bf16[128,4096]{1,0:T(8,128)(2,1)S(1)}, bf16[128,4096]{1,0:T(8,128)(2,1)}, u32[]{:S(2)}) copy-start(bf16[128,4096]{1,0:T(8,128)(2,1)} %param.8) | copy-start | bytes 3145732
  0.6 30.8 %collective-permute-start = (bf16[256,512]{1,0:T(8,128)(2,1)}, bf16[256,512]{1,0:T(8,128)(2,1)S(1)}, u32[]{:S(2)}, u32[]{:S(2)}) collective-permute-start(bf16[256,512]{1,0:T(8,128)(2,1)} %param.12), channel_id=1, source_target_pairs={{0,2},{2,0},{4,6},{6,4},{8,10},{10,8},{12,14},{14,12},{16,18},{18,... | collective-permute-start | bytes 786440 | tf_op jit(solution)/shard_map/ppermute | solution.py:31
  5.6 19.3 %copy-start.3 = (bf16[64,512]{1,0:T(8,128)(2,1)S(1)}, bf16[64,512]{1,0:T(8,128)(2,1)}, u32[]{:S(2)}) copy-start(bf16[64,512]{1,0:T(8,128)(2,1)} %param.13) | copy-start | bytes 196612
  7.2 21.0 %copy-start.2 = (bf16[32,4096]{1,0:T(8,128)(2,1)S(1)}, bf16[32,4096]{1,0:T(8,128)(2,1)}, u32[]{:S(2)}) copy-start(bf16[32,4096]{1,0:T(8,128)(2,1)} %param.7) | copy-start | bytes 786436
  7.2 30.8 %all-to-all-start = ((bf16[8,8,1024]{2,1,0:T(8,128)(2,1)}), bf16[8,8,1024]{2,1,0:T(8,128)(2,1)S(1)}, u32[]{:S(2)}, u32[]{:S(2)}) async-start(bf16[8,8,1024]{2,1,0:T(8,128)(2,1)} %bitcast.1), calls=%async_computation | async-start | bytes 262144 | tf_op jit(solution)/shard_map/all_to_all | solution.py:37
  25.0 4.0 %collective-permute-start.2 = (bf16[8,2,2,512]{3,2,1,0:T(2,128)(2,1)S(1)}, bf16[8,2,2,512]{3,2,1,0:T(2,128)(2,1)S(1)}, u32[]{:S(2)}, u32[]{:S(2)}) collective-permute-start(bf16[8,2,2,512]{3,2,1,0:T(2,128)(2,1)S(1)} %get-tuple-element.29), channel_id=1, source_target_pairs={{0,1},{1,0},{2,3},{3,2},{4,5},{5,4},{6,7},{7,6},{8,9},{9,8},{10,11... | collective-permute-start | bytes 98312 | tf_op jit(solution)/shard_map/ppermute | solution.py:34
  28.8 2.7 %copy-start.1 = (bf16[256,512]{1,0:T(8,128)(2,1)S(1)}, bf16[256,512]{1,0:T(8,128)(2,1)}, u32[]{:S(2)}) copy-start(bf16[256,512]{1,0:T(8,128)(2,1)} %param.12) | copy-start | bytes 786436
  29.2 5.6 %collective-permute-start.3 = (bf16[2,8,2,512]{3,2,0,1:T(2,128)(2,1)S(1)}, bf16[2,8,2,512]{3,2,0,1:T(2,128)(2,1)S(1)}, u32[]{:S(2)}, u32[]{:S(2)}) collective-permute-start(bf16[2,8,2,512]{3,2,0,1:T(2,128)(2,1)S(1)} %bitcast.67), channel_id=1, source_target_pairs={{0,2},{2,0},{4,6},{6,4},{8,10},{10,8},{12,14},{14,12},{16,18},{18,... | collective-permute-start | bytes 98312 | tf_op jit(solution)/shard_map/ppermute | solution.py:31
  32.3 16.1 %collective-permute-start.1 = (bf16[2,256,512]{2,1,0:T(8,128)(2,1)}, bf16[2,256,512]{2,1,0:T(8,128)(2,1)S(1)}, u32[]{:S(2)}, u32[]{:S(2)}) collective-permute-start(bf16[2,256,512]{2,1,0:T(8,128)(2,1)} %maximum_select_fusion.2), channel_id=1, source_target_pairs={{0,1},{1,0},{2,3},{3,2},{4,5},{5,4},{6,7},{7,6},{8,9},{9,8},{10,11... | collective-permute-start | bytes 1572872 | tf_op jit(solution)/shard_map/ppermute | solution.py:34
  49.8 28.4 %all-to-all-start.1 = ((bf16[8,40,512]{2,1,0:T(8,128)(2,1)}), bf16[8,40,512]{2,1,0:T(8,128)(2,1)S(1)}, u32[]{:S(2)}, u32[]{:S(2)}) async-start(bf16[8,40,512]{2,1,0:T(8,128)(2,1)} %pad_maximum_fusion), calls=%async_computation.1 | async-start | bytes 655360 | tf_op jit(solution)/shard_map/all_to_all | solution.py:37
  59.8 0.7 copy-start.4
  60.8 17.5 %copy-start.5 = (s32[32]{0:T(128)S(1)}, s32[32]{0:T(128)}, u32[]{:S(2)}) copy-start(s32[32]{0:T(128)} %param.9) | copy-start | bytes 388
  60.8 19.0 %collective-permute-start.4 = (bf16[256,512]{1,0:T(8,128)(2,1)S(1)}, bf16[256,512]{1,0:T(8,128)(2,1)S(1)}, u32[]{:S(2)}, u32[]{:S(2)}) collective-permute-start(bf16[256,512]{1,0:T(8,128)(2,1)S(1)} %get-tuple-element.12), channel_id=1, source_target_pairs={{0,2},{2,0},{4,6},{6,4},{8,10},{10,8},{12,14},{14,12},{16,18},{18,... | collective-permute-start | bytes 786440 | tf_op jit(solution)/shard_map/ppermute | solution.py:31
  79.8 27.6 %all-to-all-start.2 = ((bf16[8,40,512]{2,1,0:T(8,128)(2,1)}), bf16[8,40,512]{2,1,0:T(8,128)(2,1)S(1)}, u32[]{:S(2)}, u32[]{:S(2)}) async-start(bf16[8,40,512]{2,1,0:T(8,128)(2,1)} %pad_maximum_fusion.1), calls=%async_computation.2 | async-start | bytes 655360 | tf_op jit(solution)/shard_map/all_to_all | solution.py:37
  107.4 8.5 %collective-permute-start.6 = (bf16[256,512]{1,0:T(8,128)(2,1)S(1)}, bf16[256,512]{1,0:T(8,128)(2,1)S(1)}, u32[]{:S(2)}, u32[]{:S(2)}) collective-permute-start(bf16[256,512]{1,0:T(8,128)(2,1)S(1)} %bitcast.57), channel_id=1, source_target_pairs={{0,2},{2,0},{4,6},{6,4},{8,10},{10,8},{12,14},{14,12},{16,18},{18,... | collective-permute-start | bytes 786440 | tf_op jit(solution)/shard_map/ppermute | solution.py:31
  110.8 5.0 %collective-permute-start.5 = (bf16[8,2,2,512]{3,2,1,0:T(2,128)(2,1)S(1)}, bf16[8,2,2,512]{3,2,1,0:T(2,128)(2,1)S(1)}, u32[]{:S(2)}, u32[]{:S(2)}) collective-permute-start(bf16[8,2,2,512]{3,2,1,0:T(2,128)(2,1)S(1)} %get-tuple-element.15), channel_id=1, source_target_pairs={{0,2},{2,0},{4,6},{6,4},{8,10},{10,8},{12,14},{14,12},{16,18},{18,... | collective-permute-start | bytes 98312 | tf_op jit(solution)/shard_map/ppermute | solution.py:31
  116.2 16.9 %collective-permute-start.8 = (bf16[256,512]{1,0:T(8,128)(2,1)S(1)}, bf16[256,512]{1,0:T(8,128)(2,1)S(1)}, u32[]{:S(2)}, u32[]{:S(2)}) collective-permute-start(bf16[256,512]{1,0:T(8,128)(2,1)S(1)} %fusion), channel_id=1, source_target_pairs={{0,1},{1,0},{2,3},{3,2},{4,5},{5,4},{6,7},{7,6},{8,9},{9,8},{10,11... | collective-permute-start | bytes 786440 | tf_op jit(solution)/shard_map/ppermute | solution.py:34
  129.3 3.1 %collective-permute-start.7 = (bf16[8,2,2,512]{3,2,1,0:T(2,128)(2,1)S(1)}, bf16[8,2,2,512]{3,2,1,0:T(2,128)(2,1)S(1)}, u32[]{:S(2)}, u32[]{:S(2)}) collective-permute-start(bf16[8,2,2,512]{3,2,1,0:T(2,128)(2,1)S(1)} %get-tuple-element.18), channel_id=1, source_target_pairs={{0,1},{1,0},{2,3},{3,2},{4,5},{5,4},{6,7},{7,6},{8,9},{9,8},{10,11... | collective-permute-start | bytes 98312 | tf_op jit(solution)/shard_map/ppermute | solution.py:34

commit v8 on v7

--- a/solution.py
+++ b/solution.py
@@ -36,12 +36,13 @@
     def exchange(x):
         return lax.all_to_all(x, "z", 0, 0, tiled=True, axis_index_groups=stride2)
 
+    share = local // nx
+    sent = lax.dynamic_slice_in_dim(rows, lax.axis_index("x") * share, share, 0)
+    sent, weight = lax.optimization_barrier((sent, weight))
+    came = exchange(sent.reshape(share, nj, quad).transpose(1, 0, 2))
+
     w_pair = both(b, weight, pair(weight), 0)
     w_quad = both(c, w_pair, core(w_pair), 1).reshape(quad, cols)
-
-    share = local // nx
-    sent = lax.dynamic_slice_in_dim(rows, lax.axis_index("x") * share, share, 0)
-    came = exchange(sent.reshape(share, nj, quad).transpose(1, 0, 2))
 
     projected = lax.dot_general(
         proj_grads, inv_factor, (((1,), (1,)), ((), ())), preferred_element_type=F32
@@ -79,9 +80,9 @@
     _, score, x_same, x_sent = lax.optimization_barrier(
         (partial[:8, :128], score, x_same, x_sent)
     )
+    came = exchange(sent)
+    scores, x_sent = lax.optimization_barrier((lax.psum(score, "y"), x_sent))
     x_flip = pair(x_sent)
-    came = exchange(sent)
-    scores = lax.psum(score, "y")
     importance = (counts.astype(F32) * proj_grads.shape[1] / scores).astype(BF)
     hidden = jnp.sum(came[:, :local].astype(F32), axis=0)
     cot = jnp.dot(placer, came[:, local:].reshape(2 * groups, cols), preferred_element_type=F32)

time: 135 us -> 141 us (1.044)
  waiting for transfers between devices: 23 us -> 27.4 us
    ppermute x5, waiting for transfers between devices: 2.97 us -> 10.3 us  [pair(): return lax.ppermute(x, 'z', flip)]
    all_to_all x3, waiting for transfers between devices: 18.9 us -> 16.1 us  [exchange(): return lax.all_to_all(x, 'z', 0, 0, tiled=True, axis_index_groups=stride2)]
    all_to_all x3, starting transfers between devices: 39.2 us -> 41.3 us  [exchange(): return lax.all_to_all(x, 'z', 0, 0, tiled=True, axis_index_groups=stride2)]
    ppermute x5, starting transfers between devices: 15.4 us -> 13.6 us  [pair(): return lax.ppermute(x, 'z', flip)]
  transfers between devices with their start and end apart: 12 -> 12, of which waited for: 6 -> 6; matrix products, arithmetic and copies ran while one was open for 5% -> 4% of each run, Pallas kernels for 0% -> 0%
where the time goes in v8:
time: 141 us; the launch traced here: 140 us
  starting transfers between devices  76.1 us (54%)
  waiting for transfers between devices  27.4 us (19%)
  blocking collectives  25.5 us (18%)
  local copies, waits for them, and re-layouts  3.59 us (3%)
  matrix products  3.44 us (2%)
  other arithmetic  3.19 us (2%)
    all_to_all x3, starting transfers between devices, exchange(): return lax.all_to_all(x, 'z', 0, 0, tiled=True, axis_index_groups=stride2)  41.3 us
    ppermute x4, starting transfers between devices, core(): return lax.ppermute(x, 'c', SWAP)  21.2 us
    all_to_all x3, waiting for transfers between devices, exchange(): return lax.all_to_all(x, 'z', 0, 0, tiled=True, axis_index_groups=stride2)  16.1 us
    psum x1, blocking collectives, shards(): scores, x_sent = lax.optimization_barrier((lax.psum(score, 'y'), x_sent))  14.2 us
    ppermute x5, starting transfers between devices, pair(): return lax.ppermute(x, 'z', flip)  13.6 us
    all_gather x1, blocking collectives, shards(): lax.all_gather(jnp.concatenate([came, thirds], 0), 'x', axis=1, tiled=True)  11.4 us
    ppermute x5, waiting for transfers between devices, pair(): return lax.ppermute(x, 'z', flip)  10.3 us
  transfers between devices with their start and end apart: 12, of which 6 were waited for; matrix products, arithmetic and copies ran while one was open for 4% of the time, Pallas kernels for 0%

profile of v8, /device:TPU:1, one launch (start us, length us, event | category | flops | bytes accessed | tf_op | source)
XLA Modules:
  0.0 140.3 jit_solution(16709362485606100012)
XLA Ops:
  0.6 0.0 copy-start
  0.7 1.7 %constant_dynamic-slice_fusion.6 = bf16[8,8192]{1,0:T(8,128)(2,1)} fusion(bf16[32,8192]{1,0:T(8,128)(2,1)} %param.11, s32[]{:T(128)S(6)} %select_n.117), kind=kLoop, calls=%fused_computation.60 | loop fusion | bytes 262148 | tf_op jit(solution)/shard_map/dynamic_slice | solution.py:40
  2.3 19.4 %all-to-all-start = ((bf16[8,8,1024]{2,1,0:T(8,128)(2,1)}), bf16[8,8,1024]{2,1,0:T(8,128)(2,1)S(1)}, u32[]{:S(2)}, u32[]{:S(2)}) async-start(bf16[8,8,1024]{2,1,0:T(8,128)(2,1)} %bitcast.1), calls=%async_computation | async-start | bytes 262144 | tf_op jit(solution)/shard_map/all_to_all | solution.py:37
  21.8 3.1 %collective-permute-start = (bf16[256,512]{1,0:T(8,128)(2,1)S(1)}, bf16[256,512]{1,0:T(8,128)(2,1)S(1)}, u32[]{:S(2)}, u32[]{:S(2)}) collective-permute-start(bf16[256,512]{1,0:T(8,128)(2,1)S(1)} %copy-done.1), channel_id=1, source_target_pairs={{0,2},{2,0},{4,6},{6,4},{8,10},{10,8},{12,14},{14,12},{16,18},{18,... | collective-permute-start | bytes 786440 | tf_op jit(solution)/shard_map/ppermute | solution.py:31
  24.9 0.1 dynamic-slice_bitcast_fusion.3
  25.0 3.1 %collective-permute-start.2 = (bf16[8,2,2,512]{3,2,1,0:T(2,128)(2,1)S(1)}, bf16[8,2,2,512]{3,2,1,0:T(2,128)(2,1)S(1)}, u32[]{:S(2)}, u32[]{:S(2)}) collective-permute-start(bf16[8,2,2,512]{3,2,1,0:T(2,128)(2,1)S(1)} %get-tuple-element.37), channel_id=1, source_target_pairs={{0,1},{1,0},{2,3},{3,2},{4,5},{5,4},{6,7},{7,6},{8,9},{9,8},{10,11... | collective-permute-start | bytes 98312 | tf_op jit(solution)/shard_map/ppermute | solution.py:34
  28.2 0.6 fusion.6
  28.8 0.1 pad_maximum_fusion.3
  28.8 0.1 collective-permute-done.2
  29.0 0.1 broadcast_select_fusion
  29.1 0.1 constant_dynamic-slice_fusion.3
  29.2 2.2 %collective-permute-start.3 = (bf16[2,8,2,512]{3,2,0,1:T(2,128)(2,1)S(1)}, bf16[2,8,2,512]{3,2,0,1:T(2,128)(2,1)S(1)}, u32[]{:S(2)}, u32[]{:S(2)}) collective-permute-start(bf16[2,8,2,512]{3,2,0,1:T(2,128)(2,1)S(1)} %bitcast.67), channel_id=1, source_target_pairs={{0,2},{2,0},{4,6},{6,4},{8,10},{10,8},{12,14},{14,12},{16,18},{18,... | collective-permute-start | bytes 98312 | tf_op jit(solution)/shard_map/ppermute | solution.py:31
  31.4 4.3 %collective-permute-done = bf16[256,512]{1,0:T(8,128)(2,1)S(1)} collective-permute-done((bf16[256,512]{1,0:T(8,128)(2,1)S(1)}, bf16[256,512]{1,0:T(8,128)(2,1)S(1)}, u32[]{:S(2)}, u32[]{:S(2)}) %collective-permute-start) | collective-permute-done | bytes 262176 | tf_op jit(solution)/shard_map/ppermute | solution.py:31
  35.7 0.9 maximum_select_fusion.2
  36.5 3.0 %collective-permute-start.1 = (bf16[2,256,512]{2,1,0:T(8,128)(2,1)}, bf16[2,256,512]{2,1,0:T(8,128)(2,1)S(1)}, u32[]{:S(2)}, u32[]{:S(2)}) collective-permute-start(bf16[2,256,512]{2,1,0:T(8,128)(2,1)} %maximum_select_fusion.2), channel_id=1, source_target_pairs={{0,1},{1,0},{2,3},{3,2},{4,5},{5,4},{6,7},{7,6},{8,9},{9,8},{10,11... | collective-permute-start | bytes 1572872 | tf_op jit(solution)/shard_map/ppermute | solution.py:34
  39.6 0.1 fusion.15
  39.8 0.1 maximum_select_fusion.1
  39.9 11.4 %all_gather.3 = bf16[9,32,1024]{2,1,0:T(8,128)(2,1)S(1)} all-gather(bf16[9,8,1024]{2,1,0:T(8,128)(2,1)S(1)} %pad_maximum_fusion.2), channel_id=1, replica_groups=mesh['x'=4,'y'=8,'z'=16,'c'=2] {'x'}, dimensions={1}, use_global_device_ids=true | all-gather | bytes 737280 | tf_op jit(solution)/shard_map/all_gather | solution.py:57
  51.3 0.1 maximum_select_fusion
  51.5 0.4 convolution_convert_fusion
  51.9 0.7 pad_maximum_fusion
  52.7 10.1 %all-to-all-start.1 = ((bf16[8,40,512]{2,1,0:T(8,128)(2,1)}), bf16[8,40,512]{2,1,0:T(8,128)(2,1)S(1)}, u32[]{:S(2)}, u32[]{:S(2)}) async-start(bf16[8,40,512]{2,1,0:T(8,128)(2,1)} %pad_maximum_fusion), calls=%async_computation.1 | async-start | bytes 655360 | tf_op jit(solution)/shard_map/all_to_all | solution.py:37
  62.8 0.7 copy-done.4
  63.4 0.1 fusion.5
  63.6 0.1 reshape.152
  63.8 14.2 %psum.7 = f32[32]{0:T(128)S(1)} all-reduce(f32[32]{0:T(128)S(1)} %reduce_sum.39), channel_id=1, replica_groups=mesh['x'=4,'y'=8,'z'=16,'c'=2] {'y'}, use_global_device_ids=true, to_apply=%region_2.3 | all-reduce | flops 32 | bytes 256 | tf_op jit(solution)/shard_map/psum | solution.py:84
  77.9 3.1 %collective-permute-start.4 = (bf16[256,512]{1,0:T(8,128)(2,1)S(1)}, bf16[256,512]{1,0:T(8,128)(2,1)S(1)}, u32[]{:S(2)}, u32[]{:S(2)}) collective-permute-start(bf16[256,512]{1,0:T(8,128)(2,1)S(1)} %get-tuple-element.20), channel_id=1, source_target_pairs={{0,2},{2,0},{4,6},{6,4},{8,10},{10,8},{12,14},{14,12},{16,18},{18,... | collective-permute-start | bytes 786440 | tf_op jit(solution)/shard_map/ppermute | solution.py:31
  81.1 0.2 fusion.4
  81.3 0.3 fusion.1
  81.6 0.8 pad_maximum_fusion.1
  82.4 3.0 %collective-permute-done.4 = bf16[256,512]{1,0:T(8,128)(2,1)S(1)} collective-permute-done((bf16[256,512]{1,0:T(8,128)(2,1)S(1)}, bf16[256,512]{1,0:T(8,128)(2,1)S(1)}, u32[]{:S(2)}, u32[]{:S(2)}) %collective-permute-start.4) | collective-permute-done | bytes 262176 | tf_op jit(solution)/shard_map/ppermute | solution.py:31
  85.3 11.7 %all-to-all-start.2 = ((bf16[8,40,512]{2,1,0:T(8,128)(2,1)}), bf16[8,40,512]{2,1,0:T(8,128)(2,1)S(1)}, u32[]{:S(2)}, u32[]{:S(2)}) async-start(bf16[8,40,512]{2,1,0:T(8,128)(2,1)} %pad_maximum_fusion.1), calls=%async_computation.2 | async-start | bytes 655360 | tf_op jit(solution)/shard_map/all_to_all | solution.py:37
  97.1 16.1 %all-to-all-done.2 = bf16[8,40,512]{2,1,0:T(8,128)(2,1)S(1)} async-done(((bf16[8,40,512]{2,1,0:T(8,128)(2,1)}), bf16[8,40,512]{2,1,0:T(8,128)(2,1)S(1)}, u32[]{:S(2)}, u32[]{:S(2)}) %all-to-all-start.2) | async-done | bytes 327712 | tf_op jit(solution)/shard_map/all_to_all | solution.py:37
  113.2 3.2 %collective-permute-start.6 = (bf16[256,512]{1,0:T(8,128)(2,1)S(1)}, bf16[256,512]{1,0:T(8,128)(2,1)S(1)}, u32[]{:S(2)}, u32[]{:S(2)}) collective-permute-start(bf16[256,512]{1,0:T(8,128)(2,1)S(1)} %bitcast.57), channel_id=1, source_target_pairs={{0,2},{2,0},{4,6},{6,4},{8,10},{10,8},{12,14},{14,12},{16,18},{18,... | collective-permute-start | bytes 786440 | tf_op jit(solution)/shard_map/ppermute | solution.py:31
  116.4 0.2 fusion.13
  116.7 0.1 constant_dynamic-slice_fusion.1
  116.7 2.1 %collective-permute-start.5 = (bf16[8,2,2,512]{3,2,1,0:T(2,128)(2,1)S(1)}, bf16[8,2,2,512]{3,2,1,0:T(2,128)(2,1)S(1)}, u32[]{:S(2)}, u32[]{:S(2)}) collective-permute-start(bf16[8,2,2,512]{3,2,1,0:T(2,128)(2,1)S(1)} %get-tuple-element.23), channel_id=1, source_target_pairs={{0,2},{2,0},{4,6},{6,4},{8,10},{10,8},{12,14},{14,12},{16,18},{18,... | collective-permute-start | bytes 98312 | tf_op jit(solution)/shard_map/ppermute | solution.py:31
  118.8 3.0 %collective-permute-done.5 = bf16[8,2,2,512]{3,2,1,0:T(2,128)(2,1)S(1)} collective-permute-done((bf16[8,2,2,512]{3,2,1,0:T(2,128)(2,1)S(1)}, bf16[8,2,2,512]{3,2,1,0:T(2,128)(2,1)S(1)}, u32[]{:S(2)}, u32[]{:S(2)}) %collective-permute-start.5) | collective-permute-done | bytes 32800 | tf_op jit(solution)/shard_map/ppermute | solution.py:31
  121.9 0.1 broadcast_select_fusion.2
  122.0 0.1 constant_dynamic-slice_fusion
  122.1 0.3 fusion
  122.3 13.1 %collective-permute-start.8 = (bf16[256,512]{1,0:T(8,128)(2,1)S(1)}, bf16[256,512]{1,0:T(8,128)(2,1)S(1)}, u32[]{:S(2)}, u32[]{:S(2)}) collective-permute-start(bf16[256,512]{1,0:T(8,128)(2,1)S(1)} %fusion), channel_id=1, source_target_pairs={{0,1},{1,0},{2,3},{3,2},{4,5},{5,4},{6,7},{7,6},{8,9},{9,8},{10,11... | collective-permute-start | bytes 786440 | tf_op jit(solution)/shard_map/ppermute | solution.py:34
  135.4 1.9 %collective-permute-start.7 = (bf16[8,2,2,512]{3,2,1,0:T(2,128)(2,1)S(1)}, bf16[8,2,2,512]{3,2,1,0:T(2,128)(2,1)S(1)}, u32[]{:S(2)}, u32[]{:S(2)}) collective-permute-start(bf16[8,2,2,512]{3,2,1,0:T(2,128)(2,1)S(1)} %get-tuple-element.26), channel_id=1, source_target_pairs={{0,1},{1,0},{2,3},{3,2},{4,5},{5,4},{6,7},{7,6},{8,9},{9,8},{10,11... | collective-permute-start | bytes 98312 | tf_op jit(solution)/shard_map/ppermute | solution.py:34
  137.3 0.3 fusion.10
  137.6 0.9 collective-permute-done.7
  138.5 0.1 broadcast_select_fusion.3
  138.6 0.7 select_n.138
  139.2 1.1 convert_add_fusion
  (36 shorter events, 0.4 us)
Async XLA Ops:
  0.6 27.5 %copy-start = (bf16[128,4096]{1,0:T(8,128)(2,1)S(1)}, bf16[128,4096]{1,0:T(8,128)(2,1)}, u32[]{:S(2)}) copy-start(bf16[128,4096]{1,0:T(8,128)(2,1)} %param.8) | copy-start | bytes 3145732
  0.7 21.1 %copy-start.1 = (bf16[256,512]{1,0:T(8,128)(2,1)S(1)}, bf16[256,512]{1,0:T(8,128)(2,1)}, u32[]{:S(2)}) copy-start(bf16[256,512]{1,0:T(8,128)(2,1)} %param.12) | copy-start | bytes 786436
  0.7 24.2 %copy-start.3 = (bf16[64,512]{1,0:T(8,128)(2,1)S(1)}, bf16[64,512]{1,0:T(8,128)(2,1)}, u32[]{:S(2)}) copy-start(bf16[64,512]{1,0:T(8,128)(2,1)} %param.13) | copy-start | bytes 196612
  2.3 25.8 %copy-start.2 = (bf16[32,4096]{1,0:T(8,128)(2,1)S(1)}, bf16[32,4096]{1,0:T(8,128)(2,1)}, u32[]{:S(2)}) copy-start(bf16[32,4096]{1,0:T(8,128)(2,1)} %param.7) | copy-start | bytes 786436
  2.3 37.5 %all-to-all-start = ((bf16[8,8,1024]{2,1,0:T(8,128)(2,1)}), bf16[8,8,1024]{2,1,0:T(8,128)(2,1)S(1)}, u32[]{:S(2)}, u32[]{:S(2)}) async-start(bf16[8,8,1024]{2,1,0:T(8,128)(2,1)} %bitcast.1), calls=%async_computation | async-start | bytes 262144 | tf_op jit(solution)/shard_map/all_to_all | solution.py:37
  21.8 13.9 %collective-permute-start = (bf16[256,512]{1,0:T(8,128)(2,1)S(1)}, bf16[256,512]{1,0:T(8,128)(2,1)S(1)}, u32[]{:S(2)}, u32[]{:S(2)}) collective-permute-start(bf16[256,512]{1,0:T(8,128)(2,1)S(1)} %copy-done.1), channel_id=1, source_target_pairs={{0,2},{2,0},{4,6},{6,4},{8,10},{10,8},{12,14},{14,12},{16,18},{18,... | collective-permute-start | bytes 786440 | tf_op jit(solution)/shard_map/ppermute | solution.py:31
  25.0 4.0 %collective-permute-start.2 = (bf16[8,2,2,512]{3,2,1,0:T(2,128)(2,1)S(1)}, bf16[8,2,2,512]{3,2,1,0:T(2,128)(2,1)S(1)}, u32[]{:S(2)}, u32[]{:S(2)}) collective-permute-start(bf16[8,2,2,512]{3,2,1,0:T(2,128)(2,1)S(1)} %get-tuple-element.37), channel_id=1, source_target_pairs={{0,1},{1,0},{2,3},{3,2},{4,5},{5,4},{6,7},{7,6},{8,9},{9,8},{10,11... | collective-permute-start | bytes 98312 | tf_op jit(solution)/shard_map/ppermute | solution.py:34
  29.2 10.4 %collective-permute-start.3 = (bf16[2,8,2,512]{3,2,0,1:T(2,128)(2,1)S(1)}, bf16[2,8,2,512]{3,2,0,1:T(2,128)(2,1)S(1)}, u32[]{:S(2)}, u32[]{:S(2)}) collective-permute-start(bf16[2,8,2,512]{3,2,0,1:T(2,128)(2,1)S(1)} %bitcast.67), channel_id=1, source_target_pairs={{0,2},{2,0},{4,6},{6,4},{8,10},{10,8},{12,14},{14,12},{16,18},{18,... | collective-permute-start | bytes 98312 | tf_op jit(solution)/shard_map/ppermute | solution.py:31
  36.5 14.7 %collective-permute-start.1 = (bf16[2,256,512]{2,1,0:T(8,128)(2,1)}, bf16[2,256,512]{2,1,0:T(8,128)(2,1)S(1)}, u32[]{:S(2)}, u32[]{:S(2)}) collective-permute-start(bf16[2,256,512]{2,1,0:T(8,128)(2,1)} %maximum_select_fusion.2), channel_id=1, source_target_pairs={{0,1},{1,0},{2,3},{3,2},{4,5},{5,4},{6,7},{7,6},{8,9},{9,8},{10,11... | collective-permute-start | bytes 1572872 | tf_op jit(solution)/shard_map/ppermute | solution.py:34
  52.7 28.4 %all-to-all-start.1 = ((bf16[8,40,512]{2,1,0:T(8,128)(2,1)}), bf16[8,40,512]{2,1,0:T(8,128)(2,1)S(1)}, u32[]{:S(2)}, u32[]{:S(2)}) async-start(bf16[8,40,512]{2,1,0:T(8,128)(2,1)} %pad_maximum_fusion), calls=%async_computation.1 | async-start | bytes 655360 | tf_op jit(solution)/shard_map/all_to_all | solution.py:37
  62.8 0.7 copy-start.4
  63.8 17.3 %copy-start.5 = (s32[32]{0:T(128)S(1)}, s32[32]{0:T(128)}, u32[]{:S(2)}) copy-start(s32[32]{0:T(128)} %param.9) | copy-start | bytes 388
  77.9 7.4 %collective-permute-start.4 = (bf16[256,512]{1,0:T(8,128)(2,1)S(1)}, bf16[256,512]{1,0:T(8,128)(2,1)S(1)}, u32[]{:S(2)}, u32[]{:S(2)}) collective-permute-start(bf16[256,512]{1,0:T(8,128)(2,1)S(1)} %get-tuple-element.20), channel_id=1, source_target_pairs={{0,2},{2,0},{4,6},{6,4},{8,10},{10,8},{12,14},{14,12},{16,18},{18,... | collective-permute-start | bytes 786440 | tf_op jit(solution)/shard_map/ppermute | solution.py:31
  85.3 27.8 %all-to-all-start.2 = ((bf16[8,40,512]{2,1,0:T(8,128)(2,1)}), bf16[8,40,512]{2,1,0:T(8,128)(2,1)S(1)}, u32[]{:S(2)}, u32[]{:S(2)}) async-start(bf16[8,40,512]{2,1,0:T(8,128)(2,1)} %pad_maximum_fusion.1), calls=%async_computation.2 | async-start | bytes 655360 | tf_op jit(solution)/shard_map/all_to_all | solution.py:37
  113.2 8.8 %collective-permute-start.6 = (bf16[256,512]{1,0:T(8,128)(2,1)S(1)}, bf16[256,512]{1,0:T(8,128)(2,1)S(1)}, u32[]{:S(2)}, u32[]{:S(2)}) collective-permute-start(bf16[256,512]{1,0:T(8,128)(2,1)S(1)} %bitcast.57), channel_id=1, source_target_pairs={{0,2},{2,0},{4,6},{6,4},{8,10},{10,8},{12,14},{14,12},{16,18},{18,... | collective-permute-start | bytes 786440 | tf_op jit(solution)/shard_map/ppermute | solution.py:31
  116.7 5.2 %collective-permute-start.5 = (bf16[8,2,2,512]{3,2,1,0:T(2,128)(2,1)S(1)}, bf16[8,2,2,512]{3,2,1,0:T(2,128)(2,1)S(1)}, u32[]{:S(2)}, u32[]{:S(2)}) collective-permute-start(bf16[8,2,2,512]{3,2,1,0:T(2,128)(2,1)S(1)} %get-tuple-element.23), channel_id=1, source_target_pairs={{0,2},{2,0},{4,6},{6,4},{8,10},{10,8},{12,14},{14,12},{16,18},{18,... | collective-permute-start | bytes 98312 | tf_op jit(solution)/shard_map/ppermute | solution.py:31
  122.3 16.9 %collective-permute-start.8 = (bf16[256,512]{1,0:T(8,128)(2,1)S(1)}, bf16[256,512]{1,0:T(8,128)(2,1)S(1)}, u32[]{:S(2)}, u32[]{:S(2)}) collective-permute-start(bf16[256,512]{1,0:T(8,128)(2,1)S(1)} %fusion), channel_id=1, source_target_pairs={{0,1},{1,0},{2,3},{3,2},{4,5},{5,4},{6,7},{7,6},{8,9},{9,8},{10,11... | collective-permute-start | bytes 786440 | tf_op jit(solution)/shard_map/ppermute | solution.py:34
  135.4 3.1 %collective-permute-start.7 = (bf16[8,2,2,512]{3,2,1,0:T(2,128)(2,1)S(1)}, bf16[8,2,2,512]{3,2,1,0:T(2,128)(2,1)S(1)}, u32[]{:S(2)}, u32[]{:S(2)}) collective-permute-start(bf16[8,2,2,512]{3,2,1,0:T(2,128)(2,1)S(1)} %get-tuple-element.26), channel_id=1, source_target_pairs={{0,1},{1,0},{2,3},{3,2},{4,5},{5,4},{6,7},{7,6},{8,9},{9,8},{10,11... | collective-permute-start | bytes 98312 | tf_op jit(solution)/shard_map/ppermute | solution.py:34

commit v9 on v7

--- a/solution.py
+++ b/solution.py
@@ -53,7 +53,10 @@
     thirds = jnp.concatenate([high, middle, low, jnp.zeros(quad - 3 * local, F32)]).astype(BF)
     thirds = jnp.broadcast_to(thirds[None, None, :], (1, share, quad))
 
-    came = lax.all_gather(jnp.concatenate([came, thirds], 0), "x", axis=1, tiled=True)
+    sent = jnp.concatenate([came, thirds], 0)
+    sent = jnp.broadcast_to(sent[None], (nx, nj + 1, share, quad))
+    came = lax.all_to_all(sent, "x", 0, 0, tiled=True)
+    came = came.transpose(1, 0, 2, 3).reshape(nj + 1, local, quad)
     x_class = came[:nj].reshape(nj * local, quad)
     thirds = came[nj].reshape(nx, share, quad)[:, 0, : 3 * local].astype(F32)
     score = jnp.sum(thirds.reshape(nx * 3, local), axis=0)

time: 135 us -> 140 us (1.037)
  blocking collectives: 24.8 us -> 14.5 us
  waiting for transfers between devices: 23 us -> 29.7 us
  starting transfers between devices: 75.2 us -> 80.7 us
  local copies, waits for them, and re-layouts: 3.52 us -> 6.47 us
    all_gather x1 -> x0, blocking collectives: 10.4 us -> none  [shards(): lax.all_gather(jnp.concatenate([came, thirds], 0), 'x', axis=1, tiled=True)]
    ppermute x5, waiting for transfers between devices: 2.97 us -> 11.7 us  [pair(): return lax.ppermute(x, 'z', flip)]
    all_to_all x0 -> x1, starting transfers between devices: none -> 4.01 us  [shards(): came = lax.all_to_all(sent, 'x', 0, 0, tiled=True)]
    all_to_all x3, starting transfers between devices: 39.2 us -> 42.2 us  [exchange(): return lax.all_to_all(x, 'z', 0, 0, tiled=True, axis_index_groups=stride2)]
    all_to_all x3, waiting for transfers between devices: 18.9 us -> 16.2 us  [exchange(): return lax.all_to_all(x, 'z', 0, 0, tiled=True, axis_index_groups=stride2)]
  transfers between devices with their start and end apart: 12 -> 13, of which waited for: 6 -> 7; matrix products, arithmetic and copies ran while one was open for 5% -> 5% of each run, Pallas kernels for 0% -> 0%
where the time goes in v9:
time: 140 us; the launch traced here: 139 us
  starting transfers between devices  80.7 us (58%)
  waiting for transfers between devices  29.7 us (21%)
  blocking collectives  14.5 us (10%)
  local copies, waits for them, and re-layouts  6.47 us (5%)
  other arithmetic  3.61 us (3%)
  matrix products  3.43 us (2%)
    all_to_all x3, starting transfers between devices, exchange(): return lax.all_to_all(x, 'z', 0, 0, tiled=True, axis_index_groups=stride2)  42.2 us
    ppermute x4, starting transfers between devices, core(): return lax.ppermute(x, 'c', SWAP)  19.7 us
    all_to_all x3, waiting for transfers between devices, exchange(): return lax.all_to_all(x, 'z', 0, 0, tiled=True, axis_index_groups=stride2)  16.2 us
    ppermute x5, starting transfers between devices, pair(): return lax.ppermute(x, 'z', flip)  14.7 us
    psum x1, blocking collectives, shards(): scores = lax.psum(score, 'y')  14.5 us
    ppermute x5, waiting for transfers between devices, pair(): return lax.ppermute(x, 'z', flip)  11.7 us
    all_to_all x1, starting transfers between devices, shards(): came = lax.all_to_all(sent, 'x', 0, 0, tiled=True)  4.01 us
  transfers between devices with their start and end apart: 13, of which 7 were waited for; matrix products, arithmetic and copies ran while one was open for 5% of the time, Pallas kernels for 0%

profile of v9, /device:TPU:1, one launch (start us, length us, event | category | flops | bytes accessed | tf_op | source)
XLA Modules:
  0.0 139.4 jit_solution(13062440602447053210)
XLA Ops:
  0.7 1.7 %constant_dynamic-slice_fusion.6 = bf16[8,8192]{1,0:T(8,128)(2,1)} fusion(bf16[32,8192]{1,0:T(8,128)(2,1)} %param.11, s32[]{:T(128)S(6)} %select_n.117), kind=kLoop, calls=%fused_computation.61 | loop fusion | bytes 262148 | tf_op jit(solution)/shard_map/dynamic_slice | solution.py:43
  2.3 19.4 %all-to-all-start = ((bf16[8,8,1024]{2,1,0:T(8,128)(2,1)}), bf16[8,8,1024]{2,1,0:T(8,128)(2,1)S(1)}, u32[]{:S(2)}, u32[]{:S(2)}) async-start(bf16[8,8,1024]{2,1,0:T(8,128)(2,1)} %bitcast.1), calls=%async_computation | async-start | bytes 262144 | tf_op jit(solution)/shard_map/all_to_all | solution.py:37
  21.8 3.1 %collective-permute-start = (bf16[256,512]{1,0:T(8,128)(2,1)S(1)}, bf16[256,512]{1,0:T(8,128)(2,1)S(1)}, u32[]{:S(2)}, u32[]{:S(2)}) collective-permute-start(bf16[256,512]{1,0:T(8,128)(2,1)S(1)} %copy-done.2), channel_id=1, source_target_pairs={{0,2},{2,0},{4,6},{6,4},{8,10},{10,8},{12,14},{14,12},{16,18},{18,... | collective-permute-start | bytes 786440 | tf_op jit(solution)/shard_map/ppermute | solution.py:31
  25.0 3.1 %collective-permute-start.2 = (bf16[8,2,2,512]{3,2,1,0:T(2,128)(2,1)S(1)}, bf16[8,2,2,512]{3,2,1,0:T(2,128)(2,1)S(1)}, u32[]{:S(2)}, u32[]{:S(2)}) collective-permute-start(bf16[8,2,2,512]{3,2,1,0:T(2,128)(2,1)S(1)} %get-tuple-element.29), channel_id=1, source_target_pairs={{0,1},{1,0},{2,3},{3,2},{4,5},{5,4},{6,7},{7,6},{8,9},{9,8},{10,11... | collective-permute-start | bytes 98312 | tf_op jit(solution)/shard_map/ppermute | solution.py:34
  28.2 0.6 fusion.6
  28.8 0.1 pad_maximum_fusion.3
  28.9 6.8 %collective-permute-done = bf16[256,512]{1,0:T(8,128)(2,1)S(1)} collective-permute-done((bf16[256,512]{1,0:T(8,128)(2,1)S(1)}, bf16[256,512]{1,0:T(8,128)(2,1)S(1)}, u32[]{:S(2)}, u32[]{:S(2)}) %collective-permute-start) | collective-permute-done | bytes 262176 | tf_op jit(solution)/shard_map/ppermute | solution.py:31
  35.7 0.1 maximum_select_fusion.2
  35.8 2.7 %collective-permute-start.1 = (bf16[2,256,512]{2,1,0:T(8,128)(2,1)S(1)}, bf16[2,256,512]{2,1,0:T(8,128)(2,1)S(1)}, u32[]{:S(2)}, u32[]{:S(2)}) collective-permute-start(bf16[2,256,512]{2,1,0:T(8,128)(2,1)S(1)} %maximum_select_fusion.2), channel_id=1, source_target_pairs={{0,1},{1,0},{2,3},{3,2},{4,5},{5,4},{6,7},{7,6},{8,9},{9,8},{10,11... | collective-permute-start | bytes 1572872 | tf_op jit(solution)/shard_map/ppermute | solution.py:34
  38.5 0.1 broadcast_select_fusion
  38.6 0.9 broadcast_in_dim.10
  39.5 4.0 %all-to-all-start.1 = ((bf16[4,9,8,1024]{3,2,1,0:T(8,128)(2,1)}), bf16[4,9,8,1024]{3,2,1,0:T(8,128)(2,1)S(1)}, u32[]{:S(2)}, u32[]{:S(2)}) async-start(bf16[4,9,8,1024]{3,2,1,0:T(8,128)(2,1)} %broadcast_in_dim.10), calls=%async_computation.1 | async-start | bytes 1179648 | tf_op jit(solution)/shard_map/all_to_all | solution.py:58
  43.6 3.2 %collective-permute-start.3 = (bf16[2,8,2,512]{3,2,0,1:T(2,128)(2,1)S(1)}, bf16[2,8,2,512]{3,2,0,1:T(2,128)(2,1)S(1)}, u32[]{:S(2)}, u32[]{:S(2)}) collective-permute-start(bf16[2,8,2,512]{3,2,0,1:T(2,128)(2,1)S(1)} %bitcast.72), channel_id=1, source_target_pairs={{0,2},{2,0},{4,6},{6,4},{8,10},{10,8},{12,14},{14,12},{16,18},{18,... | collective-permute-start | bytes 98312 | tf_op jit(solution)/shard_map/ppermute | solution.py:31
  46.9 1.7 %collective-permute-done.3 = bf16[2,8,2,512]{3,2,0,1:T(2,128)(2,1)S(1)} collective-permute-done((bf16[2,8,2,512]{3,2,0,1:T(2,128)(2,1)S(1)}, bf16[2,8,2,512]{3,2,0,1:T(2,128)(2,1)S(1)}, u32[]{:S(2)}, u32[]{:S(2)}) %collective-permute-start.3) | collective-permute-done | bytes 32800 | tf_op jit(solution)/shard_map/ppermute | solution.py:31
  48.6 0.1 fusion.15
  48.7 0.1 maximum_select_fusion.1
  48.8 0.8 copy-done.3
  49.6 1.4 maximum_select_fusion
  51.0 1.0 all-to-all-done.1
  52.1 0.4 convolution_convert_fusion
  52.5 0.3 copy-done.1
  52.8 0.7 pad_maximum_fusion
  53.6 11.7 %all-to-all-start.2 = ((bf16[8,40,512]{2,1,0:T(8,128)(2,1)}), bf16[8,40,512]{2,1,0:T(8,128)(2,1)S(1)}, u32[]{:S(2)}, u32[]{:S(2)}) async-start(bf16[8,40,512]{2,1,0:T(8,128)(2,1)} %pad_maximum_fusion), calls=%async_computation.2 | async-start | bytes 655360 | tf_op jit(solution)/shard_map/all_to_all | solution.py:37
  65.3 0.7 copy-done.6
  65.9 0.1 fusion.5
  66.1 0.8 slice_bitcast_fusion.2
  67.0 0.1 reshape.158
  67.1 3.1 %collective-permute-start.4 = (bf16[256,512]{1,0:T(8,128)(2,1)S(1)}, bf16[256,512]{1,0:T(8,128)(2,1)S(1)}, u32[]{:S(2)}, u32[]{:S(2)}) collective-permute-start(bf16[256,512]{1,0:T(8,128)(2,1)S(1)} %get-tuple-element.12), channel_id=1, source_target_pairs={{0,2},{2,0},{4,6},{6,4},{8,10},{10,8},{12,14},{14,12},{16,18},{18,... | collective-permute-start | bytes 786440 | tf_op jit(solution)/shard_map/ppermute | solution.py:31
  70.2 14.5 %psum.7 = f32[32]{0:T(128)S(1)} all-reduce(f32[32]{0:T(128)S(1)} %reduce_sum.39), channel_id=1, replica_groups=mesh['x'=4,'y'=8,'z'=16,'c'=2] {'y'}, use_global_device_ids=true, to_apply=%region_2.3 | all-reduce | flops 32 | bytes 256 | tf_op jit(solution)/shard_map/psum | solution.py:87
  84.7 0.2 fusion.4
  84.9 0.3 fusion.1
  85.2 0.7 pad_maximum_fusion.1
  86.0 0.2 collective-permute-done.4
  86.2 11.1 %all-to-all-start.3 = ((bf16[8,40,512]{2,1,0:T(8,128)(2,1)}), bf16[8,40,512]{2,1,0:T(8,128)(2,1)S(1)}, u32[]{:S(2)}, u32[]{:S(2)}) async-start(bf16[8,40,512]{2,1,0:T(8,128)(2,1)} %pad_maximum_fusion.1), calls=%async_computation.3 | async-start | bytes 655360 | tf_op jit(solution)/shard_map/all_to_all | solution.py:37
  97.3 16.1 %all-to-all-done.3 = bf16[8,40,512]{2,1,0:T(8,128)(2,1)S(1)} async-done(((bf16[8,40,512]{2,1,0:T(8,128)(2,1)}), bf16[8,40,512]{2,1,0:T(8,128)(2,1)S(1)}, u32[]{:S(2)}, u32[]{:S(2)}) %all-to-all-start.3) | async-done | bytes 327712 | tf_op jit(solution)/shard_map/all_to_all | solution.py:37
  113.5 3.3 %collective-permute-start.6 = (bf16[256,512]{1,0:T(8,128)(2,1)S(1)}, bf16[256,512]{1,0:T(8,128)(2,1)S(1)}, u32[]{:S(2)}, u32[]{:S(2)}) collective-permute-start(bf16[256,512]{1,0:T(8,128)(2,1)S(1)} %bitcast.60), channel_id=1, source_target_pairs={{0,2},{2,0},{4,6},{6,4},{8,10},{10,8},{12,14},{14,12},{16,18},{18,... | collective-permute-start | bytes 786440 | tf_op jit(solution)/shard_map/ppermute | solution.py:31
  116.8 0.2 fusion.13
  117.2 2.0 %collective-permute-start.5 = (bf16[8,2,2,512]{3,2,1,0:T(2,128)(2,1)S(1)}, bf16[8,2,2,512]{3,2,1,0:T(2,128)(2,1)S(1)}, u32[]{:S(2)}, u32[]{:S(2)}) collective-permute-start(bf16[8,2,2,512]{3,2,1,0:T(2,128)(2,1)S(1)} %get-tuple-element.15), channel_id=1, source_target_pairs={{0,2},{2,0},{4,6},{6,4},{8,10},{10,8},{12,14},{14,12},{16,18},{18,... | collective-permute-start | bytes 98312 | tf_op jit(solution)/shard_map/ppermute | solution.py:31
  119.1 3.0 %collective-permute-done.5 = bf16[8,2,2,512]{3,2,1,0:T(2,128)(2,1)S(1)} collective-permute-done((bf16[8,2,2,512]{3,2,1,0:T(2,128)(2,1)S(1)}, bf16[8,2,2,512]{3,2,1,0:T(2,128)(2,1)S(1)}, u32[]{:S(2)}, u32[]{:S(2)}) %collective-permute-start.5) | collective-permute-done | bytes 32800 | tf_op jit(solution)/shard_map/ppermute | solution.py:31
  122.1 0.1 broadcast_select_fusion.2
  122.3 0.3 fusion
  122.6 11.9 %collective-permute-start.8 = (bf16[256,512]{1,0:T(8,128)(2,1)S(1)}, bf16[256,512]{1,0:T(8,128)(2,1)S(1)}, u32[]{:S(2)}, u32[]{:S(2)}) collective-permute-start(bf16[256,512]{1,0:T(8,128)(2,1)S(1)} %fusion), channel_id=1, source_target_pairs={{0,1},{1,0},{2,3},{3,2},{4,5},{5,4},{6,7},{7,6},{8,9},{9,8},{10,11... | collective-permute-start | bytes 786440 | tf_op jit(solution)/shard_map/ppermute | solution.py:34
  134.5 1.9 %collective-permute-start.7 = (bf16[8,2,2,512]{3,2,1,0:T(2,128)(2,1)S(1)}, bf16[8,2,2,512]{3,2,1,0:T(2,128)(2,1)S(1)}, u32[]{:S(2)}, u32[]{:S(2)}) collective-permute-start(bf16[8,2,2,512]{3,2,1,0:T(2,128)(2,1)S(1)} %get-tuple-element.18), channel_id=1, source_target_pairs={{0,1},{1,0},{2,3},{3,2},{4,5},{5,4},{6,7},{7,6},{8,9},{9,8},{10,11... | collective-permute-start | bytes 98312 | tf_op jit(solution)/shard_map/ppermute | solution.py:34
  136.4 0.3 fusion.10
  136.7 0.9 collective-permute-done.7
  137.6 0.1 broadcast_select_fusion.3
  137.7 0.7 select_n.138
  138.4 1.1 convert_add_fusion
  (43 shorter events, 0.7 us)
Async XLA Ops:
  0.6 27.5 %copy-start = (bf16[128,4096]{1,0:T(8,128)(2,1)S(1)}, bf16[128,4096]{1,0:T(8,128)(2,1)}, u32[]{:S(2)}) copy-start(bf16[128,4096]{1,0:T(8,128)(2,1)} %param.8) | copy-start | bytes 3145732
  0.7 21.1 %copy-start.2 = (bf16[256,512]{1,0:T(8,128)(2,1)S(1)}, bf16[256,512]{1,0:T(8,128)(2,1)}, u32[]{:S(2)}) copy-start(bf16[256,512]{1,0:T(8,128)(2,1)} %param.12) | copy-start | bytes 786436
  0.7 24.2 %copy-start.5 = (bf16[64,512]{1,0:T(8,128)(2,1)S(1)}, bf16[64,512]{1,0:T(8,128)(2,1)}, u32[]{:S(2)}) copy-start(bf16[64,512]{1,0:T(8,128)(2,1)} %param.13) | copy-start | bytes 196612
  2.3 25.8 %copy-start.4 = (bf16[32,4096]{1,0:T(8,128)(2,1)S(1)}, bf16[32,4096]{1,0:T(8,128)(2,1)}, u32[]{:S(2)}) copy-start(bf16[32,4096]{1,0:T(8,128)(2,1)} %param.7) | copy-start | bytes 786436
  2.3 36.3 %all-to-all-start = ((bf16[8,8,1024]{2,1,0:T(8,128)(2,1)}), bf16[8,8,1024]{2,1,0:T(8,128)(2,1)S(1)}, u32[]{:S(2)}, u32[]{:S(2)}) async-start(bf16[8,8,1024]{2,1,0:T(8,128)(2,1)} %bitcast.1), calls=%async_computation | async-start | bytes 262144 | tf_op jit(solution)/shard_map/all_to_all | solution.py:37
  21.8 13.9 %collective-permute-start = (bf16[256,512]{1,0:T(8,128)(2,1)S(1)}, bf16[256,512]{1,0:T(8,128)(2,1)S(1)}, u32[]{:S(2)}, u32[]{:S(2)}) collective-permute-start(bf16[256,512]{1,0:T(8,128)(2,1)S(1)} %copy-done.2), channel_id=1, source_target_pairs={{0,2},{2,0},{4,6},{6,4},{8,10},{10,8},{12,14},{14,12},{16,18},{18,... | collective-permute-start | bytes 786440 | tf_op jit(solution)/shard_map/ppermute | solution.py:31
  25.0 13.5 %collective-permute-start.2 = (bf16[8,2,2,512]{3,2,1,0:T(2,128)(2,1)S(1)}, bf16[8,2,2,512]{3,2,1,0:T(2,128)(2,1)S(1)}, u32[]{:S(2)}, u32[]{:S(2)}) collective-permute-start(bf16[8,2,2,512]{3,2,1,0:T(2,128)(2,1)S(1)} %get-tuple-element.29), channel_id=1, source_target_pairs={{0,1},{1,0},{2,3},{3,2},{4,5},{5,4},{6,7},{7,6},{8,9},{9,8},{10,11... | collective-permute-start | bytes 98312 | tf_op jit(solution)/shard_map/ppermute | solution.py:34
  35.8 13.0 %collective-permute-start.1 = (bf16[2,256,512]{2,1,0:T(8,128)(2,1)S(1)}, bf16[2,256,512]{2,1,0:T(8,128)(2,1)S(1)}, u32[]{:S(2)}, u32[]{:S(2)}) collective-permute-start(bf16[2,256,512]{2,1,0:T(8,128)(2,1)S(1)} %maximum_select_fusion.2), channel_id=1, source_target_pairs={{0,1},{1,0},{2,3},{3,2},{4,5},{5,4},{6,7},{7,6},{8,9},{9,8},{10,11... | collective-permute-start | bytes 1572872 | tf_op jit(solution)/shard_map/ppermute | solution.py:34
  39.5 12.4 %all-to-all-start.1 = ((bf16[4,9,8,1024]{3,2,1,0:T(8,128)(2,1)}), bf16[4,9,8,1024]{3,2,1,0:T(8,128)(2,1)S(1)}, u32[]{:S(2)}, u32[]{:S(2)}) async-start(bf16[4,9,8,1024]{3,2,1,0:T(8,128)(2,1)} %broadcast_in_dim.10), calls=%async_computation.1 | async-start | bytes 1179648 | tf_op jit(solution)/shard_map/all_to_all | solution.py:58
  43.6 5.0 %collective-permute-start.3 = (bf16[2,8,2,512]{3,2,0,1:T(2,128)(2,1)S(1)}, bf16[2,8,2,512]{3,2,0,1:T(2,128)(2,1)S(1)}, u32[]{:S(2)}, u32[]{:S(2)}) collective-permute-start(bf16[2,8,2,512]{3,2,0,1:T(2,128)(2,1)S(1)} %bitcast.72), channel_id=1, source_target_pairs={{0,2},{2,0},{4,6},{6,4},{8,10},{10,8},{12,14},{14,12},{16,18},{18,... | collective-permute-start | bytes 98312 | tf_op jit(solution)/shard_map/ppermute | solution.py:31
  48.8 0.8 copy-start.3
  52.0 0.8 copy-start.1
  53.6 31.1 %all-to-all-start.2 = ((bf16[8,40,512]{2,1,0:T(8,128)(2,1)}), bf16[8,40,512]{2,1,0:T(8,128)(2,1)S(1)}, u32[]{:S(2)}, u32[]{:S(2)}) async-start(bf16[8,40,512]{2,1,0:T(8,128)(2,1)} %pad_maximum_fusion), calls=%async_computation.2 | async-start | bytes 655360 | tf_op jit(solution)/shard_map/all_to_all | solution.py:37
  65.3 0.7 copy-start.6
  67.1 17.6 %copy-start.7 = (s32[32]{0:T(128)S(1)}, s32[32]{0:T(128)}, u32[]{:S(2)}) copy-start(s32[32]{0:T(128)} %param.9) | copy-start | bytes 388
  67.1 19.1 %collective-permute-start.4 = (bf16[256,512]{1,0:T(8,128)(2,1)S(1)}, bf16[256,512]{1,0:T(8,128)(2,1)S(1)}, u32[]{:S(2)}, u32[]{:S(2)}) collective-permute-start(bf16[256,512]{1,0:T(8,128)(2,1)S(1)} %get-tuple-element.12), channel_id=1, source_target_pairs={{0,2},{2,0},{4,6},{6,4},{8,10},{10,8},{12,14},{14,12},{16,18},{18,... | collective-permute-start | bytes 786440 | tf_op jit(solution)/shard_map/ppermute | solution.py:31
  86.2 27.2 %all-to-all-start.3 = ((bf16[8,40,512]{2,1,0:T(8,128)(2,1)}), bf16[8,40,512]{2,1,0:T(8,128)(2,1)S(1)}, u32[]{:S(2)}, u32[]{:S(2)}) async-start(bf16[8,40,512]{2,1,0:T(8,128)(2,1)} %pad_maximum_fusion.1), calls=%async_computation.3 | async-start | bytes 655360 | tf_op jit(solution)/shard_map/all_to_all | solution.py:37
  113.5 8.8 %collective-permute-start.6 = (bf16[256,512]{1,0:T(8,128)(2,1)S(1)}, bf16[256,512]{1,0:T(8,128)(2,1)S(1)}, u32[]{:S(2)}, u32[]{:S(2)}) collective-permute-start(bf16[256,512]{1,0:T(8,128)(2,1)S(1)} %bitcast.60), channel_id=1, source_target_pairs={{0,2},{2,0},{4,6},{6,4},{8,10},{10,8},{12,14},{14,12},{16,18},{18,... | collective-permute-start | bytes 786440 | tf_op jit(solution)/shard_map/ppermute | solution.py:31
  117.2 5.0 %collective-permute-start.5 = (bf16[8,2,2,512]{3,2,1,0:T(2,128)(2,1)S(1)}, bf16[8,2,2,512]{3,2,1,0:T(2,128)(2,1)S(1)}, u32[]{:S(2)}, u32[]{:S(2)}) collective-permute-start(bf16[8,2,2,512]{3,2,1,0:T(2,128)(2,1)S(1)} %get-tuple-element.15), channel_id=1, source_target_pairs={{0,2},{2,0},{4,6},{6,4},{8,10},{10,8},{12,14},{14,12},{16,18},{18,... | collective-permute-start | bytes 98312 | tf_op jit(solution)/shard_map/ppermute | solution.py:31
  122.6 15.8 %collective-permute-start.8 = (bf16[256,512]{1,0:T(8,128)(2,1)S(1)}, bf16[256,512]{1,0:T(8,128)(2,1)S(1)}, u32[]{:S(2)}, u32[]{:S(2)}) collective-permute-start(bf16[256,512]{1,0:T(8,128)(2,1)S(1)} %fusion), channel_id=1, source_target_pairs={{0,1},{1,0},{2,3},{3,2},{4,5},{5,4},{6,7},{7,6},{8,9},{9,8},{10,11... | collective-permute-start | bytes 786440 | tf_op jit(solution)/shard_map/ppermute | solution.py:34
  134.5 3.1 %collective-permute-start.7 = (bf16[8,2,2,512]{3,2,1,0:T(2,128)(2,1)S(1)}, bf16[8,2,2,512]{3,2,1,0:T(2,128)(2,1)S(1)}, u32[]{:S(2)}, u32[]{:S(2)}) collective-permute-start(bf16[8,2,2,512]{3,2,1,0:T(2,128)(2,1)S(1)} %get-tuple-element.18), channel_id=1, source_target_pairs={{0,1},{1,0},{2,3},{3,2},{4,5},{5,4},{6,7},{7,6},{8,9},{9,8},{10,11... | collective-permute-start | bytes 98312 | tf_op jit(solution)/shard_map/ppermute | solution.py:34
